TPU v7x, 32 devices: a whole 2x2x4 slice. The times are simulated.
32 devices in a mesh: seq: 16 (over z, y, x), head: 2 (over core).
Axes of the slice: x: 2, y: 2, z: 4, core: 2. Of those that a mesh axis runs over, the one named last changes fastest.
Arguments:
- tokens: bfloat16 [16384, 768], P('seq'), may hold values from -6 to 6
- mix_gain: bfloat16 [768], replicated, may hold values from 0.099609375 to 1.8984375
- mix_shift: bfloat16 [768], replicated, may hold values from -1.75 to 1.75
- query_weight: bfloat16 [768, 768], P(None, 'head'), may hold values from -0.21875 to 0.21875
- query_bias: bfloat16 [768], P('head'), may hold values from -3 to 3
- key_weight: bfloat16 [768, 768], P(None, 'head'), may hold values from -0.21875 to 0.21875
- value_weight: bfloat16 [768, 768], P(None, 'head'), may hold values from -0.21875 to 0.21875
- value_bias: bfloat16 [768], P('head'), may hold values from -3 to 3
- attn_gain: bfloat16 [768], P('head'), may hold values from 0.099609375 to 1.8984375
- attn_shift: bfloat16 [768], P('head'), may hold values from -1.75 to 1.75
- out_weight: bfloat16 [768, 768], P('head'), may hold values from -0.21875 to 0.21875
- out_bias: bfloat16 [768], replicated, may hold values from -1.75 to 1.75
- feed_gain: bfloat16 [768], P(('seq', 'head')), may hold values from 0.099609375 to 1.8984375
- feed_shift: bfloat16 [768], P(('seq', 'head')), may hold values from -1.75 to 1.75
- up_weight: bfloat16 [768, 3072], P(('seq', 'head')), may hold values from -0.21875 to 0.21875
- up_bias: bfloat16 [3072], P(('seq', 'head')), may hold values from -1.75 to 1.75
- inner_gain: bfloat16 [3072], P(('seq', 'head')), may hold values from 0.099609375 to 1.8984375
- inner_shift: bfloat16 [3072], P(('seq', 'head')), may hold values from -1.75 to 1.75
- down_weight: bfloat16 [3072, 768], P(('seq', 'head')), may hold values from -0.109375 to 0.109375
- down_bias: bfloat16 [768], P(('seq', 'head')), may hold values from -1.75 to 1.75
- cotangent: bfloat16 [16384, 768], P(('seq', 'head')), may hold values from -6 to 6
Outputs:
- output: bfloat16 [16384, 768], P(('seq', 'head'))
- tokens_grad: float32 [16384, 768], P(('seq', 'head'))
- mix_gain_grad: float32 [768], P(('seq', 'head'))
- mix_shift_grad: float32 [768], P(('seq', 'head'))
- query_weight_grad: float32 [768, 768], P('seq', 'head')
- query_bias_grad: float32 [768], P(('head', 'seq'))
- key_weight_grad: float32 [768, 768], P('seq', 'head')
- value_weight_grad: float32 [768, 768], P('seq', 'head')
- value_bias_grad: float32 [768], P(('head', 'seq'))
- attn_gain_grad: float32 [768], P(('head', 'seq'))
- attn_shift_grad: float32 [768], P(('head', 'seq'))
- out_weight_grad: float32 [768, 768], P('head', 'seq')
- out_bias_grad: float32 [768], P(('seq', 'head'))
- feed_gain_grad: float32 [768], P(('seq', 'head'))
- feed_shift_grad: float32 [768], P(('seq', 'head'))
- up_weight_grad: float32 [768, 3072], P(('seq', 'head'))
- up_bias_grad: float32 [3072], P(('seq', 'head'))
- inner_gain_grad: float32 [3072], P(('seq', 'head'))
- inner_shift_grad: float32 [3072], P(('seq', 'head'))
- down_weight_grad: float32 [3072, 768], P(('seq', 'head'))
- down_bias_grad: float32 [768], P(('seq', 'head'))
All inputs are finite; a program needn't handle non-finite values.
Results may differ from a plain program's by a relative error of at most 0.017.
Values may be sent and summed in bfloat16 or wider, within the bound.
No kernel may reach another device: no remote copies, remote signals or barrier semaphores. Data moves between devices by JAX's collectives and lax.ppermute only.
A program may use at most 384 MiB of HBM per device.

v0:
```python
import jax
import jax.numpy as jnp
from jax import lax
from jax.sharding import PartitionSpec as P

HEAD_DIM = 64
W0 = 2048


dilation_rates = (1, 2, 4, 6, 12)
norm_eps = 1e-05
neg_big = -1e30


def from_behind(array, axis, by):
    count = lax.axis_size(axis)
    pairs = [(i, i + by) for i in range(count) if 0 <= i + by < count]
    return lax.ppermute(array, axis, pairs)


def layer_norm(values, gain, shift):
    center = jnp.mean(values, axis=-1, keepdims=True)
    centered = values - center
    spread = jnp.mean(centered * centered, axis=-1, keepdims=True)
    return centered * lax.rsqrt(spread + norm_eps) * gain + shift


def gelu_norm(before, gain, shift):
    return layer_norm(jax.nn.gelu(before, approximate=False), gain, shift)


def dot_rows(left_side, right_side):
    return lax.dot_general(
        left_side, right_side, (((0,), (0,)), ((), ())), preferred_element_type=jnp.float32
    )


def dot_cols(left_side, right_side):
    return lax.dot_general(
        left_side, right_side, (((1,), (1,)), ((), ())), preferred_element_type=jnp.float32
    )


def pick_rows(source, picks, slot_count):
    stride = picks.shape[0]
    extra = slot_count * stride - source.shape[-3]
    widths = [(0, 0)] * (source.ndim - 3) + [(0, extra), (0, 0), (0, 0)]
    padded = jnp.pad(source, widths)
    grouped = padded.reshape(source.shape[:-3] + (slot_count, stride) + source.shape[-2:])
    return jnp.sum(grouped * picks.astype(source.dtype)[:, :, None], axis=-3)


def spread_rows(source, picks, tok_rows):
    stride = picks.shape[0]
    slot_count = source.shape[-3]
    placed = source[..., :, None, :, :] * picks.astype(source.dtype)[:, :, None]
    placed = placed.reshape(source.shape[:-3] + (slot_count * stride,) + source.shape[-2:])
    return placed[..., :tok_rows, :, :]


def pattern_layout(level_idx, tok_rows, length, seq_index, head_ids):
    stride = dilation_rates[level_idx]
    window_len = min(W0 * 2**level_idx, length)
    group_size = window_len // tok_rows
    slot_count = -(-tok_rows // stride)
    offsets = head_ids % stride
    slot_steps = stride * jnp.arange(slot_count, dtype=jnp.int32)
    segment_start = seq_index - seq_index % group_size
    members = seq_index - (group_size - 1) + jnp.arange(group_size, dtype=jnp.int32)
    member_first = jnp.mod(
        offsets[None, :] - jnp.mod(members[:, None] * tok_rows, window_len), stride
    )
    key_local = member_first[:, None, :] + slot_steps[None, :, None]
    inside = (key_local < tok_rows) & (members >= segment_start)[:, None, None]
    key_ok = inside.reshape(group_size * slot_count, head_ids.shape[0])
    key_pos = (members[:, None, None] * tok_rows + key_local).reshape(
        group_size * slot_count, head_ids.shape[0]
    )
    own_first = jnp.mod(offsets - seq_index * tok_rows % window_len, stride)
    picks = jnp.arange(stride, dtype=jnp.int32)[:, None] == own_first[None, :]
    own_local = slot_steps[:, None] + own_first[None, :]
    own_ok = own_local < tok_rows
    own_pos = seq_index * tok_rows + own_local
    return (
        stride,
        slot_count,
        group_size.bit_length() - 1,
        picks,
        own_pos,
        own_ok,
        key_pos,
        key_ok,
    )


def double_apart(pair_piece, bit_count):
    for bit_index in range(bit_count):
        earlier = from_behind(pair_piece, "seq", 2**bit_index)
        pair_piece = jnp.concatenate((earlier, pair_piece), axis=1)
    return pair_piece


def halve_apart(pair_piece, bit_count):
    for bit_index in reversed(range(bit_count)):
        half_len = pair_piece.shape[1] // 2
        older_part = pair_piece[:, :half_len]
        newer_part = pair_piece[:, half_len:]
        pair_piece = newer_part + from_behind(
            older_part.astype(jnp.bfloat16), "seq", -(2**bit_index)
        ).astype(older_part.dtype)
    return pair_piece


def allowed_mask(own_pos, own_ok, key_pos, key_ok):
    return (
        own_ok.T[:, :, None]
        & key_ok.T[:, None, :]
        & (key_pos.T[:, None, :] <= own_pos.T[:, :, None])
    )


def per_device(
    tokens,
    mix_gain,
    mix_shift,
    query_weight,
    query_bias,
    key_weight,
    value_weight,
    value_bias,
    attn_gain,
    attn_shift,
    out_weight,
    out_bias,
    feed_gain,
    feed_shift,
    up_weight,
    up_bias,
    inner_gain,
    inner_shift,
    down_weight,
    down_bias,
    cotangent,
):
    feed_params = (
        lax.all_gather(up_weight, ("seq", "head"), axis=0, tiled=True),
        lax.all_gather(down_weight, ("seq", "head"), axis=0, tiled=True),
        lax.all_gather(up_bias, ("seq", "head"), axis=0, tiled=True),
        lax.all_gather(down_bias, ("seq", "head"), axis=0, tiled=True),
        lax.all_gather(feed_gain, ("seq", "head"), axis=0, tiled=True),
        lax.all_gather(feed_shift, ("seq", "head"), axis=0, tiled=True),
        lax.all_gather(inner_gain, ("seq", "head"), axis=0, tiled=True),
        lax.all_gather(inner_shift, ("seq", "head"), axis=0, tiled=True),
    )
    (
        up_full,
        down_full,
        up_bias_full,
        down_bias_full,
        feed_gain_full,
        feed_shift_full,
        inner_gain_full,
        inner_shift_full,
    ) = feed_params
    tok_rows = tokens.shape[0]
    length = tok_rows * lax.axis_size("seq")
    half_rows = tok_rows // lax.axis_size("head")
    seq_index = lax.axis_index("seq")
    head_index = lax.axis_index("head")
    heads_here = query_weight.shape[1] // HEAD_DIM
    local_cols = heads_here * HEAD_DIM
    column_total = local_cols * lax.axis_size("head")
    head_ids = head_index * heads_here + jnp.arange(heads_here, dtype=jnp.int32)
    score_scale = HEAD_DIM ** (-0.5)
    tokens_wide = tokens.astype(jnp.float32)
    mix_in = layer_norm(
        tokens_wide, mix_gain.astype(jnp.float32), mix_shift.astype(jnp.float32)
    ).astype(jnp.bfloat16)
    queries = (
        jnp.dot(mix_in, query_weight, preferred_element_type=jnp.float32)
        + query_bias.astype(jnp.float32)
    ).astype(jnp.bfloat16)
    keys_flat = jnp.dot(mix_in, key_weight, preferred_element_type=jnp.float32).astype(jnp.bfloat16)
    values_flat = (
        jnp.dot(mix_in, value_weight, preferred_element_type=jnp.float32)
        + value_bias.astype(jnp.float32)
    ).astype(jnp.bfloat16)
    query_split = queries.reshape(tok_rows, heads_here, HEAD_DIM)
    pair_split = jnp.stack((keys_flat, values_flat)).reshape(2, tok_rows, heads_here, HEAD_DIM)
    layouts = [
        pattern_layout(level_idx, tok_rows, length, seq_index, head_ids)
        for level_idx in range(len(dilation_rates))
    ]
    query_parts = [pick_rows(query_split, layout[3], layout[1]) for layout in layouts]
    pair_parts = [
        pick_rows(pair_split, layout[3], layout[1]).reshape(2, layout[1], local_cols)
        for layout in layouts
    ]
    bit_totals = [layout[2] for layout in layouts]
    pair_groups = [
        double_apart(pair_piece, bit_count) for pair_piece, bit_count in zip(pair_parts, bit_totals)
    ]
    out_fulls = []
    lse_fulls = []
    lse_parts = []
    for level_idx, layout in enumerate(layouts):
        stride, slot_count, bit_count, picks, own_pos, own_ok, key_pos, key_ok = layout
        attend_pair_block = pair_groups[level_idx]
        attend_pair_heads = attend_pair_block.reshape(
            2, attend_pair_block.shape[1], heads_here, HEAD_DIM
        )
        attend_scores = (
            jnp.einsum(
                "qhd,khd->hqk",
                query_parts[level_idx],
                attend_pair_heads[0],
                preferred_element_type=jnp.float32,
            )
            * score_scale
        )
        attend_allowed = allowed_mask(own_pos, own_ok, key_pos, key_ok)
        masked = jnp.where(attend_allowed, attend_scores, neg_big)
        row_top = jnp.max(masked, axis=2)
        exp_scores = jnp.where(attend_allowed, jnp.exp(masked - row_top[:, :, None]), 0.0)
        row_total = jnp.where(own_ok.T, jnp.sum(exp_scores, axis=2), 1.0)
        weights_low = (exp_scores / row_total[:, :, None]).astype(jnp.bfloat16)
        out_part = jnp.einsum(
            "hqk,khd->qhd", weights_low, attend_pair_heads[1], preferred_element_type=jnp.float32
        )
        out_part, lse_part = (out_part, (row_top + jnp.log(row_total)).T)
        chosen = spread_rows(own_ok.astype(jnp.float32)[:, :, None], picks, tok_rows)[:, :, 0] > 0.5
        lse_full = jnp.where(
            chosen, spread_rows(lse_part[:, :, None], picks, tok_rows)[:, :, 0], neg_big
        )
        out_fulls.append(spread_rows(out_part, picks, tok_rows))
        lse_fulls.append(lse_full)
        lse_parts.append(lse_part)
    lse_stack = jnp.stack(lse_fulls)
    lse_total = jax.nn.logsumexp(lse_stack, axis=0)
    weights_all = jnp.exp(lse_stack - lse_total[None])
    mixed_wide = jnp.sum(weights_all[:, :, :, None] * jnp.stack(out_fulls), axis=0)
    attn_gain_heads = attn_gain.astype(jnp.float32).reshape(1, heads_here, HEAD_DIM)
    attn_shift_heads = attn_shift.astype(jnp.float32).reshape(1, heads_here, HEAD_DIM)
    row_sum, row_square = lax.psum(
        (jnp.sum(mixed_wide, axis=(1, 2)), jnp.sum(mixed_wide * mixed_wide, axis=(1, 2))), "head"
    )
    row_mean = row_sum / column_total
    row_var = jnp.maximum(row_square / column_total - row_mean * row_mean, 0.0)
    row_scale = lax.rsqrt(row_var + norm_eps)
    attn_normed = (mixed_wide - row_mean[:, None, None]) * row_scale[:, None, None]
    mixed = (
        (attn_normed * attn_gain_heads + attn_shift_heads)
        .reshape(tok_rows, local_cols)
        .astype(jnp.bfloat16)
    )
    branch = lax.psum_scatter(
        jnp.dot(mixed, out_weight, preferred_element_type=jnp.float32).astype(jnp.bfloat16),
        "head",
        scatter_dimension=0,
        tiled=True,
    ).astype(jnp.float32) + out_bias.astype(jnp.float32)
    tokens_half = lax.dynamic_slice_in_dim(tokens_wide, head_index * half_rows, half_rows, 0)
    hidden = tokens_half + branch
    feed_wide, feed_pull = jax.vjp(
        layer_norm, hidden, feed_gain_full.astype(jnp.float32), feed_shift_full.astype(jnp.float32)
    )
    feed_in = feed_wide.astype(jnp.bfloat16)
    before = jnp.dot(feed_in, up_full, preferred_element_type=jnp.float32) + up_bias_full.astype(
        jnp.float32
    )
    inner_wide, inner_pull = jax.vjp(
        gelu_norm, before, inner_gain_full.astype(jnp.float32), inner_shift_full.astype(jnp.float32)
    )
    inner = inner_wide.astype(jnp.bfloat16)
    output = (
        hidden
        + jnp.dot(inner, down_full, preferred_element_type=jnp.float32)
        + down_bias_full.astype(jnp.float32)
    ).astype(jnp.bfloat16)
    cot_wide = cotangent.astype(jnp.float32)
    down_weight_grad = dot_rows(inner, cotangent)
    down_bias_grad = jnp.sum(cot_wide, axis=0)
    inner_grad = dot_cols(cotangent, down_full)
    before_grad, inner_gain_grad, inner_shift_grad = inner_pull(inner_grad)
    before_low = before_grad.astype(jnp.bfloat16)
    up_weight_grad = dot_rows(feed_in, before_low)
    up_bias_grad = jnp.sum(before_low.astype(jnp.float32), axis=0)
    feed_grad = dot_cols(before_low, up_full)
    hidden_norm_grad, feed_gain_grad, feed_shift_grad = feed_pull(feed_grad)
    hidden_grad = cot_wide + hidden_norm_grad
    branch_low = hidden_grad.astype(jnp.bfloat16)
    out_bias_grad = jnp.sum(branch_low.astype(jnp.float32), axis=0)
    branch_full = lax.all_gather(branch_low, "head", axis=0, tiled=True)
    out_weight_local = dot_rows(mixed, branch_full)
    normed_grad = dot_cols(branch_full, out_weight).reshape(tok_rows, heads_here, HEAD_DIM)
    attn_gain_local = jnp.sum(normed_grad * attn_normed, axis=0).reshape(local_cols)
    attn_shift_local = jnp.sum(normed_grad, axis=0).reshape(local_cols)
    scaled_up = normed_grad * attn_gain_heads
    scaled_sum, scaled_cross = lax.psum(
        (jnp.sum(scaled_up, axis=(1, 2)), jnp.sum(scaled_up * attn_normed, axis=(1, 2))), "head"
    )
    mixed_grad = (
        scaled_up
        - (scaled_sum / column_total)[:, None, None]
        - attn_normed * (scaled_cross / column_total)[:, None, None]
    ) * row_scale[:, None, None]
    mixed_dot = jnp.sum(mixed_grad * mixed_wide, axis=2)
    query_grad = jnp.zeros(query_split.shape, jnp.float32)
    pair_steps = []
    for level_idx, layout in enumerate(layouts):
        stride, slot_count, bit_count, picks, own_pos, own_ok, key_pos, key_ok = layout
        scaled_grad = (weights_all[level_idx][:, :, None] * mixed_grad).astype(jnp.bfloat16)
        lse_grad = weights_all[level_idx] * (
            jnp.sum(mixed_grad * out_fulls[level_idx], axis=2) - mixed_dot
        )
        grad_part = pick_rows(scaled_grad, picks, slot_count)
        lse_grad_part = pick_rows(lse_grad[:, :, None], picks, slot_count)[:, :, 0]
        query_block = query_parts[level_idx]
        pair_block = pair_groups[level_idx]
        pair_heads = pair_block.reshape(2, pair_block.shape[1], heads_here, HEAD_DIM)
        key_block = pair_heads[0]
        value_block = pair_heads[1]
        scores = (
            jnp.einsum("qhd,khd->hqk", query_block, key_block, preferred_element_type=jnp.float32)
            * score_scale
        )
        allowed = allowed_mask(own_pos, own_ok, key_pos, key_ok)
        weights_wide = jnp.exp(
            jnp.where(allowed, scores - lse_parts[level_idx].T[:, :, None], neg_big)
        )
        weight_grad = jnp.einsum(
            "qhd,khd->hqk", grad_part, value_block, preferred_element_type=jnp.float32
        )
        weighted = jnp.sum(weights_wide * weight_grad, axis=2)
        score_grad = (
            weights_wide * (weight_grad - weighted[:, :, None] + lse_grad_part.T[:, :, None])
        ).astype(jnp.bfloat16)
        query_grad_block = (
            jnp.einsum("hqk,khd->qhd", score_grad, key_block, preferred_element_type=jnp.float32)
            * score_scale
        )
        key_grad_block = (
            jnp.einsum("hqk,qhd->khd", score_grad, query_block, preferred_element_type=jnp.float32)
            * score_scale
        )
        value_grad_block = jnp.einsum(
            "hqk,qhd->khd",
            weights_wide.astype(jnp.bfloat16),
            grad_part,
            preferred_element_type=jnp.float32,
        )
        pair_grad_block = jnp.stack((key_grad_block, value_grad_block)).reshape(
            2, key_block.shape[0], local_cols
        )
        query_grad = query_grad + spread_rows(query_grad_block, picks, tok_rows)
        pair_steps.append(pair_grad_block)
    pair_back = [
        halve_apart(pair_piece, bit_count) for pair_piece, bit_count in zip(pair_steps, bit_totals)
    ]
    pair_grad = jnp.zeros(pair_split.shape, jnp.float32)
    for level_idx, layout in enumerate(layouts):
        back_rows = pair_back[level_idx].reshape(2, layout[1], heads_here, HEAD_DIM)
        pair_grad = pair_grad + spread_rows(back_rows, layout[3], tok_rows)
    query_low = query_grad.reshape(tok_rows, local_cols).astype(jnp.bfloat16)
    key_low = pair_grad[0].reshape(tok_rows, local_cols).astype(jnp.bfloat16)
    value_low = pair_grad[1].reshape(tok_rows, local_cols).astype(jnp.bfloat16)
    query_weight_local = dot_rows(mix_in, query_low)
    key_weight_local = dot_rows(mix_in, key_low)
    value_weight_local = dot_rows(mix_in, value_low)
    query_bias_local = jnp.sum(query_low.astype(jnp.float32), axis=0)
    value_bias_local = jnp.sum(value_low.astype(jnp.float32), axis=0)
    total = dot_cols(query_low, query_weight)
    total = total + dot_cols(key_low, key_weight)
    mix_in_grad = lax.psum_scatter(
        (total + dot_cols(value_low, value_weight)).astype(jnp.bfloat16),
        "head",
        scatter_dimension=0,
        tiled=True,
    ).astype(jnp.float32)
    unused_norm, mix_pull = jax.vjp(
        layer_norm, tokens_half, mix_gain.astype(jnp.float32), mix_shift.astype(jnp.float32)
    )
    tokens_norm_grad, mix_gain_local, mix_shift_local = mix_pull(mix_in_grad)
    tokens_grad = hidden_grad + tokens_norm_grad
    (
        query_weight_grad,
        key_weight_grad,
        value_weight_grad,
        query_bias_grad,
        value_bias_grad,
        attn_gain_grad,
        attn_shift_grad,
    ) = (
        lax.psum_scatter(query_weight_local, "seq", scatter_dimension=0, tiled=True),
        lax.psum_scatter(key_weight_local, "seq", scatter_dimension=0, tiled=True),
        lax.psum_scatter(value_weight_local, "seq", scatter_dimension=0, tiled=True),
        lax.psum_scatter(query_bias_local, "seq", scatter_dimension=0, tiled=True),
        lax.psum_scatter(value_bias_local, "seq", scatter_dimension=0, tiled=True),
        lax.psum_scatter(attn_gain_local, "seq", scatter_dimension=0, tiled=True),
        lax.psum_scatter(attn_shift_local, "seq", scatter_dimension=0, tiled=True),
    )
    out_weight_grad = lax.psum_scatter(out_weight_local, "seq", scatter_dimension=1, tiled=True)
    summed = (
        lax.psum_scatter(up_weight_grad, ("seq", "head"), scatter_dimension=0, tiled=True),
        lax.psum_scatter(down_weight_grad, ("seq", "head"), scatter_dimension=0, tiled=True),
        lax.psum_scatter(up_bias_grad, ("seq", "head"), scatter_dimension=0, tiled=True),
        lax.psum_scatter(down_bias_grad, ("seq", "head"), scatter_dimension=0, tiled=True),
        lax.psum_scatter(feed_gain_grad, ("seq", "head"), scatter_dimension=0, tiled=True),
        lax.psum_scatter(feed_shift_grad, ("seq", "head"), scatter_dimension=0, tiled=True),
        lax.psum_scatter(inner_gain_grad, ("seq", "head"), scatter_dimension=0, tiled=True),
        lax.psum_scatter(inner_shift_grad, ("seq", "head"), scatter_dimension=0, tiled=True),
        lax.psum_scatter(mix_gain_local, ("seq", "head"), scatter_dimension=0, tiled=True),
        lax.psum_scatter(mix_shift_local, ("seq", "head"), scatter_dimension=0, tiled=True),
        lax.psum_scatter(out_bias_grad, ("seq", "head"), scatter_dimension=0, tiled=True),
    )
    (
        up_weight_sum,
        down_weight_sum,
        up_bias_sum,
        down_bias_sum,
        feed_gain_sum,
        feed_shift_sum,
        inner_gain_sum,
        inner_shift_sum,
        mix_gain_sum,
        mix_shift_sum,
        out_bias_sum,
    ) = summed
    return (
        output,
        tokens_grad,
        mix_gain_sum,
        mix_shift_sum,
        query_weight_grad,
        query_bias_grad,
        key_weight_grad,
        value_weight_grad,
        value_bias_grad,
        attn_gain_grad,
        attn_shift_grad,
        out_weight_grad,
        out_bias_sum,
        feed_gain_sum,
        feed_shift_sum,
        up_weight_sum,
        up_bias_sum,
        inner_gain_sum,
        inner_shift_sum,
        down_weight_sum,
        down_bias_sum,
    )


def solution(mesh):
    return jax.shard_map(
        per_device,
        mesh=mesh,
        in_specs=(
            P("seq", None),
            P(),
            P(),
            P(None, "head"),
            P("head"),
            P(None, "head"),
            P(None, "head"),
            P("head"),
            P("head"),
            P("head"),
            P("head", None),
            P(),
            P(("seq", "head")),
            P(("seq", "head")),
            P(("seq", "head"), None),
            P(("seq", "head")),
            P(("seq", "head")),
            P(("seq", "head")),
            P(("seq", "head"), None),
            P(("seq", "head")),
            P(("seq", "head"), None),
        ),
        out_specs=(
            P(("seq", "head"), None),
            P(("seq", "head"), None),
            P(("seq", "head")),
            P(("seq", "head")),
            P("seq", "head"),
            P(("head", "seq")),
            P("seq", "head"),
            P("seq", "head"),
            P(("head", "seq")),
            P(("head", "seq")),
            P(("head", "seq")),
            P("head", "seq"),
            P(("seq", "head")),
            P(("seq", "head")),
            P(("seq", "head")),
            P(("seq", "head"), None),
            P(("seq", "head")),
            P(("seq", "head")),
            P(("seq", "head")),
            P(("seq", "head"), None),
            P(("seq", "head")),
        ),
        check_vma=False,
    )
```

profile of v0, /device:TPU:0, one launch (start us, length us, event | category | flops | bytes accessed | tf_op | source)
XLA Modules:
  0.0 2389.4 jit_solution(17494508672679206467)
XLA Ops:
  17.9 6.0 collective-permute-start
  64.5 5.7 copy.326
  75.8 9.7 pad_maximum_fusion.6
  241.2 21.5 fusion.6
  262.7 26.1 %fusion.9 = f32[6,1024]{1,0:T(8,128)S(1)} fusion(f32[6,1024,2048]{2,1,0:T(8,128)} %get-tuple-element.140, f32[6,1024]{1,0:T(8,128)S(1)} %get-tuple-element.139, s32[6,1024]{1,0:T(8,128)S(1)} %iota_add_fusion, s32[2048]{0:T(1024)S(1)} %bitcast.493, pred[2048]{0:T(1024)(128)(4,1)S(1)} %copy-done.244, pred[6,1024]{1,0:T(8,128)(4,1)S(1)} %iota_compare_fusion), kind=kLoop, calls=%fused_computation.14 | loop fusion | flops 100657152 | bytes 50421760 | tf_op jit(solution)/shard_map/reduce_sum | solution.py:225
  289.5 26.4 %bitcast_dynamic-update-slice_fusion = (f32[5,1024,6,64]{1,3,2,0:T(8,128)}, f32[6,64,1024]{2,1,0:T(8,128)}) fusion(bf16[2048,6,64]{0,2,1:T(8,128)(2,1)S(1)} %bitcast.437, f32[6,1024,2048]{2,1,0:T(8,128)} %get-tuple-element.140, f32[6,1024]{1,0:T(8,128)S(1)} %get-tuple-element.115, f32[6,1024]{1,0:T(8,128)S(1)} %get-tuple-element.139, ...), kind=kOutput, calls=%fused_computation.200 | convolution fusion | flops 1723858944 | bytes 55140352 | tf_op jit(solution)/shard_map/hqk,khd->qhd/dot_general | solution.py:227
  316.6 12.2 pad_maximum_fusion.8
  334.3 8.5 concatenate.80
  373.6 9.3 fusion.14
  383.1 13.2 fusion.21
  397.0 12.8 fusion.143
  428.0 5.7 fusion.35
  434.4 6.6 fusion.157
  451.5 24.0 %concatenate.76 = bf16[2,2736,384]{2,1,0:T(8,128)(2,1)} concatenate(bf16[2,1368,384]{2,1,0:T(8,128)(2,1)} %collective-permute-done.9, bf16[2,684,384]{2,1,0:T(8,128)(2,1)S(1)} %copy-done.52, bf16[2,342,384]{2,1,0:T(8,128)(2,1)} %copy.337, bf16[2,171,384]{2,1,0:T(8,128)(2,1)} %copy.338, bf16[2,171,384]{2,1,0:T(8,128)(2,1)S(1)} %copy-done.78), dimensions={1} | concatenate | bytes 8404992 | tf_op jit(solution)/shard_map/concatenate | solution.py:99
  496.3 9.5 fusion.156
  541.3 44.0 %all-reduce.31 = (bf16[768]{0:T(1024)(128)(2,1)S(1)}, bf16[768]{0:T(1024)(128)(2,1)S(1)}, bf16[3072]{0:T(1024)(128)(2,1)S(1)}, bf16[3072]{0:T(1024)(128)(2,1)S(1...) all-reduce(bf16[768]{0:T(1024)(128)(2,1)S(1)} %dynamic-update-slice, ...), channel_id=1, replica_groups=mesh['seq'=16,'head'=2] {'seq','head'}, use_global_device_ids=true, to_apply=%add.9 | all-reduce | flops 11520 | bytes 46080
  589.7 16.8 all-gather.4.cloned.1.call-done
  606.5 21.4 fusion.250
  627.9 43.8 %all-gather.6.cloned.1.call-done = bf16[3072,768]{1,0:T(8,128)(2,1)} async-done(((bf16[96,768]{1,0:T(8,128)(2,1)}), bf16[3072,768]{1,0:T(8,128)(2,1)}) %all-gather.6.cloned.1.call-update) | async-done | bytes 4718608 | tf_op jit(solution)/shard_map/all_gather | solution.py:147
  671.8 7.4 multiply_reduce_fusion.7
  682.5 11.3 convert_reduce_fusion
  693.8 7.1 multiply_reduce_fusion.21
  736.9 5.8 fusion.128
  753.9 9.2 fusion.162
  763.2 10.4 convolution_multiply_fusion.2
  795.0 6.0 fusion.262
  801.1 8.9 fusion.52
  810.0 24.1 %fusion.153 = f32[171,6,64]{0,2,1:T(8,128)} fusion(bf16[2736,6,64]{0,2,1:T(8,128)(2,1)S(1)} %bitcast.463, f32[6,171,2736]{2,1,0:T(8,128)} %fusion.262, f32[6,171]{1,0:T(8,128)S(1)} %bitcast.498, f32[6,171,2736]{2,1,0:T(8,128)} %copy-done.28, f32[6,171]{1,0:T(8,128)S(1)} %copy-done.240, s32[6,171]{1,0:T(8,128)S(1)} %copy-done.177, ...), kind=kOutput, calls=%fused_computation.257 | convolution fusion | flops 407104128 | bytes 24916410 | tf_op jit(solution)/shard_map/hqk,khd->qhd/dot_general | solution.py:339
  834.1 27.6 %convolution_multiply_fusion = f32[6,64,2736]{2,1,0:T(8,128)} fusion(bf16[171,6,64]{2,0,1:T(8,128)(2,1)} %multiply_reduce_fusion.16, f32[6,171,2736]{2,1,0:T(8,128)} %fusion.262, f32[6,171]{1,0:T(8,128)S(1)} %bitcast.499, f32[6,171,2736]{2,1,0:T(8,128)} %copy-done.28, f32[6,171]{1,0:T(8,128)} %get-tuple-element.79, s32[6,171]{1,0:T(8,128)S(1)} %copy-done.177, ...), kind=kOutput, calls=%fused_computation.94 | convolution fusion | flops 408089088 | bytes 26886330 | tf_op jit(solution)/shard_map/hqk,qhd->khd/dot_general | solution.py:343
  864.1 9.2 multiply_reduce_fusion.17
  873.6 6.4 fusion.261
  880.0 9.0 fusion.37
  889.4 27.9 %fusion.147 = f32[256,6,64]{0,2,1:T(8,128)} fusion(bf16[2048,6,64]{0,2,1:T(8,128)(2,1)S(1)} %bitcast.476, f32[6,256,2048]{2,1,0:T(8,128)} %fusion.261, f32[6,256]{1,0:T(8,128)S(1)} %bitcast.500, f32[6,256,2048]{2,1,0:T(8,128)} %copy-done.22, f32[6,256]{1,0:T(8,128)S(1)} %copy-done.239, s32[6,256]{1,0:T(8,128)S(1)} %copy-done.175, ...), kind=kOutput, calls=%fused_computation.255 | convolution fusion | flops 456232448 | bytes 27213312 | tf_op jit(solution)/shard_map/hqk,khd->qhd/dot_general | solution.py:339
  917.3 29.7 %fusion.98 = f32[6,64,2048]{2,1,0:T(8,128)} fusion(bf16[256,6,64]{0,2,1:T(8,128)(2,1)S(1)} %copy-done.123, f32[6,256,2048]{2,1,0:T(8,128)} %fusion.261, f32[6,256]{1,0:T(8,128)S(1)} %bitcast.501, f32[6,256,2048]{2,1,0:T(8,128)} %copy-done.22, f32[6,256]{1,0:T(8,128)S(1)} %copy-done.239, s32[6,256]{1,0:T(8,128)S(1)} %copy-done.175, ...), kind=kOutput, calls=%fused_computation.148 | convolution fusion | flops 456920576 | bytes 28589568 | tf_op jit(solution)/shard_map/hqk,qhd->khd/dot_general | solution.py:343
  948.3 9.9 multiply_reduce_fusion.18
  960.0 10.4 fusion.260
  970.4 14.7 fusion.24
  985.1 50.4 %fusion.140 = f32[512,6,64]{0,2,1:T(8,128)S(1)} fusion(bf16[2048,6,64]{0,2,1:T(8,128)(2,1)S(1)} %bitcast.474, f32[6,512,2048]{2,1,0:T(8,128)} %fusion.260, f32[6,512]{1,0:T(8,128)S(1)} %copy.379, f32[6,512,2048]{2,1,0:T(8,128)} %copy-done.4, f32[6,512]{1,0:T(8,128)S(1)} %copy-done.217, s32[6,512]{1,0:T(8,128)S(1)} %copy-done.163, ...), kind=kOutput, calls=%fused_computation.252 | convolution fusion | flops 912462848 | bytes 52792320 | tf_op jit(solution)/shard_map/hqk,khd->qhd/dot_general | solution.py:339
  1035.5 50.3 %fusion.101 = f32[6,64,2048]{2,1,0:T(8,128)} fusion(bf16[512,6,64]{0,2,1:T(8,128)(2,1)S(1)} %copy-done.111, f32[6,512,2048]{2,1,0:T(8,128)} %fusion.260, f32[6,512]{1,0:T(8,128)S(1)} %copy.379, f32[6,512,2048]{2,1,0:T(8,128)} %copy-done.4, f32[6,512]{1,0:T(8,128)S(1)} %copy-done.217, s32[6,512]{1,0:T(8,128)S(1)} %copy-done.163, ...), kind=kOutput, calls=%fused_computation.149 | convolution fusion | flops 913052672 | bytes 53971968 | tf_op jit(solution)/shard_map/hqk,qhd->khd/dot_general | solution.py:343
  1093.2 21.2 fusion.168
  1114.4 24.4 %fusion.10 = f32[6,64,2048]{2,1,0:T(8,128)} fusion(f32[1024,6,64]{0,2,1:T(8,128)S(1)} %copy-done.11, f32[1024,6]{0,1:T(8,128)S(1)} %copy-done.84, f32[6,1024,2048]{2,1,0:T(8,128)} %get-tuple-element.140, f32[6,1024]{1,0:T(8,128)S(1)} %copy-done.183, s32[6,1024]{1,0:T(8,128)S(1)} %copy-done.135, s32[2048]{0:T(1024)S(1)} %bitcast.495, ...), kind=kOutput, calls=%fused_computation.15 | convolution fusion | flops 1699479552 | bytes 55140352 | tf_op jit(solution)/shard_map/hqk,qhd->khd/dot_general | solution.py:346
  1194.9 86.0 %fusion.84 = f32[6,64,2048]{2,1,0:T(8,128)} fusion(bf16[1024,6,64]{0,2,1:T(8,128)(2,1)S(1)} %bitcast.453, f32[6,1024,2048]{2,1,0:T(8,128)} %fusion.168, f32[6,1024]{1,0:T(8,128)S(1)} %copy-done.185, f32[6,1024,2048]{2,1,0:T(8,128)} %get-tuple-element.140, f32[6,1024]{1,0:T(8,128)S(1)} %copy-done.184, s32[6,1024]{1,0:T(8,128)S(1)} %copy-done.135, ...), kind=kOutput, calls=%fused_computation.122 | convolution fusion | flops 1825316864 | bytes 104685568 | tf_op jit(solution)/shard_map/hqk,qhd->khd/dot_general | solution.py:343
  1285.6 80.0 %convert_reduce_fusion.6 = (f32[6,64]{1,0:T(8,128)S(1)}, bf16[1024,6,64]{0,2,1:T(8,128)(2,1)}) fusion(f32[1024,6,64]{0,2,1:T(8,128)} %copy.443, f32[1024,6]{0,1:T(8,128)S(1)} %copy-done.98, f32[1024,6,64]{0,2,1:T(8,128)} %copy.442, f32[1024,6]{0,1:T(8,128)S(1)} %copy-done.102, f32[1024,6,64]{0,2,1:T(8,128)} %copy.391, f32[1024,6]{0,1:T(8,128)S(1)} %copy-done.88, ...), kind=kOutput, calls=%fused_computation.216 | convolution fusion | flops 1829248640 | bytes 109504000 | tf_op jit(solution)/shard_map/hqk,khd->qhd/dot_general | solution.py:339
  1384.3 7.3 collective-permute-done.25
  1420.0 16.3 collective-permute-done.27
  1441.0 7.7 slice.317
  1448.7 9.5 copy.445
  1478.0 6.6 mul.1647
  1484.6 6.1 copy.404
  1500.3 6.2 copy.408
  1506.6 13.4 collective-permute-done.23
  1525.3 7.6 slice.307
  1532.9 9.5 copy.444
  1542.4 7.7 multiply_add_fusion
  1569.4 7.3 fusion.246
  1577.9 8.1 fusion.270
  1587.9 6.8 add_convert_fusion.4
  1594.8 63.2 %all-reduce.28 = (f32[384]{0:T(512)S(1)}, f32[384]{0:T(512)S(1)}, f32[384]{0:T(512)S(1)}, f32[384]{0:T(512)S(1)}) all-reduce(f32[384]{0:T(512)S(1)} %reduce_sum.768, f32[384]{0:T(512)S(1)} %reduce_sum.770, f32[384]{0:T(512)S(1)} %copy-done.254, f32[384]{0:T(512)S(1)} %copy-done.255), channel_id=7, replica_groups=mesh['seq'=16,'head'=2] {'seq'}, use_global_device_ids=true, to_apply=%region_69.70.clone | all-reduce | flops 1536 | bytes 12288
  1668.7 38.5 %all-reduce.27 = (f32[768]{0:T(1024)S(1)}, f32[768]{0:T(1024)S(1)}, f32[768]{0:T(1024)S(1)}, f32[768]{0:T(1024)S(1)}, f32[768]{0:T(1024)S(1)}, /*index=5*/f32[30...) all-reduce(f32[768]{0:T(1024)S(1)} %get-tuple-element.28, ...), channel_id=4, replica_groups=mesh['seq'=16,'head'=2] {'seq','head'}, use_global_device_ids=true, to_apply=%region_64.65.clone | all-reduce | flops 13824 | bytes 110592
  1715.1 127.7 %reduce-scatter.13.cloned.1.call-done = f32[48,384]{1,0:T(8,128)} async-done(((f32[768,384]{1,0:T(8,128)}), f32[48,384]{1,0:T(8,128)}) %reduce-scatter.13.cloned.1.call-update) | async-done | bytes 73744 | tf_op jit(solution)/shard_map/reduce_scatter | solution.py:394
  1842.8 127.8 %reduce-scatter.15.cloned.1.call-done = f32[48,384]{1,0:T(8,128)} async-done(((f32[768,384]{1,0:T(8,128)}), f32[48,384]{1,0:T(8,128)}) %reduce-scatter.15.cloned.1.call-update) | async-done | bytes 73744 | tf_op jit(solution)/shard_map/reduce_scatter | solution.py:395
  1970.6 128.0 %reduce-scatter.17.cloned.1.call-done = f32[48,384]{1,0:T(8,128)} async-done(((f32[768,384]{1,0:T(8,128)}), f32[48,384]{1,0:T(8,128)}) %reduce-scatter.17.cloned.1.call-update) | async-done | bytes 73744 | tf_op jit(solution)/shard_map/reduce_scatter | solution.py:396
  2098.6 141.1 %reduce-scatter.21.cloned.1.call-done = f32[24,3072]{1,0:T(8,128)} async-done(((f32[768,3072]{1,0:T(8,128)}), f32[24,3072]{1,0:T(8,128)}) %reduce-scatter.21.cloned.1.call-update) | async-done | bytes 294928 | tf_op jit(solution)/shard_map/reduce_scatter | solution.py:404
  2239.7 142.2 %reduce-scatter.23.cloned.1.call-done = f32[96,768]{1,0:T(8,128)} async-done(((f32[3072,768]{1,0:T(8,128)}), f32[96,768]{1,0:T(8,128)}) %reduce-scatter.23.cloned.1.call-update) | async-done | bytes 294928 | tf_op jit(solution)/shard_map/reduce_scatter | solution.py:405
  (1030 shorter events, 609.9 us)
Async XLA Ops:
  8.0 524.7 %copy-start = (bf16[384,768]{1,0:T(8,128)(2,1)S(1)}, bf16[384,768]{1,0:T(8,128)(2,1)}, u32[]{:S(2)}) copy-start(bf16[384,768]{1,0:T(8,128)(2,1)} %param.31) | copy-start | bytes 1769476
  8.1 577.3 %reduce-scatter.9.cloned.1.call-start = ((), (), s32[]{:S(2)}) async-start(), calls=%async_computation.8 | async-start | bytes 2359296 | tf_op jit(solution)/shard_map/reduce_scatter | solution.py:256
  16.5 53.7 %copy-start.26 = (bf16[1024,384]{0,1:T(8,128)(2,1)}, bf16[1024,384]{0,1:T(8,128)(2,1)S(1)}, u32[]{:S(2)}) copy-start(bf16[1024,384]{0,1:T(8,128)(2,1)S(1)} %add_convert_fusion.7) | copy-start | bytes 2359300
  17.9 220.4 %collective-permute-start = (bf16[2,1024,384]{1,2,0:T(8,128)(2,1)}, bf16[2,1024,384]{1,2,0:T(8,128)(2,1)}, u32[]{:S(2)}, u32[]{:S(2)}) collective-permute-start(bf16[2,1024,384]{1,2,0:T(8,128)(2,1)} %pad_maximum_fusion.9), channel_id=1, source_target_pairs={{0,2},{2,4},{4,6},{6,8},{8,10},{10,12},{12,14},{14,16},{16,18},{18... | collective-permute-start | bytes 4718600 | tf_op jit(solution)/shard_map/ppermute | solution.py:18
  41.2 191.8 %copy-start.42 = (bf16[2,256,6,64]{1,3,2,0:T(8,128)(2,1)}, bf16[2,256,6,64]{1,3,2,0:T(8,128)(2,1)S(1)}, u32[]{:S(2)}) copy-start(bf16[2,256,6,64]{1,3,2,0:T(8,128)(2,1)S(1)} %fusion.122) | copy-start | bytes 1179652
  41.2 155.6 %collective-permute-start.3 = (bf16[2,256,384]{1,2,0:T(8,128)(2,1)S(1)}, bf16[2,256,384]{1,2,0:T(8,128)(2,1)}, u32[]{:S(2)}, u32[]{:S(2)}) collective-permute-start(bf16[2,256,384]{1,2,0:T(8,128)(2,1)S(1)} %bitcast.439), channel_id=1, source_target_pairs={{0,2},{2,4},{4,6},{6,8},{8,10},{10,12},{12,14},{14,16},{16,18},{18... | collective-permute-start | bytes 1179656 | tf_op jit(solution)/shard_map/ppermute | solution.py:18
  50.7 71.1 %copy-start.193 = (s32[6]{0:T(128)}, s32[6]{0:T(128)S(1)}, u32[]{:S(2)}) copy-start(s32[6]{0:T(128)S(1)} %get-tuple-element.163) | copy-start | bytes 76
  59.5 158.1 %collective-permute-start.1 = (bf16[2,512,384]{1,2,0:T(8,128)(2,1)}, bf16[2,512,384]{1,2,0:T(8,128)(2,1)}, u32[]{:S(2)}, u32[]{:S(2)}) collective-permute-start(bf16[2,512,384]{1,2,0:T(8,128)(2,1)} %bitcast.9), channel_id=1, source_target_pairs={{0,2},{2,4},{4,6},{6,8},{8,10},{10,12},{12,14},{14,16},{16,18},{18... | collective-permute-start | bytes 2359304 | tf_op jit(solution)/shard_map/ppermute | solution.py:18
  63.7 50.8 %copy-start.200 = (s32[6]{0:T(128)}, s32[6]{0:T(128)S(1)}, u32[]{:S(2)}) copy-start(s32[6]{0:T(128)S(1)} %get-tuple-element.157) | copy-start | bytes 76
  94.1 73.7 %collective-permute-start.10 = (bf16[2,86,384]{1,2,0:T(8,128)(2,1)S(1)}, bf16[2,86,384]{1,2,0:T(8,128)(2,1)}, u32[]{:S(2)}, u32[]{:S(2)}) collective-permute-start(bf16[2,86,384]{1,2,0:T(8,128)(2,1)S(1)} %bitcast.456), channel_id=1, source_target_pairs={{0,2},{2,4},{4,6},{6,8},{8,10},{10,12},{12,14},{14,16},{16,18},{18... | collective-permute-start | bytes 396296 | tf_op jit(solution)/shard_map/ppermute | solution.py:18
  97.9 91.1 %copy-start.153 = (f32[6,6]{0,1:T(8,128)}, f32[6,6]{0,1:T(8,128)S(1)}, u32[]{:S(2)}) copy-start(f32[6,6]{0,1:T(8,128)S(1)} %get-tuple-element.133) | copy-start | bytes 436
  110.1 63.2 %collective-permute-start.6 = (bf16[2,171,384]{1,2,0:T(8,128)(2,1)}, bf16[2,171,384]{1,2,0:T(8,128)(2,1)}, u32[]{:S(2)}, u32[]{:S(2)}) collective-permute-start(bf16[2,171,384]{1,2,0:T(8,128)(2,1)} %bitcast.25), channel_id=1, source_target_pairs={{0,2},{2,4},{4,6},{6,8},{8,10},{10,12},{12,14},{14,16},{16,18},{18... | collective-permute-start | bytes 787976 | tf_op jit(solution)/shard_map/ppermute | solution.py:18
  135.2 216.6 %copy-start.140 = (pred[6,1376]{1,0:T(8,128)(4,1)}, pred[6,1376]{1,0:T(8,128)(4,1)S(1)}, u32[]{:S(2)}) copy-start(pred[6,1376]{1,0:T(8,128)(4,1)S(1)} %and_bitcast_fusion.3) | copy-start | bytes 24772
  169.7 32.5 %collective-permute-start.11 = (bf16[2,172,384]{1,2,0:T(8,128)(2,1)}, bf16[2,172,384]{1,2,0:T(8,128)(2,1)}, u32[]{:S(2)}, u32[]{:S(2)}) collective-permute-start(bf16[2,172,384]{1,2,0:T(8,128)(2,1)} %pad_maximum_fusion.17), channel_id=1, source_target_pairs={{0,4},{2,6},{4,8},{6,10},{8,12},{10,14},{12,16},{14,18},{16,20},{1... | collective-permute-start | bytes 792584 | tf_op jit(solution)/shard_map/ppermute | solution.py:18
  176.4 47.0 %collective-permute-start.7 = (bf16[2,342,384]{2,0,1:T(2,128)(2,1)}, bf16[2,342,384]{2,0,1:T(2,128)(2,1)S(1)}, u32[]{:S(2)}, u32[]{:S(2)}) collective-permute-start(bf16[2,342,384]{2,0,1:T(2,128)(2,1)} %copy.330), channel_id=1, source_target_pairs={{0,4},{2,6},{4,8},{6,10},{8,12},{10,14},{12,16},{14,18},{16,20},{1... | collective-permute-start | bytes 1575944 | tf_op jit(solution)/shard_map/ppermute | solution.py:18
  179.7 109.8 %copy-start.134 = (s32[6,1024]{1,0:T(8,128)}, s32[6,1024]{1,0:T(8,128)S(1)}, u32[]{:S(2)}) copy-start(s32[6,1024]{1,0:T(8,128)S(1)} %iota_add_fusion) | copy-start | bytes 73732
  179.9 49.7 %copy-start.76 = (bf16[2,86,384]{2,1,0:T(8,128)(2,1)}, bf16[2,86,384]{2,1,0:T(8,128)(2,1)S(1)}, u32[]{:S(2)}) copy-start(bf16[2,86,384]{2,1,0:T(8,128)(2,1)S(1)} %copy.348) | copy-start | bytes 396292
  198.8 34.2 %collective-permute-start.4 = (bf16[2,512,384]{1,2,0:T(8,128)(2,1)}, bf16[2,512,384]{1,2,0:T(8,128)(2,1)S(1)}, u32[]{:S(2)}, u32[]{:S(2)}) collective-permute-start(bf16[2,512,384]{1,2,0:T(8,128)(2,1)} %pad_maximum_fusion.14), channel_id=1, source_target_pairs={{0,4},{2,6},{4,8},{6,10},{8,12},{10,14},{12,16},{14,18},{16,20},{1... | collective-permute-start | bytes 2359304 | tf_op jit(solution)/shard_map/ppermute | solution.py:18
  206.6 23.0 collective-permute-start.12
  210.8 78.7 %copy-start.191 = (pred[6,1024]{1,0:T(8,128)(4,1)}, pred[6,1024]{1,0:T(8,128)(4,1)S(1)}, u32[]{:S(2)}) copy-start(pred[6,1024]{1,0:T(8,128)(4,1)S(1)} %iota_compare_fusion) | copy-start | bytes 18436
  220.4 149.1 %collective-permute-start.2 = (bf16[2,1024,384]{1,2,0:T(8,128)(2,1)}, bf16[2,1024,384]{1,2,0:T(8,128)(2,1)}, u32[]{:S(2)}, u32[]{:S(2)}) collective-permute-start(bf16[2,1024,384]{1,2,0:T(8,128)(2,1)} %pad_maximum_fusion.10), channel_id=1, source_target_pairs={{0,4},{2,6},{4,8},{6,10},{8,12},{10,14},{12,16},{14,18},{16,20},{1... | collective-permute-start | bytes 4718600 | tf_op jit(solution)/shard_map/ppermute | solution.py:18
  227.2 89.4 %collective-permute-start.8 = (bf16[2,684,384]{2,0,1:T(2,128)(2,1)S(1)}, bf16[2,684,384]{2,0,1:T(2,128)(2,1)S(1)}, u32[]{:S(2)}, u32[]{:S(2)}) collective-permute-start(bf16[2,684,384]{2,0,1:T(2,128)(2,1)S(1)} %pad_maximum_fusion.13), channel_id=1, source_target_pairs={{0,8},{2,10},{4,12},{6,14},{8,16},{10,18},{12,20},{14,22},{16,24},... | collective-permute-start | bytes 3151880 | tf_op jit(solution)/shard_map/ppermute | solution.py:18
  230.8 103.6 %collective-permute-start.13 = (bf16[2,688,384]{2,1,0:T(8,128)(2,1)S(1)}, bf16[2,688,384]{2,1,0:T(8,128)(2,1)}, u32[]{:S(2)}, u32[]{:S(2)}) collective-permute-start(bf16[2,688,384]{2,1,0:T(8,128)(2,1)S(1)} %pad_maximum_fusion.12), channel_id=1, source_target_pairs={{0,16},{2,18},{4,20},{6,22},{8,24},{10,26},{12,28},{14,30},{1,17},... | collective-permute-start | bytes 3170312 | tf_op jit(solution)/shard_map/ppermute | solution.py:18
  235.7 184.5 %collective-permute-start.5 = (bf16[2,1024,384]{1,2,0:T(8,128)(2,1)}, bf16[2,1024,384]{1,2,0:T(8,128)(2,1)}, u32[]{:S(2)}, u32[]{:S(2)}) collective-permute-start(bf16[2,1024,384]{1,2,0:T(8,128)(2,1)} %pad_maximum_fusion.11), channel_id=1, source_target_pairs={{0,8},{2,10},{4,12},{6,14},{8,16},{10,18},{12,20},{14,22},{16,24},... | collective-permute-start | bytes 4718600 | tf_op jit(solution)/shard_map/ppermute | solution.py:18
  240.4 49.1 %copy-start.41 = (bf16[1,2048,384]{1,2,0:T(8,128)(2,1)}, bf16[1,2048,384]{1,2,0:T(8,128)(2,1)S(1)}, u32[]{:S(2)}) copy-start(bf16[1,2048,384]{1,2,0:T(8,128)(2,1)S(1)} %get-tuple-element.101) | copy-start | bytes 4718596
  262.7 53.2 %copy-start.104 = (f32[6,1024]{1,0:T(8,128)}, f32[6,1024]{1,0:T(8,128)S(1)}, u32[]{:S(2)}) copy-start(f32[6,1024]{1,0:T(8,128)S(1)} %get-tuple-element.139) | copy-start | bytes 73732
  330.3 121.1 %collective-permute-start.9 = (bf16[2,1368,384]{2,1,0:T(8,128)(2,1)}, bf16[2,1368,384]{2,1,0:T(8,128)(2,1)}, u32[]{:S(2)}, u32[]{:S(2)}) collective-permute-start(bf16[2,1368,384]{2,1,0:T(8,128)(2,1)} %copy.335), channel_id=1, source_target_pairs={{0,16},{2,18},{4,20},{6,22},{8,24},{10,26},{12,28},{14,30},{1,17},... | collective-permute-start | bytes 6303752 | tf_op jit(solution)/shard_map/ppermute | solution.py:18
  532.4 184.9 %copy-start.138 = (f32[1024]{0:T(1024)}, f32[1024]{0:T(1024)S(1)}, u32[]{:S(2)}) copy-start(f32[1024]{0:T(1024)S(1)} %get-tuple-element.120) | copy-start | bytes 12292
  535.0 71.5 %all-gather.4.cloned.1.call-start = ((), (), s32[]{:S(2)}) async-start(), calls=%async_computation.9 | async-start | bytes 4866048 | tf_op jit(solution)/shard_map/all_gather | solution.py:146
  535.6 136.2 %all-gather.6.cloned.1.call-start = ((), (), s32[]{:S(2)}) async-start(), calls=%async_computation.10 | async-start | bytes 4866048 | tf_op jit(solution)/shard_map/all_gather | solution.py:147
  536.2 184.5 %all-gather.8.cloned.1.call-start = ((), (), s32[]{:S(2)}) async-start(), calls=%async_computation.11 | async-start | bytes 2359296 | tf_op jit(solution)/shard_map/all_gather | solution.py:293
  585.3 42.6 %copy-start.248 = (f32[768]{0:T(1024)}, f32[768]{0:T(1024)S(1)}, u32[]{:S(2)}) copy-start(f32[768]{0:T(1024)S(1)} %convert_element_type.494) | copy-start | bytes 9220
  585.3 115.7 %copy-start.220 = (f32[768]{0:T(1024)}, f32[768]{0:T(1024)S(1)}, u32[]{:S(2)}) copy-start(f32[768]{0:T(1024)S(1)} %convert_element_type.493) | copy-start | bytes 9220
  588.2 112.7 %copy-start.203 = (f32[512]{0:T(512)}, f32[512]{0:T(512)S(1)}, u32[]{:S(2)}) copy-start(f32[512]{0:T(512)S(1)} %broadcast_multiply_fusion.10) | copy-start | bytes 6148
  589.7 111.3 %copy-start.233 = (f32[512]{0:T(512)}, f32[512]{0:T(512)S(1)}, u32[]{:S(2)}) copy-start(f32[512]{0:T(512)S(1)} %fusion.198) | copy-start | bytes 6148
  589.7 82.1 %copy-start.54 = (bf16[512,768]{1,0:T(8,128)(2,1)S(1)}, bf16[512,768]{1,0:T(8,128)(2,1)}, u32[]{:S(2)}) copy-start(bf16[512,768]{1,0:T(8,128)(2,1)} %param.41) | copy-start | bytes 2359300
  704.6 955.8 %reduce-scatter.11.cloned.1.call-start = ((), (), s32[]{:S(2)}) async-start(), calls=%async_computation.12 | async-start | bytes 2359296 | tf_op jit(solution)/shard_map/reduce_scatter | solution.py:374
  917.3 31.0 %copy-start.81 = (f32[512,2]{1,0:T(8,128)S(1)}, f32[512,2]{1,0:T(8,128)}, u32[]{:S(2)}) copy-start(f32[512,2]{1,0:T(8,128)} %sub.526) | copy-start | bytes 12292
  985.1 50.4 %copy-start.111 = (bf16[512,6,64]{0,2,1:T(8,128)(2,1)S(1)}, bf16[512,6,64]{0,2,1:T(8,128)(2,1)}, u32[]{:S(2)}) copy-start(bf16[512,6,64]{0,2,1:T(8,128)(2,1)} %copy.314) | copy-start | bytes 1179652
  1035.5 51.4 %copy-start.5 = (f32[6,64,1376]{2,1,0:T(8,128)S(1)}, f32[6,64,1376]{2,1,0:T(8,128)}, u32[]{:S(2)}) copy-start(f32[6,64,1376]{2,1,0:T(8,128)} %fusion.131) | copy-start | bytes 6340612
  1091.8 273.8 %collective-permute-start.24 = (bf16[2,688,384]{2,1,0:T(8,128)(2,1)}, bf16[2,688,384]{2,1,0:T(8,128)(2,1)}, u32[]{:S(2)}, u32[]{:S(2)}) collective-permute-start(bf16[2,688,384]{2,1,0:T(8,128)(2,1)} %copy.421), channel_id=1, source_target_pairs={{16,0},{18,2},{20,4},{22,6},{24,8},{26,10},{28,12},{30,14},{17,1},... | collective-permute-start | bytes 3170312 | tf_op jit(solution)/shard_map/ppermute | solution.py:18
  1157.9 236.8 %collective-permute-start.20 = (bf16[2,1368,384]{2,1,0:T(8,128)(2,1)}, bf16[2,1368,384]{2,1,0:T(8,128)(2,1)}, u32[]{:S(2)}, u32[]{:S(2)}) collective-permute-start(bf16[2,1368,384]{2,1,0:T(8,128)(2,1)} %copy.411), channel_id=1, source_target_pairs={{16,0},{18,2},{20,4},{22,6},{24,8},{26,10},{28,12},{30,14},{17,1},... | collective-permute-start | bytes 6303752 | tf_op jit(solution)/shard_map/ppermute | solution.py:18
  1176.8 200.6 %collective-permute-start.17 = (bf16[2,1024,384]{1,2,0:T(8,128)(2,1)}, bf16[2,1024,384]{1,2,0:T(8,128)(2,1)}, u32[]{:S(2)}, u32[]{:S(2)}) collective-permute-start(bf16[2,1024,384]{1,2,0:T(8,128)(2,1)} %fusion.93), channel_id=1, source_target_pairs={{8,0},{10,2},{12,4},{14,6},{16,8},{18,10},{20,12},{22,14},{24,16},... | collective-permute-start | bytes 4718600 | tf_op jit(solution)/shard_map/ppermute | solution.py:18
  1193.5 213.4 %collective-permute-start.15 = (bf16[2,1024,384]{1,2,0:T(8,128)(2,1)}, bf16[2,1024,384]{1,2,0:T(8,128)(2,1)}, u32[]{:S(2)}, u32[]{:S(2)}) collective-permute-start(bf16[2,1024,384]{1,2,0:T(8,128)(2,1)} %fusion.94), channel_id=1, source_target_pairs={{4,0},{6,2},{8,4},{10,6},{12,8},{14,10},{16,12},{18,14},{20,16},{2... | collective-permute-start | bytes 4718600 | tf_op jit(solution)/shard_map/ppermute | solution.py:18
  1284.3 132.1 %collective-permute-start.14 = (bf16[2,1024,384]{1,2,0:T(8,128)(2,1)}, bf16[2,1024,384]{1,2,0:T(8,128)(2,1)}, u32[]{:S(2)}, u32[]{:S(2)}) collective-permute-start(bf16[2,1024,384]{1,2,0:T(8,128)(2,1)} %fusion.95), channel_id=1, source_target_pairs={{2,0},{4,2},{6,4},{8,6},{10,8},{12,10},{14,12},{16,14},{18,16},{20... | collective-permute-start | bytes 4718600 | tf_op jit(solution)/shard_map/ppermute | solution.py:18
  1372.2 19.4 collective-permute-start.25
  1383.0 85.1 %collective-permute-start.18 = (bf16[2,512,384]{1,2,0:T(8,128)(2,1)}, bf16[2,512,384]{1,2,0:T(8,128)(2,1)}, u32[]{:S(2)}, u32[]{:S(2)}) collective-permute-start(bf16[2,512,384]{1,2,0:T(8,128)(2,1)} %slice.415), channel_id=1, source_target_pairs={{4,0},{6,2},{8,4},{10,6},{12,8},{14,10},{16,12},{18,14},{20,16},{2... | collective-permute-start | bytes 2359304 | tf_op jit(solution)/shard_map/ppermute | solution.py:18
  1393.4 21.3 collective-permute-start.26
  1405.6 52.6 %collective-permute-start.21 = (bf16[2,684,384]{2,0,1:T(2,128)(2,1)S(1)}, bf16[2,684,384]{2,0,1:T(2,128)(2,1)}, u32[]{:S(2)}, u32[]{:S(2)}) collective-permute-start(bf16[2,684,384]{2,0,1:T(2,128)(2,1)S(1)} %copy.413), channel_id=1, source_target_pairs={{8,0},{10,2},{12,4},{14,6},{16,8},{18,10},{20,12},{22,14},{24,16},... | collective-permute-start | bytes 3151880 | tf_op jit(solution)/shard_map/ppermute | solution.py:18
  1411.1 61.1 %collective-permute-start.16 = (bf16[2,512,384]{1,2,0:T(8,128)(2,1)}, bf16[2,512,384]{1,2,0:T(8,128)(2,1)}, u32[]{:S(2)}, u32[]{:S(2)}) collective-permute-start(bf16[2,512,384]{1,2,0:T(8,128)(2,1)} %slice.416), channel_id=1, source_target_pairs={{2,0},{4,2},{6,4},{8,6},{10,8},{12,10},{14,12},{16,14},{18,16},{20... | collective-permute-start | bytes 2359304 | tf_op jit(solution)/shard_map/ppermute | solution.py:18
  1415.0 21.2 collective-permute-start.27
  1466.5 24.2 %collective-permute-start.22 = (bf16[2,342,384]{2,0,1:T(2,128)(2,1)S(1)}, bf16[2,342,384]{2,0,1:T(2,128)(2,1)}, u32[]{:S(2)}, u32[]{:S(2)}) collective-permute-start(bf16[2,342,384]{2,0,1:T(2,128)(2,1)S(1)} %copy.415), channel_id=1, source_target_pairs={{4,0},{6,2},{8,4},{10,6},{12,8},{14,10},{16,12},{18,14},{20,16},{2... | collective-permute-start | bytes 1575944 | tf_op jit(solution)/shard_map/ppermute | solution.py:18
  1470.9 24.2 %collective-permute-start.19 = (bf16[2,256,384]{1,2,0:T(8,128)(2,1)}, bf16[2,256,384]{1,2,0:T(8,128)(2,1)}, u32[]{:S(2)}, u32[]{:S(2)}) collective-permute-start(bf16[2,256,384]{1,2,0:T(8,128)(2,1)} %slice.421), channel_id=1, source_target_pairs={{2,0},{4,2},{6,4},{8,6},{10,8},{12,10},{14,12},{16,14},{18,16},{20... | collective-permute-start | bytes 1179656 | tf_op jit(solution)/shard_map/ppermute | solution.py:18
  1493.4 26.6 %collective-permute-start.23 = (bf16[2,171,384]{1,2,0:T(8,128)(2,1)S(1)}, bf16[2,171,384]{1,2,0:T(8,128)(2,1)S(1)}, u32[]{:S(2)}, u32[]{:S(2)}) collective-permute-start(bf16[2,171,384]{1,2,0:T(8,128)(2,1)S(1)} %slice.420), channel_id=1, source_target_pairs={{2,0},{4,2},{6,4},{8,6},{10,8},{12,10},{14,12},{16,14},{18,16},{20... | collective-permute-start | bytes 787976 | tf_op jit(solution)/shard_map/ppermute | solution.py:18
  1554.6 160.5 %reduce-scatter.19.cloned.1.call-start = ((), (), s32[]{:S(2)}) async-start(), calls=%async_computation.16 | async-start | bytes 1253376 | tf_op jit(solution)/shard_map/reduce_scatter | solution.py:402
  1558.4 284.5 %reduce-scatter.13.cloned.1.call-start = ((), (), s32[]{:S(2)}) async-start(), calls=%async_computation.13 | async-start | bytes 1253376 | tf_op jit(solution)/shard_map/reduce_scatter | solution.py:394
  1562.1 408.5 %reduce-scatter.15.cloned.1.call-start = ((), (), s32[]{:S(2)}) async-start(), calls=%async_computation.14 | async-start | bytes 1253376 | tf_op jit(solution)/shard_map/reduce_scatter | solution.py:395
  1565.7 532.9 %reduce-scatter.17.cloned.1.call-start = ((), (), s32[]{:S(2)}) async-start(), calls=%async_computation.15 | async-start | bytes 1253376 | tf_op jit(solution)/shard_map/reduce_scatter | solution.py:396
  1569.3 670.3 %reduce-scatter.21.cloned.1.call-start = ((), (), s32[]{:S(2)}) async-start(), calls=%async_computation.17 | async-start | bytes 9732096 | tf_op jit(solution)/shard_map/reduce_scatter | solution.py:404
  1576.8 805.1 %reduce-scatter.23.cloned.1.call-start = ((), (), s32[]{:S(2)}) async-start(), calls=%async_computation.18 | async-start | bytes 9732096 | tf_op jit(solution)/shard_map/reduce_scatter | solution.py:405
  1587.9 72.5 %copy-start.137 = (f32[768]{0:T(1024)S(1)}, f32[768]{0:T(1024)}, u32[]{:S(2)}) copy-start(f32[768]{0:T(1024)} %copy-done.136) | copy-start | bytes 9220
  1594.7 70.6 %copy-start.17 = (f32[512,768]{1,0:T(8,128)S(1)}, f32[512,768]{1,0:T(8,128)}, u32[]{:S(2)}) copy-start(f32[512,768]{1,0:T(8,128)} %copy-done.16) | copy-start | bytes 4718596
  1594.7 70.6 %copy-start.209 = (f32[512]{0:T(512)S(1)}, f32[512]{0:T(512)}, u32[]{:S(2)}) copy-start(f32[512]{0:T(512)} %copy-done.208) | copy-start | bytes 6148
  1665.2 716.7 %copy-start.1 = (bf16[384,768]{1,0:T(8,128)(2,1)S(1)}, bf16[384,768]{1,0:T(8,128)(2,1)}, u32[]{:S(2)}) copy-start(bf16[384,768]{1,0:T(8,128)(2,1)} %param.31) | copy-start | bytes 1769476
  (242 other events, 1953.9 us)
Sparse Core Ops, SparseCore 0:
  535.1 12.6 reduce-scatter.8
  704.7 8.0 all-gather.7
  1554.7 30.3 reduce-scatter.10
  1590.2 124.7 reduce-scatter.18
  1720.2 122.5 reduce-scatter.12
  1848.0 122.5 reduce-scatter.14
  1975.9 122.6 reduce-scatter.16
  2105.1 134.5 reduce-scatter.20
  2247.2 134.6 reduce-scatter.22
Sparse Core Ops, SparseCore 1:
  538.8 67.6 all-gather.3
  609.7 62.0 all-gather.5
where the time goes:
time: 2400 us; the launch traced here: 2390 us
  waiting for transfers between devices  770 us (32%)
  matrix products  694 us (29%)
  local copies, waits for them, and re-layouts  402 us (17%)
  other arithmetic  286 us (12%)
  blocking collectives  151 us (6%)
  starting transfers between devices  66 us (3%)
    dot_general x5, matrix products, per_device(): jnp.einsum('hqk,qhd->khd', score_grad, query_block, preferred_element_typ...  204 us
    dot_general x5, matrix products, per_device(): jnp.einsum('hqk,khd->qhd', score_grad, key_block, preferred_element_type=...  192 us
    unnamed x3, blocking collectives  146 us
    reduce_scatter x1, waiting for transfers between devices, per_device(): lax.psum_scatter(down_weight_grad, ('seq', 'head'), scatter_dimension=0,...  142 us
    reduce_scatter x1, waiting for transfers between devices, per_device(): lax.psum_scatter(up_weight_grad, ('seq', 'head'), scatter_dimension=0, ti...  141 us
    reduce_scatter x1, waiting for transfers between devices, per_device(): lax.psum_scatter(value_weight_local, 'seq', scatter_dimension=0, tiled=True)  128 us
    reduce_scatter x1, waiting for transfers between devices, per_device(): lax.psum_scatter(key_weight_local, 'seq', scatter_dimension=0, tiled=True)  128 us
    reduce_scatter x1, waiting for transfers between devices, per_device(): lax.psum_scatter(query_weight_local, 'seq', scatter_dimension=0, tiled=True)  128 us
  transfers between devices with their start and end apart: 39, of which 12 were waited for; matrix products, arithmetic and copies ran while one was open for 35% of the time, Pallas kernels for 0%

commit v1 on v0

v1 whole, which is shorter than its diff:
```python
import functools

import jax
import jax.numpy as jnp
from jax import lax
from jax.experimental import pallas as pl
from jax.experimental.pallas import tpu as pltpu
from jax.sharding import PartitionSpec as P

HEAD_DIM = 64
W0 = 2048
RATES = (1, 2, 4, 6, 12)
EPS = 1e-05
NEG = -1e30
CHUNK = 256
BF = jnp.bfloat16
F32 = jnp.float32
VMEM_LIMIT = 56 * 2**20
LSE_ROW = 33
HALF = HEAD_DIM
BOTH = ("seq", "head")


def layer_norm(values, gain, shift):
    center = jnp.mean(values, axis=-1, keepdims=True)
    centered = values - center
    spread = jnp.mean(centered * centered, axis=-1, keepdims=True)
    return centered * lax.rsqrt(spread + EPS) * gain + shift


def gelu_norm(before, gain, shift):
    return layer_norm(jax.nn.gelu(before, approximate=False), gain, shift)


def dot_rows(left_side, right_side):
    return lax.dot_general(
        left_side, right_side, (((0,), (0,)), ((), ())), preferred_element_type=F32
    )


def dot_cols(left_side, right_side):
    return lax.dot_general(
        left_side, right_side, (((1,), (1,)), ((), ())), preferred_element_type=F32
    )


def mm(left_side, right_side):
    return jnp.dot(left_side, right_side, preferred_element_type=F32)


class Space:
    def __init__(self, stride, levels, window):
        self.stride = stride
        self.levels = levels
        self.factor = stride if stride == 2 else stride // 2
        self.base = window if stride == 2 else window // 2
        span = CHUNK if self.factor == 2 else 128 * self.factor
        self.chunks = []
        start, rows = 0, 0
        while start < self.base:
            size = min(span, self.base - start)
            real = -(-size // self.factor)
            self.chunks.append((start, size, rows, min(128, -(-real // 16) * 16)))
            rows += 128
            start += size
        self.queries = rows
        self.keys = rows - 128 + self.chunks[-1][3]


class Plan:
    def __init__(self, tok_rows, seq_count):
        self.window = 2 * tok_rows
        windows = seq_count // 2
        self.spans = [min(2**k, windows) for k in range(len(RATES))]
        self.fold = self.spans[3] == self.spans[4]
        self.seq_count = seq_count
        top = windows.bit_length() - 1
        lists = {2: [1], 4: [2], 6: [2, 3]}
        if not self.fold:
            lists[12] = [3, 4]
        lists = {s: [b for b in bs if b <= top] for s, bs in lists.items()}
        self.spaces = [Space(s, bs, self.window) for s, bs in lists.items() if bs]
        self.levels = sorted({b for s in self.spaces for b in s.levels})
        self.packet = {}
        for level in self.levels:
            parts, at = [], 0
            for space in self.spaces:
                if level in space.levels:
                    parts.append((space.stride, at))
                    at += space.keys
            self.packet[level] = (dict(parts), at)

    def space(self, stride):
        return [s for s in self.spaces if s.stride == stride][0]

    def masks(self, level):
        found = [0]
        for bit in reversed(range(level - 1)):
            found = found + [m | (1 << bit) for m in found]
        return found


def first_of(plan, stride, window_index, heads):
    if stride == 2:
        return heads % 2
    if stride == 4:
        return heads % 4
    span = plan.spans[RATES.index(stride)]
    into = (window_index % span) * plan.window
    return jnp.mod(heads - into, stride)


def flags_at(plan, window_index, heads, place):
    code = jnp.zeros(place.shape, jnp.int32)
    for bit, stride in enumerate((2, 4, 6, 12)):
        first = first_of(plan, stride, window_index, heads)[:, None]
        code = code + jnp.where(jnp.mod(place - first, stride) == 0, 1 << bit, 0)
    return code


def weight_log(code_here, code_there, plan, stride):
    both = code_here & code_there
    f4, f6, f12 = [jnp.where((both & b) > 0, 1.0, 0.0) for b in (2, 4, 8)]
    if stride == 1:
        total = 1.0 + jnp.where((both & 1) > 0, 1.0, 0.0) + f4 + f6 + f12
    elif stride == 2:
        total = 1.0 + f4 + f6 + f12
    elif stride == 4:
        total = 1.0 + f12
    elif stride == 6 and plan.fold:
        total = 1.0 + f12
    else:
        total = jnp.ones_like(f12)
    return jnp.log(total)


def places(plan, stride, count, window_index, heads):
    steps = jnp.arange(count, dtype=jnp.int32)[None, :]
    if stride == 1:
        return jnp.broadcast_to(steps, (heads.shape[0], count))
    return first_of(plan, stride, window_index, heads)[:, None] + stride * steps


def extra_keys(plan, stride, count, window_index, heads, on):
    place = places(plan, stride, count, window_index, heads)
    code = flags_at(plan, window_index, heads, place)[:, :, None]
    bad = ((place >= plan.window) | jnp.logical_not(on))[:, :, None]
    lane = lax.broadcasted_iota(jnp.int32, (1, 1, 2 * HALF), 2) - HALF
    hot = (lane >= 0) & (lane < 32) & ((lane & 15) == code)
    hot = hot | ((lane == 32) & bad) | ((lane >= LSE_ROW) & (lane < LSE_ROW + 3))
    return jnp.where(hot, 1.0, 0.0).astype(BF)


def extra_queries(plan, stride, count, window_index, heads):
    place = places(plan, stride, count, window_index, heads)
    code = flags_at(plan, window_index, heads, place)[:, None, :]
    row = lax.broadcasted_iota(jnp.int32, (1, HALF, 1), 1)
    value = weight_log(code, row & 15, plan, stride)
    high = lax.reduce_precision(value, 8, 7)
    out = jnp.where(row < 16, high, jnp.where(row < 32, value - high, 0.0))
    return jnp.where(row == 32, NEG, out).astype(BF)


def hot_rows(count, size, factor, first):
    row = lax.broadcasted_iota(jnp.int32, (count, size), 0)
    col = lax.broadcasted_iota(jnp.int32, (count, size), 1)
    return jnp.where(col == factor * row + first, 1.0, 0.0).astype(BF)


def hot_cols(size, count, factor, first):
    row = lax.broadcasted_iota(jnp.int32, (size, count), 0)
    col = lax.broadcasted_iota(jnp.int32, (size, count), 1)
    return jnp.where(row == factor * col + first, 1.0, 0.0).astype(BF)


def lanes_down(space, first, array):
    parts = []
    hot = {}
    for start, size, at, real in space.chunks:
        if size not in hot:
            hot[size] = hot_cols(size, 128, space.factor, first)
        parts.append(mm(array[:, start : start + size], hot[size]))
    return jnp.concatenate(parts, axis=1)


def lanes_up(space, first, array):
    parts = []
    hot = {}
    for start, size, at, real in space.chunks:
        if size not in hot:
            hot[size] = hot_rows(128, size, space.factor, first)
        parts.append(mm(array[:, at : at + 128], hot[size]))
    return jnp.concatenate(parts, axis=1)


def rows_down(space, first, array):
    parts = []
    for start, size, at, real in space.chunks:
        hot = hot_rows(real, size, space.factor, first)
        parts.append(mm(hot, array[start : start + size]))
    return jnp.concatenate(parts, axis=0)


def rows_up(space, first, array):
    parts = []
    for start, size, at, real in space.chunks:
        hot = hot_cols(size, real, space.factor, first)
        parts.append(mm(hot, array[at : at + real]))
    return jnp.concatenate(parts, axis=0)


def split_two(values):
    high = values.astype(BF)
    return high, (values - high.astype(F32)).astype(BF)


def thirds(values):
    high = values.astype(BF).astype(F32)
    rest = values - high
    middle = rest.astype(BF).astype(F32)
    return high, middle, rest - middle


def stat_rows(values, rows):
    high, middle, low = thirds(values)
    row = lax.broadcasted_iota(jnp.int32, (rows, values.shape[1]), 0)
    out = jnp.where(row == 0, high, jnp.where(row == 1, middle, jnp.where(row == 2, low, 0.0)))
    return out.astype(BF)


def stat_up(space, first, values):
    got = lanes_up(space, first, stat_rows(values, 16))
    return jnp.sum(got[0:8], axis=0, keepdims=True)


def stat_down(space, first, values):
    got = lanes_down(space, first, stat_rows(values, 16))
    return jnp.sum(got[0:8], axis=0, keepdims=True)


def wide_up(space, first, values):
    high, low = split_two(values)
    m = values.shape[0]
    got = lanes_up(space, first, jnp.concatenate([high, low], axis=0))
    return got[:m] + got[m:]


def chosen_lanes(space, first):
    lane = lax.broadcasted_iota(jnp.int32, (1, space.base), 1)
    return lax.rem(lane - first + 2 * space.factor, space.factor) == 0


def log_add(*values):
    top = functools.reduce(jnp.maximum, values)
    return top + jnp.log(functools.reduce(jnp.add, [jnp.exp(v - top) for v in values]))


def with_extra(packet, extra):
    lane = lax.broadcasted_iota(jnp.int32, packet.shape, 1)
    return jnp.where(lane < HALF, packet, extra)


def with_ones(packet):
    lane = lax.broadcasted_iota(jnp.int32, packet.shape, 1)
    ones = jnp.where(lane < 3, 1.0, 0.0).astype(BF)
    return jnp.where(lane >= HALF, packet, ones)


def causal(scores, size):
    above = scores.shape[0] - size
    key = lax.broadcasted_iota(jnp.int32, (size, size), 0)
    query = lax.broadcasted_iota(jnp.int32, (size, size), 1)
    last = jnp.where(key <= query, scores[above:], NEG)
    return jnp.concatenate([scores[:above], last], axis=0) if above else last


def attend(keys_extra, values_turned, queries, size=0):
    scores = mm(keys_extra, queries)
    if size:
        scores = causal(scores, size)
    top = jnp.max(scores, axis=0, keepdims=True)
    weights = jnp.exp(scores - top)
    total = jnp.sum(weights, axis=0, keepdims=True)
    out = mm(values_turned, weights.astype(BF))
    return out / total, top + jnp.log(total)


def attend_back(keys_extra, values_ones, keys_turned, queries, grads, rows, size=0):
    scores = mm(keys_extra, queries)
    if size:
        scores = causal(scores, size)
    weights = jnp.exp(scores)
    steps = (weights * mm(values_ones, grads)).astype(BF)
    lane = lax.broadcasted_iota(jnp.int32, rows.shape, 1)
    zero = jnp.zeros_like(rows)
    pair = mm(steps, jnp.where(lane < HALF, rows, zero))
    pair = pair + mm(weights.astype(BF), jnp.where(lane >= HALF, rows, zero))
    return pair, mm(keys_turned, steps) * HEAD_DIM**-0.5


def first_in(facts, head, stride):
    return facts[head * 4 + (2, 4, 6, 12).index(stride)]


def project_kernel(
    plan, group, facts, tok, gain, shift, wq, bq, wkv, bkv, normed, q_out, kv_out, *packets
):
    for start in range(0, plan.window, CHUNK):
        rows = slice(start, start + CHUNK)
        values = tok[rows].astype(F32)
        center = jnp.mean(values, axis=1, keepdims=True)
        values = values - center
        spread = jnp.mean(values * values, axis=1, keepdims=True)
        low = (values * lax.rsqrt(spread + EPS) * gain[...] + shift[...]).astype(BF)
        normed[rows] = low
        pair = (mm(low, wkv[...]) + bkv[...]).astype(BF)
        turned = (dot_cols(wq[...], low) + bq[...]).astype(BF) * jnp.asarray(HEAD_DIM**-0.5, BF)
        for head in range(group):
            kv_out[head, rows] = pair[:, head * 128 : head * 128 + 128]
            q_out[head, :, rows] = turned[head * HALF : head * HALF + HALF]
    for head in range(group):
        picked = {}
        for space in plan.spaces:
            first = first_in(facts, head, space.stride)
            source = kv_out[head] if space.stride == 2 else picked[2]
            picked[space.stride] = rows_down(space, first, source).astype(BF)
        for ref, level in zip(packets, plan.levels):
            for stride, at in plan.packet[level][0].items():
                ref[head, at : at + plan.space(stride).keys] = picked[stride]


def own_kernel(plan, block, kv, extra_k, q, extra_q, out, lse):
    keys_extra = with_extra(kv[0], extra_k[0])
    values_turned = kv[0].T[HALF:]
    queries = jnp.concatenate([q[0], extra_q[0]], axis=0)
    for start in range(0, plan.window, block):
        stop = start + block
        got, stat = attend(
            keys_extra[:stop], values_turned[:, :stop], queries[:, start:stop], block
        )
        out[0, :, start:stop] = got
        lse[0, :, start:stop] = jnp.broadcast_to(stat, (8, block))


def space_sources(plan, space, refs):
    found = []
    for level in space.levels:
        at = plan.packet[level][0][space.stride]
        for ref in refs[level]:
            found.append((level, ref, at))
    return found


def space_attend(plan, space, refs, extra_k, queries, out, lse):
    packet = jnp.concatenate(
        [ref[0, at : at + space.keys] for level, ref, at in space_sources(plan, space, refs)],
        axis=0,
    )
    keys_extra = with_extra(packet, extra_k)
    values_turned = packet.T[HALF:]
    block = min(512, space.queries)
    for start in range(0, space.queries, block):
        got, stat = attend(keys_extra, values_turned, queries[:, start : start + block])
        out[:, start : start + block] = got
        lse[:, start : start + block] = jnp.broadcast_to(stat, (8, block))


def reach_flag(plan, facts, group, space):
    flags = [facts[4 * group + level - 1] for level in space.levels]
    return functools.reduce(jnp.maximum, flags)


def queries_of(plan, space, facts, head, q, extra_q, held):
    first = first_in(facts, head, space.stride)
    source = q if space.stride == 2 else held[2]
    picked = lanes_down(space, first, source).astype(BF)
    held[space.stride] = picked
    return jnp.concatenate([picked, extra_q], axis=0)


def near_kernel(plan, group, facts, q, *refs):
    space = plan.spaces[0]
    count = len(plan.masks(1))
    packets, (extra_k, extra_q, out, lse) = refs[:count], refs[count:]
    head = pl.program_id(0)
    flag = reach_flag(plan, facts, group, space)

    @pl.when(flag > 0)
    def _():
        queries = queries_of(plan, space, facts, head, q[0], extra_q[0], {})
        space_attend(plan, space, {1: packets}, extra_k[0], queries, out.at[0], lse.at[0])

    @pl.when(flag == 0)
    def _():
        out[...] = jnp.zeros_like(out)
        lse[...] = jnp.full_like(lse, NEG)


def far_kernel(plan, group, facts, q, out_own, lse_own, out_near, lse_near, *refs):
    refs = list(refs)
    packets = {}
    for level in plan.levels[1:]:
        packets[level] = [refs.pop(0) for _ in plan.masks(level)]
    spaces = plan.spaces[1:]
    extras = {s.stride: (refs.pop(0), refs.pop(0)) for s in spaces}
    combined, lse_all = refs.pop(0), refs.pop(0)
    held = {s.stride: (refs.pop(0), refs.pop(0)) for s in spaces}
    head = pl.program_id(0)
    near = plan.spaces[0]
    for space in spaces:
        out, lse = held[space.stride]
        flag = reach_flag(plan, facts, group, space)

        @pl.when(flag > 0)
        def _(space=space, out=out, lse=lse):
            extra_k, extra_q = extras[space.stride]
            picked = lanes_down(near, first_in(facts, head, 2), q[0]).astype(BF)
            queries = queries_of(plan, space, facts, head, None, extra_q[0], {2: picked})
            space_attend(plan, space, packets, extra_k[0], queries, out, lse)

        @pl.when(flag == 0)
        def _(out=out, lse=lse):
            out[...] = jnp.zeros_like(out)
            lse[...] = jnp.full_like(lse, NEG)

    firsts = {s.stride: first_in(facts, head, s.stride) for s in plan.spaces}
    stats = [lse_near[0, 0:1]]
    for space in spaces:
        first = firsts[space.stride]
        up = stat_up(space, first, held[space.stride][1][0:1])
        stats.append(jnp.where(chosen_lanes(space, first), up, NEG))
    lse_two = log_add(*stats)
    up = stat_up(near, firsts[2], lse_two)
    total = log_add(lse_own[0, 0:1], jnp.where(chosen_lanes(near, firsts[2]), up, NEG))
    lse_all[0] = jnp.broadcast_to(total, lse_all.shape[1:])
    total_two = stat_down(near, firsts[2], total)
    two = out_near[0] * jnp.exp(lse_near[0, 0:1] - total_two)
    for space in spaces:
        first = firsts[space.stride]
        out, lse = held[space.stride]
        total_here = stat_down(space, first, total_two)
        two = two + wide_up(space, first, out[...] * jnp.exp(lse[0:1] - total_here))
    combined[0] = out_own[0] * jnp.exp(lse_own[0, 0:1] - total) + wide_up(near, firsts[2], two)


def prepare_kernel(plan, group, facts, q, g, combined, lse, *refs):
    refs = list(refs)
    strides = [1] + [s.stride for s in plan.spaces]
    extras = {s: refs.pop(0) for s in strides}
    outs = {s: (refs.pop(0), refs.pop(0), refs.pop(0)) for s in strides}
    head = pl.program_id(0)
    total = -lse[0, 0:1]
    dots = -jnp.sum(g[0].astype(F32) * combined[0], axis=0, keepdims=True)
    stats = jnp.concatenate([stat_rows(total, 16), stat_rows(dots, 16)], axis=0)
    stack = jnp.concatenate([q[0], g[0], stats], axis=0)
    held = {1: stack}
    for stride in strides:
        if stride > 1:
            space = plan.space(stride)
            source = held[1] if stride == 2 else held[2]
            held[stride] = lanes_down(space, first_in(facts, head, stride), source).astype(BF)
        mine = held[stride]
        queries, grads, rows = outs[stride]
        stat = mine[2 * HALF :].astype(F32)
        extra = extras[stride][0].astype(F32)
        row = lax.broadcasted_iota(jnp.int32, extra.shape, 0)
        low = jnp.zeros_like(extra)
        for j in range(3):
            extra = jnp.where(row == LSE_ROW + j, stat[j : j + 1], extra)
            low = jnp.where(row == j, stat[16 + j : 17 + j], low)
        queries[0] = jnp.concatenate([mine[:HALF], extra.astype(BF)], axis=0)
        grads[0] = jnp.concatenate([low.astype(BF), mine[HALF : 2 * HALF]], axis=0)
        rows[0] = mine[: 2 * HALF].T


def space_back(plan, space, refs, extra_k, queries, grads, rows, out_q, out_refs):
    sources = space_sources(plan, space, refs)
    targets = space_sources(plan, space, out_refs)
    packet = jnp.concatenate([ref[0, at : at + space.keys] for level, ref, at in sources], axis=0)
    keys_extra = with_extra(packet, extra_k)
    values_ones = with_ones(packet)
    keys_turned = packet.T[:HALF]
    block = min(512, space.queries)
    pair = None
    for start in range(0, space.queries, block):
        stop = start + block
        got, turned = attend_back(
            keys_extra,
            values_ones,
            keys_turned,
            queries[:, start:stop],
            grads[:, start:stop],
            rows[start:stop],
        )
        pair = got if pair is None else pair + got
        out_q[:, start:stop] = turned
    for j, (level, ref, at) in enumerate(targets):
        ref[0, at : at + space.keys] = pair[j * space.keys : (j + 1) * space.keys].astype(BF)


def spaces_back_kernel(plan, group, spaces, levels, facts, *refs):
    refs = list(refs)
    packets = {lv: [refs.pop(0) for _ in plan.masks(lv)] for lv in levels}
    ins = {s.stride: [refs.pop(0) for _ in range(4)] for s in spaces}
    outs = {lv: [refs.pop(0) for _ in plan.masks(lv)] for lv in levels}
    out_q = {s.stride: refs.pop(0) for s in spaces}
    for space in spaces:
        flag = reach_flag(plan, facts, group, space)

        @pl.when(flag > 0)
        def _(space=space):
            extra_k, queries, grads, rows = [r[0] for r in ins[space.stride]]
            space_back(
                plan,
                space,
                packets,
                extra_k,
                queries,
                grads,
                rows,
                out_q[space.stride].at[0],
                outs,
            )

        @pl.when(flag == 0)
        def _(space=space):
            out_q[space.stride][...] = jnp.zeros_like(out_q[space.stride])
            for level, ref, at in space_sources(plan, space, outs):
                ref[0, at : at + space.keys] = jnp.zeros((space.keys, 128), BF)


def own_back_kernel(plan, block, kv, extra_k, queries, grads, rows, pair, out_q):
    keys_extra = with_extra(kv[0], extra_k[0])
    values_ones = with_ones(kv[0])
    keys_turned = kv[0].T[:HALF]
    for start in reversed(range(0, plan.window, block)):
        stop = start + block
        got, turned = attend_back(
            keys_extra[:stop],
            values_ones[:stop],
            keys_turned[:, :stop],
            queries[0, :, start:stop],
            grads[0, :, start:stop],
            rows[0, start:stop],
            block,
        )
        if stop == plan.window:
            pair[0] = got
        else:
            pair[0, :stop] += got
        out_q[0, :, start:stop] = turned


def gather_kernel(plan, group, facts, pair, own_q, *refs):
    refs = list(refs)
    queries = {s.stride: refs.pop(0) for s in plan.spaces}
    returns = {lv: refs.pop(0) for lv in plan.levels}
    out_pair, out_q = refs
    head = pl.program_id(0)
    near = plan.spaces[0]
    rows_two = jnp.zeros((near.keys, 128), F32)
    lanes_two = queries[2][0]
    for space in plan.spaces:
        first = first_in(facts, head, space.stride)
        total = None
        for level in space.levels:
            at = plan.packet[level][0][space.stride]
            got = returns[level][0, at : at + space.keys]
            if space.stride == 2:
                rows_two = rows_two + got.astype(F32)
            else:
                rows_two = rows_two + rows_up(space, first, got)
        if space.stride != 2:
            lanes_two = lanes_two + wide_up(space, first, queries[space.stride][0])
    first = first_in(facts, head, 2)
    high, low = split_two(rows_two)
    got = rows_up(near, first, jnp.concatenate([high, low], axis=1))
    out_pair[...] = (pair[0] + got[:, :128] + got[:, 128:]).astype(BF)
    out_q[0] = (own_q[0] + wide_up(near, first, lanes_two)).astype(BF)


def per_head(rows, cols):
    return pl.BlockSpec((1, rows, cols), lambda h: (h, 0, 0))


def head_call(kernel, group, facts, ins, outs, scratch=(), cost=0, specs=None):
    in_specs = [per_head(*a.shape[1:]) for a in ins]
    out_specs = [per_head(r, c) for r, c, d in outs]
    shapes = [jax.ShapeDtypeStruct((group, r, c), d) for r, c, d in outs]
    for j, (spec, shape) in (specs or {}).items():
        out_specs[j], shapes[j] = spec, shape
    moved = sum(a.size * a.dtype.itemsize for a in ins)
    front = [] if facts is None else [facts]
    return pl.pallas_call(
        kernel,
        grid=(group,),
        in_specs=[pl.BlockSpec(memory_space=pltpu.SMEM)] * len(front) + in_specs,
        out_specs=out_specs,
        out_shape=shapes,
        scratch_shapes=list(scratch),
        compiler_params=pltpu.CompilerParams(vmem_limit_bytes=VMEM_LIMIT),
        cost_estimate=pl.CostEstimate(flops=cost, bytes_accessed=moved, transcendentals=0),
    )(*front, *ins)


def swap(array, axis, bit, only=lambda i: True):
    count = lax.axis_size(axis)
    return lax.ppermute(array, axis, [(i, i ^ bit) for i in range(count) if only(i)])


def level_send(plan, level, packet):
    step = 1 << level
    pairs = [(i, i + step) for i in range(plan.seq_count) if not i & step]
    found = [lax.ppermute(packet, "seq", pairs)]
    for bit in reversed(range(level - 1)):
        found = found + [swap(f, "seq", 2 << bit, lambda i: i & step) for f in found]
    return found


def level_return(plan, level, grads):
    step = 1 << level
    for bit in range(level - 1):
        half = len(grads) // 2
        got = [swap(g, "seq", 2 << bit, lambda i: i & step) for g in grads[half:]]
        grads = [(a.astype(F32) + b.astype(F32)).astype(BF) for a, b in zip(grads[:half], got)]
    pairs = [(i + step, i) for i in range(plan.seq_count) if not i & step]
    return lax.ppermute(grads[0], "seq", pairs)


def in_order(bit, mine, other, axis):
    zero = bit == 0
    first = jnp.where(zero, mine, other)
    second = jnp.where(zero, other, mine)
    return jnp.concatenate([first, second], axis=axis)


def pick_half(array, index, axis):
    half = array.shape[axis] // 2
    return lax.dynamic_slice_in_dim(array, index * half, half, axis)


def per_device(
    tokens,
    mix_gain,
    mix_shift,
    query_weight,
    query_bias,
    key_weight,
    value_weight,
    value_bias,
    attn_gain,
    attn_shift,
    out_weight,
    out_bias,
    feed_gain,
    feed_shift,
    up_weight,
    up_bias,
    inner_gain,
    inner_shift,
    down_weight,
    down_bias,
    cotangent,
):
    tok_rows, width = tokens.shape
    seq_count = lax.axis_size("seq")
    devices = seq_count * lax.axis_size("head")
    plan = Plan(tok_rows, seq_count)
    seq_index = lax.axis_index("seq")
    core = lax.axis_index("head")
    cross = seq_index % 2
    window_index = seq_index // 2
    heads_here = query_weight.shape[1] // HEAD_DIM
    group = heads_here // 2
    cols = group * HEAD_DIM
    half_rows = tok_rows // 2
    heads = core * heads_here + cross * group + jnp.arange(group, dtype=jnp.int32)
    ff = up_weight.shape[1]

    up_rows = up_weight.shape[0]
    fold = ff // width
    down_rows = down_weight.shape[0]
    small = jnp.concatenate([up_bias, inner_gain, inner_shift, feed_gain, feed_shift, down_bias])
    small_at = [down_rows, down_rows, down_rows, up_rows, up_rows, up_rows]
    pad = -small.shape[0] % width
    small_rows = jnp.pad(small, (0, pad)).reshape(-1, width)
    up_packed = jnp.concatenate(
        [up_weight[:, j * width : (j + 1) * width] for j in range(fold)], axis=0
    )
    packed = jnp.concatenate([up_packed, down_weight, small_rows], axis=0)
    packed = jnp.pad(packed, ((0, -packed.shape[0] % 16), (0, 0)))
    gathered = lax.all_gather(packed, BOTH, axis=0, tiled=False)

    got = swap(pick_half(tokens, core, 0), "seq", 1)
    other = swap(got, "head", 1)
    partner = in_order(core, got, other, 0)
    window_tokens = in_order(cross, tokens, partner, 0)
    out_extra = jnp.concatenate([attn_gain, attn_shift]).reshape(1, width)
    out_packed = jnp.concatenate([out_weight, jnp.pad(out_extra, ((0, 15), (0, 0)))], axis=0)
    out_other = swap(out_packed, "head", 1)
    out_full = in_order(core, out_packed[: width // 2], out_other[: width // 2], 0)
    gain_mine, gain_other = out_packed[width // 2], out_other[width // 2]
    attn_gain_full = in_order(core, gain_mine[: width // 2], gain_other[: width // 2], 0)
    attn_shift_full = in_order(core, gain_mine[width // 2 :], gain_other[width // 2 :], 0)

    firsts = [first_of(plan, s, window_index, heads) for s in (2, 4, 6, 12)]
    firsts = [firsts[0]] + [jnp.mod(f - firsts[0], s) // 2 for f, s in zip(firsts[1:], (4, 6, 12))]
    flags = jnp.stack([(window_index >> b) & 1 for b in range(4)])
    facts = jnp.concatenate([jnp.stack(firsts, axis=1).reshape(-1), flags]).astype(jnp.int32)

    wq = pick_half(query_weight, cross, 1).T
    wk = pick_half(key_weight, cross, 1).reshape(width, group, HEAD_DIM)
    wv = pick_half(value_weight, cross, 1).reshape(width, group, HEAD_DIM)
    wkv = jnp.concatenate([wk, wv], axis=2).reshape(width, 2 * cols)
    bq = pick_half(query_bias, cross, 0).astype(F32).reshape(cols, 1)
    bv = pick_half(value_bias, cross, 0).astype(F32).reshape(group, HEAD_DIM)
    bkv = jnp.concatenate([jnp.zeros_like(bv), bv], axis=1).reshape(1, 2 * cols)
    mix_gain_wide = mix_gain.astype(F32).reshape(1, width)
    mix_shift_wide = mix_shift.astype(F32).reshape(1, width)

    whole = pl.BlockSpec(memory_space=pltpu.VMEM)
    packet_shapes = [
        jax.ShapeDtypeStruct((group, plan.packet[level][1], 128), BF) for level in plan.levels
    ]
    normed, queries_turned, pair_rows, *packets = pl.pallas_call(
        functools.partial(project_kernel, plan, group),
        in_specs=[pl.BlockSpec(memory_space=pltpu.SMEM)] + [whole] * 7,
        out_specs=[whole] * (3 + len(packet_shapes)),
        out_shape=[
            jax.ShapeDtypeStruct((plan.window, width), BF),
            jax.ShapeDtypeStruct((group, HEAD_DIM, plan.window), BF),
            jax.ShapeDtypeStruct((group, plan.window, 128), BF),
        ]
        + packet_shapes,
        compiler_params=pltpu.CompilerParams(vmem_limit_bytes=VMEM_LIMIT),
    )(facts, window_tokens, mix_gain_wide, mix_shift_wide, wq, bq, wkv, bkv)

    received = {lv: level_send(plan, lv, pk) for lv, pk in zip(plan.levels, packets)}

    on = jnp.asarray(True)
    extra_k = {1: extra_keys(plan, 1, plan.window, window_index, heads, on)}
    extra_q = {1: extra_queries(plan, 1, plan.window, window_index, heads)}
    for space in plan.spaces:
        parts = []
        for level in space.levels:
            for mask in plan.masks(level):
                source = (window_index ^ mask) ^ (1 << (level - 1))
                on = flags[level - 1] == 1
                parts.append(extra_keys(plan, space.stride, space.keys, source, heads, on))
        extra_k[space.stride] = jnp.concatenate(parts, axis=1)
        extra_q[space.stride] = extra_queries(
            plan, space.stride, space.queries, window_index, heads
        )

    window = plan.window
    near, far = plan.spaces[0], plan.spaces[1:]
    block = 512
    out_own, lse_own = head_call(
        functools.partial(own_kernel, plan, block),
        group,
        None,
        [pair_rows, extra_k[1], queries_turned, extra_q[1]],
        [(HEAD_DIM, window, F32), (8, window, F32)],
        cost=4 * group * window * window * 128,
    )
    out_near, lse_near = head_call(
        functools.partial(near_kernel, plan, group),
        group,
        facts,
        [queries_turned, *received[1], extra_k[2], extra_q[2]],
        [(HEAD_DIM, near.queries, F32), (8, near.queries, F32)],
        cost=2 * group * window * window * 128,
    )
    far_packets = [r for lv in plan.levels[1:] for r in received[lv]]
    far_extras = [e for s in far for e in (extra_k[s.stride], extra_q[s.stride])]
    scratch = []
    for s in far:
        scratch += [pltpu.VMEM((HEAD_DIM, s.queries), F32), pltpu.VMEM((8, s.queries), F32)]
    combined, lse_all = head_call(
        functools.partial(far_kernel, plan, group),
        group,
        facts,
        [queries_turned, out_own, lse_own, out_near, lse_near, *far_packets, *far_extras],
        [(HEAD_DIM, window, F32), (8, window, F32)],
        scratch,
        cost=2 * group * window * window * 128,
    )

    mixed_low = combined.reshape(cols, window).astype(BF)
    got = swap(pick_half(mixed_low, 1 - cross, 1), "seq", 1)
    joined = in_order(cross, pick_half(mixed_low, cross, 1), got, 0)
    got = swap(pick_half(joined, 1 - core, 1), "head", 1)
    joined = in_order(core, pick_half(joined, core, 1), got, 0)

    mixed_wide = joined.astype(F32).T
    attn_gain_wide = attn_gain_full.astype(F32)
    normal_wide, attn_pull = jax.vjp(
        layer_norm, mixed_wide, attn_gain_wide, attn_shift_full.astype(F32)
    )
    mixed = normal_wide.astype(BF)
    tokens_half = pick_half(tokens, core, 0).astype(F32)
    hidden = tokens_half + mm(mixed, out_full) + out_bias.astype(F32)

    up_full = jnp.concatenate(
        [
            gathered[:, j * up_rows : (j + 1) * up_rows].reshape(width, width)
            for j in range(fold)
        ],
        axis=1,
    )
    down_at = fold * up_rows
    down_full = gathered[:, down_at : down_at + down_rows].reshape(ff, width)
    small_full = gathered[:, down_at + down_rows : down_at + down_rows + small_rows.shape[0]]
    small_full = small_full.reshape(devices, -1).astype(F32)
    pieces, at = [], 0
    for size in small_at:
        pieces.append(small_full[:, at : at + size].reshape(-1))
        at += size
    up_bias_w, inner_gain_w, inner_shift_w, feed_gain_w, feed_shift_w, down_bias_w = pieces

    feed_wide, feed_pull = jax.vjp(layer_norm, hidden, feed_gain_w, feed_shift_w)
    feed_in = feed_wide.astype(BF)
    before = mm(feed_in, up_full) + up_bias_w
    inner_wide, inner_pull = jax.vjp(gelu_norm, before, inner_gain_w, inner_shift_w)
    inner = inner_wide.astype(BF)
    output = (hidden + mm(inner, down_full) + down_bias_w).astype(BF)

    cot_wide = cotangent.astype(F32)
    down_weight_grad = dot_rows(inner, cotangent)
    down_bias_grad = jnp.sum(cot_wide, axis=0)
    inner_grad = dot_cols(cotangent, down_full)
    before_grad, inner_gain_grad, inner_shift_grad = inner_pull(inner_grad)
    before_low = before_grad.astype(BF)
    up_weight_grad = dot_rows(feed_in, before_low)
    up_bias_grad = jnp.sum(before_low.astype(F32), axis=0)
    feed_grad = dot_cols(before_low, up_full)
    hidden_norm_grad, feed_gain_grad, feed_shift_grad = feed_pull(feed_grad)
    hidden_grad = cot_wide + hidden_norm_grad
    branch_low = hidden_grad.astype(BF)
    out_bias_grad = jnp.sum(branch_low.astype(F32), axis=0)
    out_grad_turned = dot_rows(branch_low, mixed)
    mixed_grad, attn_gain_grad, attn_shift_grad = attn_pull(dot_cols(branch_low, out_full))

    out_rows = width // seq_count
    out_blocks = out_grad_turned.reshape(seq_count, 2, out_rows // 2, 2, width // 2)
    out_blocks = out_blocks.transpose(0, 3, 2, 1, 4).reshape(devices, out_rows // 2, width)
    by_device = [up_bias_grad, inner_gain_grad, inner_shift_grad, down_bias_grad]
    by_device += [feed_gain_grad, feed_shift_grad, out_bias_grad]
    by_core = [attn_gain_grad, attn_shift_grad]
    small_grads = [g.reshape(devices, -1) for g in by_device]
    small_grads += [
        g.reshape(2, seq_count, -1).transpose(1, 0, 2).reshape(devices, -1) for g in by_core
    ]
    small_sizes = [g.shape[1] for g in small_grads]
    small_grads = jnp.concatenate(small_grads, axis=1)
    small_grads = jnp.pad(small_grads, ((0, 0), (0, -small_grads.shape[1] % width)))
    small_grads = small_grads.reshape(devices, -1, width)
    up_blocks = [
        up_weight_grad[:, j * width : (j + 1) * width].reshape(devices, up_rows, width)
        for j in range(fold)
    ]
    down_blocks = down_weight_grad.reshape(devices, down_rows, width)
    stack = [b.astype(BF) for b in (*up_blocks, down_blocks, out_blocks, small_grads)]
    stack = jnp.concatenate(stack, axis=1)
    stack = jnp.pad(stack, ((0, 0), (0, -stack.shape[1] % 16), (0, 0)))
    summed = lax.psum_scatter(
        stack.reshape(-1, width), BOTH, scatter_dimension=0, tiled=True
    ).astype(F32)

    grad_turned = mixed_grad.astype(BF).T
    got = swap(pick_half(grad_turned, 1 - core, 0), "head", 1)
    joined = in_order(core, pick_half(grad_turned, core, 0), got, 1)
    got = swap(pick_half(joined, 1 - cross, 0), "seq", 1)
    joined = in_order(cross, pick_half(joined, cross, 0), got, 1)
    grads_turned = joined.reshape(group, HEAD_DIM, window)

    strides = [1] + [s.stride for s in plan.spaces]
    counts = [window] + [s.queries for s in plan.spaces]
    prepared = head_call(
        functools.partial(prepare_kernel, plan, group),
        group,
        facts,
        [queries_turned, grads_turned, combined, lse_all, *[extra_q[s] for s in strides]],
        [o for n in counts for o in ((128, n, BF), (128, n, BF), (n, 128, BF))],
    )
    prepared = {s: prepared[3 * j : 3 * j + 3] for j, s in enumerate(strides)}

    def back(spaces, levels, cost):
        ins = [r for lv in levels for r in received[lv]]
        shapes = [(r.shape[1], 128, BF) for r in ins]
        for s in spaces:
            ins += [extra_k[s.stride], *prepared[s.stride]]
        shapes += [(HEAD_DIM, s.queries, F32) for s in spaces]
        outs = head_call(
            functools.partial(spaces_back_kernel, plan, group, spaces, levels),
            group,
            facts,
            ins,
            shapes,
            cost=cost,
        )
        pairs, at = {}, 0
        for lv in levels:
            pairs[lv] = list(outs[at : at + len(received[lv])])
            at += len(received[lv])
        return pairs, list(outs[at:])

    far_pairs, far_queries = back(far, plan.levels[1:], 5 * group * window * window * 128)
    returned = {lv: level_return(plan, lv, far_pairs[lv]) for lv in plan.levels[1:]}
    near_pairs, near_queries = back([near], [1], 5 * group * window * window * 128)
    returned[1] = level_return(plan, 1, near_pairs[1])
    own_pair, own_q = head_call(
        functools.partial(own_back_kernel, plan, 256),
        group,
        None,
        [pair_rows, extra_k[1], *prepared[1]],
        [(window, 128, F32), (HEAD_DIM, window, F32)],
        cost=10 * group * window * window * 128,
    )
    pair_spec = pl.BlockSpec((window, 128), lambda h: (0, h))
    pair_shape = jax.ShapeDtypeStruct((window, group * 128), BF)
    pair_low, query_low = head_call(
        functools.partial(gather_kernel, plan, group),
        group,
        facts,
        [own_pair, own_q, *near_queries, *far_queries, *[returned[lv] for lv in plan.levels]],
        [(window, 128, BF), (HEAD_DIM, window, BF)],
        specs={0: (pair_spec, pair_shape)},
    )
    query_low = query_low.reshape(cols, window)

    part = dot_rows(query_low, wq) + dot_cols(pair_low, wkv)
    tokens_wide = window_tokens.astype(F32)
    center = jnp.mean(tokens_wide, axis=1, keepdims=True)
    centered = tokens_wide - center
    spread = jnp.mean(centered * centered, axis=1, keepdims=True)
    plain = centered * lax.rsqrt(spread + EPS)
    mix_part = jnp.concatenate([jnp.sum(part * plain, axis=0), jnp.sum(part, axis=0)])
    part_low = part.astype(BF).reshape(2, 2, half_rows, width)
    mine = lax.dynamic_index_in_dim(part_low, core, 1, keepdims=False)
    away = lax.dynamic_index_in_dim(part_low, 1 - core, 1, keepdims=False)
    got = swap(away, "head", 1)
    both = (mine.astype(F32) + got.astype(F32)).astype(BF)
    mine = lax.dynamic_index_in_dim(both, cross, 0, keepdims=False)
    away = lax.dynamic_index_in_dim(both, 1 - cross, 0, keepdims=False)
    normed_grad = mine.astype(F32) + swap(away, "seq", 1).astype(F32)
    tokens_norm_grad = jax.vjp(layer_norm, tokens_half, mix_gain.astype(F32), mix_shift.astype(F32))[
        1
    ](normed_grad)[0]
    tokens_grad = hidden_grad + tokens_norm_grad

    weight_part = jnp.concatenate(
        [dot_rows(normed, pair_low), dot_cols(normed.T, query_low)], axis=1
    ).astype(BF)
    pair_sums = jnp.sum(pair_low.astype(F32), axis=0)
    query_sums = jnp.sum(query_low.astype(F32), axis=1)
    sums = jnp.concatenate([pair_sums, query_sums, mix_part])
    sums_pad = -sums.shape[0] % 1024
    sums = jnp.pad(sums, (0, sums_pad)).reshape(-1, 128)
    block_rows = width // seq_count
    weight_part = weight_part.reshape(seq_count // 2, 2 * block_rows, 3 * cols)
    bits = (seq_count // 2).bit_length() - 1
    for bit in reversed(range(bits)):
        here = (window_index >> bit) & 1
        mine = pick_half(weight_part, here, 0)
        got = swap(pick_half(weight_part, 1 - here, 0), "seq", 2 << bit)
        weight_part = (mine.astype(F32) + got.astype(F32)).astype(BF)
        sums = sums + swap(sums, "seq", 2 << bit)
    weight_part = weight_part[0]
    got = swap(pick_half(weight_part, 1 - cross, 0), "seq", 1)
    mine = pick_half(weight_part, cross, 0)
    sums_other = swap(sums, "seq", 1)
    flat, flat_other = sums.reshape(-1), sums_other.reshape(-1)
    mix_sum = flat[3 * cols : 3 * cols + 2 * width] + flat_other[3 * cols : 3 * cols + 2 * width]
    mix_sum = mix_sum.reshape(-1, 128)
    mix_sum = (mix_sum + swap(mix_sum, "head", 1)).reshape(2, devices, -1)
    mix_sum = lax.dynamic_index_in_dim(mix_sum, seq_index * 2 + core, 1, keepdims=False)

    def parts_of(array):
        pair = array[..., : 2 * cols].reshape(array.shape[:-1] + (group, 2, HEAD_DIM))
        key, value = pair[..., 0, :], pair[..., 1, :]
        lead = array.shape[:-1] + (cols,)
        return array[..., 2 * cols : 3 * cols], key.reshape(lead), value.reshape(lead)

    weight_grads = [
        in_order(cross, a, b, 1).astype(F32) for a, b in zip(parts_of(mine), parts_of(got))
    ]
    bias_grads = [
        lax.dynamic_index_in_dim(
            in_order(cross, a, b, 0).reshape(seq_count, -1), seq_index, 0, keepdims=False
        )
        for a, b in zip(parts_of(flat[: 3 * cols]), parts_of(flat_other[: 3 * cols]))
    ]

    up_sum = jnp.concatenate(
        [summed[j * up_rows : (j + 1) * up_rows] for j in range(fold)], axis=1
    )
    at = fold * up_rows
    down_sum = summed[at : at + down_rows]
    at += down_rows
    out_sum = summed[at : at + out_rows // 2].reshape(out_rows // 2, 2, width // 2)
    out_sum = out_sum.transpose(1, 0, 2).reshape(out_rows, width // 2).T
    at += out_rows // 2
    flat_small = summed[at : at + small_grads.shape[1]].reshape(-1)
    smalls, place = [], 0
    for size in small_sizes:
        smalls.append(flat_small[place : place + size])
        place += size
    (
        up_bias_sum,
        inner_gain_sum,
        inner_shift_sum,
        down_bias_sum,
        feed_gain_sum,
        feed_shift_sum,
        out_bias_sum,
        attn_gain_sum,
        attn_shift_sum,
    ) = smalls
    return (
        output,
        tokens_grad,
        mix_sum[0],
        mix_sum[1],
        weight_grads[0],
        bias_grads[0],
        weight_grads[1],
        weight_grads[2],
        bias_grads[2],
        attn_gain_sum,
        attn_shift_sum,
        out_sum,
        out_bias_sum,
        feed_gain_sum,
        feed_shift_sum,
        up_sum,
        up_bias_sum,
        inner_gain_sum,
        inner_shift_sum,
        down_sum,
        down_bias_sum,
    )


def solution(mesh):
    return jax.shard_map(
        per_device,
        mesh=mesh,
        in_specs=(
            P("seq", None),
            P(),
            P(),
            P(None, "head"),
            P("head"),
            P(None, "head"),
            P(None, "head"),
            P("head"),
            P("head"),
            P("head"),
            P("head", None),
            P(),
            P(("seq", "head")),
            P(("seq", "head")),
            P(("seq", "head"), None),
            P(("seq", "head")),
            P(("seq", "head")),
            P(("seq", "head")),
            P(("seq", "head"), None),
            P(("seq", "head")),
            P(("seq", "head"), None),
        ),
        out_specs=(
            P(("seq", "head"), None),
            P(("seq", "head"), None),
            P(("seq", "head")),
            P(("seq", "head")),
            P("seq", "head"),
            P(("head", "seq")),
            P("seq", "head"),
            P("seq", "head"),
            P(("head", "seq")),
            P(("head", "seq")),
            P(("head", "seq")),
            P("head", "seq"),
            P(("seq", "head")),
            P(("seq", "head")),
            P(("seq", "head")),
            P(("seq", "head"), None),
            P(("seq", "head")),
            P(("seq", "head")),
            P(("seq", "head")),
            P(("seq", "head"), None),
            P(("seq", "head")),
        ),
        check_vma=False,
    )
```

time: 2400 us -> 545 us (0.23)
  matrix products: 694 us -> 66.6 us
  waiting for transfers between devices: 770 us -> 151 us
  local copies, waits for them, and re-layouts: 402 us -> 98.4 us
  other arithmetic: 286 us -> 81.8 us
  blocking collectives: 151 us -> 0 us
  Pallas kernels: 0 us -> 78.2 us
    reduce_scatter x8 -> x1, waiting for transfers between devices: 669 us -> 0.01 us  [per_device(): lax.psum_scatter(stack.reshape(-1, width), BOTH, scatter_dimension=0, til...]
    dot_general x36 -> x3, matrix products: 639 us -> 30.7 us  [mm(): return jnp.dot(left_side, right_side, preferred_element_type=F32)]
    unnamed x3 -> x0, blocking collectives: 146 us -> none
    reduce_sum x31 -> x8, other arithmetic: 139 us -> 23.9 us  [the longest x1 9.06 us: per_device(): up_bias_grad = jnp.sum(before_low.astype(F32), axis=0)]
    ppermute x28 -> x32, waiting for transfers between devices: 39.1 us -> 151 us  [the longest x26 67.9 us: swap(): lax.ppermute(array, axis, [(i, i ^ bit) for i in range(count) if only(i)])]
    mul x59 -> x2, local copies, waits for them, and re-layouts: 108 us -> 0.15 us  [layer_norm(): return centered * lax.rsqrt(spread + EPS) * gain + shift]
    pallas_call x0 -> x9, Pallas kernels: none -> 78.2 us  [the longest x8 69.8 us: head_call(): pl.pallas_call(kernel, grid=(group,), in_specs=[pl.BlockSpec(memory_space...]
    all_gather x3 -> x1, waiting for transfers between devices: 60.7 us -> 0.02 us  [per_device(): gathered = lax.all_gather(packed, BOTH, axis=0, tiled=False)]
  transfers between devices with their start and end apart: 39 -> 34, of which waited for: 12 -> 13; matrix products, arithmetic and copies ran while one was open for 35% -> 28% of each run, Pallas kernels for 0% -> 15%
where the time goes in v1:
time: 545 us; the launch traced here: 538 us
  waiting for transfers between devices  151 us (28%)
  local copies, waits for them, and re-layouts  98.4 us (18%)
  other arithmetic  81.8 us (15%)
  Pallas kernels  78.2 us (14%)
  matrix products  66.6 us (12%)
  starting transfers between devices  46.9 us (9%)
  between operations  15.8 us (3%)
    pallas_call x8, Pallas kernels, head_call(): pl.pallas_call(kernel, grid=(group,), in_specs=[pl.BlockSpec(memory_space...  69.8 us
    ppermute x26, waiting for transfers between devices, swap(): lax.ppermute(array, axis, [(i, i ^ bit) for i in range(count) if only(i)])  67.9 us
    ppermute x3, waiting for transfers between devices, level_return(): return lax.ppermute(grads[0], 'seq', pairs)  57.7 us
    dot_general x3, matrix products, mm(): return jnp.dot(left_side, right_side, preferred_element_type=F32)  30.7 us
    ppermute x26, starting transfers between devices, swap(): lax.ppermute(array, axis, [(i, i ^ bit) for i in range(count) if only(i)])  29.7 us
    unnamed x168, local copies, waits for them, and re-layouts  29.6 us
    ppermute x3, waiting for transfers between devices, level_send(): found = [lax.ppermute(packet, 'seq', pairs)]  25 us
    dot_general x5, matrix products, dot_rows(): lax.dot_general(left_side, right_side, (((0,), (0,)), ((), ())), preferre...  18.7 us
  transfers between devices with their start and end apart: 34, of which 13 were waited for; matrix products, arithmetic and copies ran while one was open for 28% of the time, Pallas kernels for 15%

profile of v1, /device:TPU:0, one launch (start us, length us, event | category | flops | bytes accessed | tf_op | source)
XLA Modules:
  0.0 538.4 jit_solution(834694835384905689)
XLA Ops:
  11.4 4.1 concatenate.116
  19.2 2.5 collective-permute-start
  30.9 2.2 select_convert_fusion.3
  33.2 3.5 select_convert_fusion.extra_k
  36.7 5.6 %collective-permute-done = bf16[512,768]{1,0:T(8,128)(2,1)} collective-permute-done((bf16[512,768]{1,0:T(8,128)(2,1)S(1)}, bf16[512,768]{1,0:T(8,128)(2,1)}, u32[]{:S(2)}, u32[]{:S(2)}) %collective-permute-start) | collective-permute-done | bytes 786464 | tf_op jit(solution)/shard_map/ppermute | solution.py:608
  47.5 2.2 select_convert_fusion.1.refs_1_
  49.7 2.3 fusion.33.extra_q.refs_0_
  54.2 2.1 pad_maximum_fusion.1.tok
  56.4 8.5 %shard_map.364 = (bf16[2048,768]{1,0:T(8,128)(2,1)}, bf16[3,64,2048]{2,1,0:T(8,128)(2,1)}, bf16[3,2048,128]{2,1,0:T(8,128)(2,1)}, bf16[3,1024,128]{2,1,0:T(8,128...) custom-call(s32[16]{0:T(128)} %concatenate.102.facts, bf16[2048,768]{1,0:T(8,128)(2,1)} %pad_maximum_fusion.1.tok, ...), custom_call_target="tpu_custom_call" | custom-call | tf_op jit(solution)/shard_map/pallas_call | solution.py:725
  64.9 4.6 collective-permute-start.3
  70.4 5.2 collective-permute-start.5
  76.8 3.5 collective-permute-start.2
  80.2 1.9 pad_maximum_fusion.7.refs_6_
  82.9 25.0 %collective-permute-done.5.refs_2_ = bf16[3,352,128]{2,1,0:T(8,128)(2,1)} collective-permute-done((bf16[3,352,128]{2,1,0:T(8,128)(2,1)}, bf16[3,352,128]{2,1,0:T(8,128)(2,1)}, u32[]{:S(2)}, u32[]{:S(2)}) %collective-permute-start.5) | collective-permute-done | bytes 270368 | tf_op jit(solution)/shard_map/ppermute | solution.py:614
  109.3 13.6 %shard_map.365 = (f32[3,64,2048]{2,1,0:T(8,128)}, f32[3,8,2048]{2,1,0:T(8,128)}) custom-call(bf16[3,2048,128]{2,1,0:T(8,128)(2,1)} %get-tuple-element.60.kv, bf16[3,2048,128]{2,1,0:T(8,128)(2,1)} %select_convert_fusion.extra_k, bf16[3,64,2048]{2,1,0:T(8,128)(2,1)} %get-tuple-element.59.q, bf16[3,64,2048]{2,1,0:T(8,128)(2,1)} %fusion.33.extra_q.refs_0_), custom_call_target="tpu_custom_call" | custom-call | flops 6442450944 | bytes 4718592 | tf_op jit(solution)/shard_map/pallas_call | solution.py:594
  125.2 3.5 shard_map.366
  129.8 7.6 %shard_map.367 = (f32[3,64,2048]{2,1,0:T(8,128)}, f32[3,8,2048]{2,1,0:T(8,128)}) custom-call(s32[16]{0:T(128)} %concatenate.102.facts, bf16[3,64,2048]{2,1,0:T(8,128)(2,1)} %get-tuple-element.59.q, f32[3,64,2048]{2,1,0:T(8,128)} %get-tuple-element.61.out_own, f32[3,8,2048]{2,1,0:T(8,128)} %get-tuple-element.62.lse_own, ...), custom_call_target="tpu_custom_call" | custom-call | flops 3221225472 | bytes 8601600 | tf_op jit(solution)/shard_map/pallas_call | solution.py:594
  143.3 10.5 %collective-permute-done.9 = bf16[192,1024]{0,1:T(8,128)(2,1)} collective-permute-done((bf16[192,1024]{0,1:T(8,128)(2,1)}, bf16[192,1024]{0,1:T(8,128)(2,1)}, u32[]{:S(2)}, u32[]{:S(2)}) %collective-permute-start.9) | collective-permute-done | bytes 393248 | tf_op jit(solution)/shard_map/ppermute | solution.py:608
  161.5 4.7 fusion.327
  166.3 4.9 slice.330
  171.6 23.6 %fusion.325 = (f32[512]{0:T(512)S(1)}, f32[512,3072]{1,0:T(8,128)}, f32[512,3072]{1,0:T(8,128)}, f32[512,3072]{1,0:T(8,128)}) fusion(f32[3072]{0:T(1024)S(1)} %add.1958, bf16[768,768]{1,0:T(8,128)(2,1)} %bitcast.215, bf16[768,768]{1,0:T(8,128)(2,1)} %bitcast.217, bf16[768,768]{1,0:T(8,128)(2,1)} %bitcast.219, bf16[768,768]{1,0:T(8,128)(2,1)} %bitcast.213, ...), kind=kOutput, calls=%fused_computation.723 | convolution fusion | flops 2540568064 | bytes 25190400 | tf_op jit(solution)/shard_map/dot_general | solution.py:48
  195.3 6.7 %multiply_reduce_fusion = (f32[512]{0:T(512)S(1)}, f32[512]{0:T(512)S(1)}, f32[3072,512]{0,1:T(8,128)S(1)}) fusion(f32[512,3072]{1,0:T(8,128)} %get-tuple-element.126, f32[3072]{0:T(1024)S(1)} %mul.531, f32[512]{0:T(512)S(1)} %broadcast_multiply_fusion.1, bf16[3072,768]{1,0:T(8,128)(2,1)} %bitcast.204, bf16[512,768]{1,0:T(8,128)(2,1)S(1)} %copy-done.28), kind=kOutput, calls=%fused_computation.14 | convolution fusion | flops 2425355264 | bytes 18106368 | tf_op jit(solution)/shard_map/dot_general | solution.py:42
  202.0 4.6 fusion.6
  208.2 9.1 %fusion.322 = (bf16[3072]{0:T(1024)(128)(2,1)S(1)}, bf16[512,3072]{1,0:T(8,128)(2,1)}) fusion(f32[512,3072]{1,0:T(8,128)S(1)} %bitcast.195, f32[512]{0:T(512)S(1)} %negate_multiply_fusion.4, f32[512]{0:T(512)S(1)} %get-tuple-element.207, f32[512,3072]{1,0:T(8,128)S(1)} %bitcast.189, f32[512]{0:T(512)S(1)} %broadcast_multiply_fusion.1, ...), kind=kLoop, calls=%fused_computation.720 | loop fusion | flops 36172800 | bytes 28350464 | tf_op jit(solution)/shard_map/reduce_sum | solution.py:835
  217.2 6.7 %multiply_reduce_fusion.2 = (bf16[768]{0:T(1024)(128)(2,1)S(1)}, f32[512]{0:T(512)S(1)}, bf16[768]{0:T(1024)(128)(2,1)S(1)}, f32[512,768]{1,0:T(8,128)S(1)}) fusion(f32[512,768]{1,0:T(8,128)S(1)} %copy-done.13, f32[512]{0:T(512)S(1)} %fusion.290, f32[512]{0:T(512)S(1)} %broadcast_multiply_fusion.3, f32[768]{0:T(1024)S(1)} %mul.522, ...), kind=kOutput, calls=%fused_computation.83 | convolution fusion | flops 2437937152 | bytes 11022336 | tf_op jit(solution)/shard_map/dot_general | solution.py:42
  224.0 3.4 convolution_convert_fusion.1
  231.0 2.0 convolution_convert_fusion.2
  234.4 1.7 fusion.328
  237.9 4.3 convolution_convert_fusion
  242.2 3.8 convert_element_type.349
  246.0 3.2 copy.87
  249.2 3.9 convert_element_type.351
  253.2 3.1 reduce_sum.362
  257.2 2.6 constant_dynamic-update-slice_fusion.10
  262.0 4.9 constant_dynamic-update-slice_fusion.7
  268.8 9.8 %pad.32 = bf16[32,224,768]{2,1,0:T(8,128)(2,1)} pad(bf16[32,217,768]{2,1,0:T(8,128)(2,1)} %copy_dynamic-update-slice_fusion, bf16[]{:T(256)} %constant.781.clone.1), padding=0_0x0_7x0_0 | pad | bytes 21676034 | tf_op jit(solution)/shard_map/jit(_pad)/pad | solution.py:865
  282.8 2.9 fusion.2
  285.7 4.7 copy.82
  290.5 5.1 collective-permute-done.13
  295.6 1.7 broadcast_select_fusion.7
  298.8 7.0 %shard_map.368 = (bf16[3,128,2048]{2,1,0:T(8,128)(2,1)}, bf16[3,128,2048]{2,1,0:T(8,128)(2,1)}, bf16[3,2048,128]{2,1,0:T(8,128)(2,1)}, bf16[3,128,1024]{2,1,0:T(...) custom-call(s32[16]{0:T(128)} %concatenate.102.facts, ...), custom_call_target="tpu_custom_call" | custom-call | bytes 4866048 | tf_op jit(solution)/shard_map/pallas_call | solution.py:594
  305.9 6.3 %shard_map.371 = (bf16[3,864,128]{2,1,0:T(8,128)(2,1)}, bf16[3,864,128]{2,1,0:T(8,128)(2,1)}, bf16[3,352,128]{2,1,0:T(8,128)(2,1)}, bf16[3,352,128]{2,1,0:T(8,12...) custom-call(s32[16]{0:T(128)} %concatenate.102.facts, ...), custom_call_target="tpu_custom_call" | custom-call | flops 8053063680 | bytes 6881280 | tf_op jit(solution)/shard_map/pallas_call | solution.py:594
  313.0 6.0 %add_convert_fusion.3 = bf16[512,768]{1,0:T(8,128)(2,1)} fusion(f32[512,768]{1,0:T(8,128)S(1)} %copy-done.14, bf16[512,3072]{1,0:T(8,128)(2,1)S(1)} %copy-done.25, bf16[3072,768]{1,0:T(8,128)(2,1)} %bitcast.205, f32[768]{0:T(1024)S(1)} %add.1966), kind=kOutput, calls=%fused_computation.90 | convolution fusion | flops 2417098752 | bytes 10226688 | tf_op jit(solution)/shard_map/dot_general | solution.py:48
  321.2 4.2 shard_map.370
  329.7 21.0 %shard_map.369 = (f32[3,2048,128]{2,1,0:T(8,128)}, f32[3,64,2048]{2,1,0:T(8,128)}) custom-call(bf16[3,2048,128]{2,1,0:T(8,128)(2,1)} %get-tuple-element.60.kv, bf16[3,2048,128]{2,1,0:T(8,128)(2,1)} %select_convert_fusion.extra_k, bf16[3,128,2048]{2,1,0:T(8,128)(2,1)} %get-tuple-element.70.queries, bf16[3,128,2048]{2,1,0:T(8,128)(2,1)} %get-tuple-element.71.grads, ...), custom_call_target="tpu_custom_call" | custom-call | flops 16106127360 | bytes 7864320 | tf_op jit(solution)/shard_map/pallas_call | solution.py:594
  350.7 6.2 %collective-permute-done.14.refs_3_ = bf16[3,1024,128]{2,1,0:T(8,128)(2,1)S(1)} collective-permute-done((bf16[3,1024,128]{2,1,0:T(8,128)(2,1)}, bf16[3,1024,128]{2,1,0:T(8,128)(2,1)S(1)}, u32[]{:S(2)}, u32[]{:S(2)}) %collective-permute-start.14) | collective-permute-done | bytes 786464 | tf_op jit(solution)/shard_map/ppermute | solution.py:627
  356.9 51.5 %collective-permute-done.20.refs_5_ = bf16[3,352,128]{2,1,0:T(8,128)(2,1)S(1)} collective-permute-done((bf16[3,352,128]{2,1,0:T(8,128)(2,1)S(1)}, bf16[3,352,128]{2,1,0:T(8,128)(2,1)S(1)}, u32[]{:S(2)}, u32[]{:S(2)}) %collective-permute-start.20) | collective-permute-done | bytes 270368 | tf_op jit(solution)/shard_map/ppermute | solution.py:627
  409.3 6.6 %shard_map.372 = (bf16[2048,384]{1,0:T(8,128)(2,1)}, bf16[3,64,2048]{2,1,0:T(8,128)(2,1)}) custom-call(s32[16]{0:T(128)} %concatenate.102.facts, f32[3,2048,128]{2,1,0:T(8,128)} %get-tuple-element.73.pair, f32[3,64,2048]{2,1,0:T(8,128)} %get-tuple-element.74.own_q, f32[3,64,1024]{2,1,0:T(8,128)} %get-tuple-element.78.refs_0_, ...), custom_call_target="tpu_custom_call" | custom-call | bytes 7913472 | tf_op jit(solution)/shard_map/pallas_call | solution.py:594
  417.4 1.8 convert_reduce_fusion.1
  419.3 1.8 fusion.335
  421.1 4.7 fusion.319
  425.9 11.5 %collective-permute-start.23 = (f32[24,128]{1,0:T(8,128)S(1)}, f32[24,128]{1,0:T(8,128)S(1)}, u32[]{:S(2)}, u32[]{:S(2)}) collective-permute-start(f32[24,128]{1,0:T(8,128)S(1)} %pad_bitcast_fusion.1), channel_id=1, source_target_pairs={{0,16},{2,18},{4,20},{6,22},{8,24},{10,26},{12,28},{14,30},{16,0},... | collective-permute-start | bytes 36872 | tf_op jit(solution)/shard_map/ppermute | solution.py:608
  437.4 4.2 convolution_convert_fusion.3
  441.7 2.4 collective-permute-start.24
  444.4 2.1 collective-permute-done.24
  466.3 14.9 %collective-permute-done.28 = bf16[4,96,576]{2,1,0:T(8,128)(2,1)S(1)} collective-permute-done((bf16[4,96,576]{2,1,0:T(8,128)(2,1)S(1)}, bf16[4,96,576]{2,1,0:T(8,128)(2,1)S(1)}, u32[]{:S(2)}, u32[]{:S(2)}) %collective-permute-start.28) | collective-permute-done | bytes 442400 | tf_op jit(solution)/shard_map/ppermute | solution.py:608
  482.3 6.8 %collective-permute-done.29 = bf16[2,96,576]{2,1,0:T(8,128)(2,1)S(1)} collective-permute-done((bf16[2,96,576]{2,1,0:T(8,128)(2,1)S(1)}, bf16[2,96,576]{2,1,0:T(8,128)(2,1)S(1)}, u32[]{:S(2)}, u32[]{:S(2)}) %collective-permute-start.29) | collective-permute-done | bytes 221216 | tf_op jit(solution)/shard_map/ppermute | solution.py:608
  490.5 3.7 collective-permute-done.30
  495.0 3.6 collective-permute-done.31
  499.1 2.3 fusion.12
  505.1 13.7 %collective-permute-done.22 = bf16[512,768]{1,0:T(8,128)(2,1)} collective-permute-done((bf16[512,768]{1,0:T(8,128)(2,1)}, bf16[512,768]{1,0:T(8,128)(2,1)}, u32[]{:S(2)}, u32[]{:S(2)}) %collective-permute-start.22) | collective-permute-done | bytes 786464 | tf_op jit(solution)/shard_map/ppermute | solution.py:608
  518.9 1.8 fusion.29
  520.7 2.0 fusion.318
  522.8 3.2 add_add_fusion.4
  (417 shorter events, 107.1 us)
Async XLA Ops:
  7.2 17.2 %copy-start = (bf16[768,384]{1,0:T(8,128)(2,1)S(1)}, bf16[768,384]{1,0:T(8,128)(2,1)}, u32[]{:S(2)}) copy-start(bf16[768,384]{1,0:T(8,128)(2,1)} %param.24) | copy-start | bytes 1769476
  7.2 9.9 %copy-start.32 = (bf16[384,768]{1,0:T(8,128)(2,1)S(1)}, bf16[384,768]{1,0:T(8,128)(2,1)}, u32[]{:S(2)}) copy-start(bf16[384,768]{1,0:T(8,128)(2,1)} %param.31) | copy-start | bytes 1769476
  7.2 11.2 %copy-start.19 = (bf16[1024,768]{1,0:T(8,128)(2,1)S(1)}, bf16[1024,768]{1,0:T(8,128)(2,1)}, u32[]{:S(2)}) copy-start(bf16[1024,768]{1,0:T(8,128)(2,1)} %param.21) | copy-start | bytes 4718596
  7.2 153.2 %all-gather.3.cloned.1.call-start = ((), (), s32[]{:S(2)}) async-start(), calls=%async_computation.2 | async-start | bytes 10543104 | tf_op jit(solution)/shard_map/all_gather | solution.py:692
  16.3 509.6 %reduce-scatter.2.cloned.1.call-start = ((), (), s32[]{:S(2)}) async-start(), calls=%async_computation.1 | async-start | bytes 11354112 | tf_op jit(solution)/shard_map/reduce_scatter | solution.py:866
  18.0 64.2 %collective-permute-start.11 = (bf16[400,768]{1,0:T(8,128)(2,1)}, bf16[400,768]{1,0:T(8,128)(2,1)}, u32[]{:S(2)}, u32[]{:S(2)}) collective-permute-start(bf16[400,768]{1,0:T(8,128)(2,1)} %fusion.53), channel_id=1, source_target_pairs={{0,1},{1,0},{2,3},{3,2},{4,5},{5,4},{6,7},{7,6},{8,9},{9,8},{10,11... | collective-permute-start | bytes 1843208 | tf_op jit(solution)/shard_map/ppermute | solution.py:608
  19.2 138.7 %copy-start.10 = (bf16[512,768]{1,0:T(8,128)(2,1)}, bf16[512,768]{1,0:T(8,128)(2,1)S(1)}, u32[]{:S(2)}) copy-start(bf16[512,768]{1,0:T(8,128)(2,1)S(1)} %get-tuple-element.124) | copy-start | bytes 2359300
  19.2 23.1 %collective-permute-start = (bf16[512,768]{1,0:T(8,128)(2,1)S(1)}, bf16[512,768]{1,0:T(8,128)(2,1)}, u32[]{:S(2)}, u32[]{:S(2)}) collective-permute-start(bf16[512,768]{1,0:T(8,128)(2,1)S(1)} %get-tuple-element.124), channel_id=1, source_target_pairs={{0,2},{2,0},{4,6},{6,4},{8,10},{10,8},{12,14},{14,12},{16,18},{18,... | collective-permute-start | bytes 2359304 | tf_op jit(solution)/shard_map/ppermute | solution.py:608
  23.9 25.9 %copy-start.51 = (pred[64]{0:T(512)(128)(4,1)}, pred[64]{0:T(512)(128)(4,1)S(1)}, u32[]{:S(2)}) copy-start(pred[64]{0:T(512)(128)(4,1)S(1)} %get-tuple-element.258) | copy-start | bytes 196
  23.9 25.9 %copy-start.53 = (pred[64]{0:T(512)(128)(4,1)}, pred[64]{0:T(512)(128)(4,1)S(1)}, u32[]{:S(2)}) copy-start(pred[64]{0:T(512)(128)(4,1)S(1)} %get-tuple-element.259) | copy-start | bytes 196
  24.5 19.1 %copy-start.34 = (bf16[768,192]{1,0:T(8,128)(2,1)}, bf16[768,192]{1,0:T(8,128)(2,1)S(1)}, u32[]{:S(2)}) copy-start(bf16[768,192]{1,0:T(8,128)(2,1)S(1)} %constant_dynamic-slice_fusion.12) | copy-start | bytes 884740
  24.6 20.6 %copy-start.15 = (bf16[768,3,128]{0,2,1:T(8,128)(2,1)}, bf16[768,3,128]{0,2,1:T(8,128)(2,1)S(1)}, u32[]{:S(2)}) copy-start(bf16[768,3,128]{0,2,1:T(8,128)(2,1)S(1)} %pad_maximum_fusion.11) | copy-start | bytes 1769476
  28.7 13.6 %copy-start.62 = (bf16[384]{0:T(512)(128)(2,1)S(1)}, bf16[384]{0:T(512)(128)(2,1)}, u32[]{:S(2)}) copy-start(bf16[384]{0:T(512)(128)(2,1)} %param.25) | copy-start | bytes 2308
  28.7 13.7 %copy-start.56 = (bf16[768]{0:T(1024)(128)(2,1)S(1)}, bf16[768]{0:T(1024)(128)(2,1)}, u32[]{:S(2)}) copy-start(bf16[768]{0:T(1024)(128)(2,1)} %param.22) | copy-start | bytes 4612
  28.7 14.3 %copy-start.61 = (bf16[768]{0:T(1024)(128)(2,1)S(1)}, bf16[768]{0:T(1024)(128)(2,1)}, u32[]{:S(2)}) copy-start(bf16[768]{0:T(1024)(128)(2,1)} %param.23) | copy-start | bytes 4612
  29.2 13.1 %copy-start.49 = (bf16[3,2112,128]{2,1,0:T(8,128)(2,1)}, bf16[3,2112,128]{2,1,0:T(8,128)(2,1)S(1)}, u32[]{:S(2)}) copy-start(bf16[3,2112,128]{2,1,0:T(8,128)(2,1)S(1)} %fusion.71.refs_8_.refs_10_) | copy-start | bytes 4866052
  42.3 9.7 %collective-permute-start.1 = (bf16[512,768]{1,0:T(8,128)(2,1)}, bf16[512,768]{1,0:T(8,128)(2,1)S(1)}, u32[]{:S(2)}, u32[]{:S(2)}) collective-permute-start(bf16[512,768]{1,0:T(8,128)(2,1)} %collective-permute-done), channel_id=1, source_target_pairs={{0,1},{1,0},{2,3},{3,2},{4,5},{5,4},{6,7},{7,6},{8,9},{9,8},{10,11... | collective-permute-start | bytes 2359304 | tf_op jit(solution)/shard_map/ppermute | solution.py:608
  56.4 13.1 %copy-start.52 = (pred[64]{0:T(512)(128)(4,1)S(1)}, pred[64]{0:T(512)(128)(4,1)}, u32[]{:S(2)}) copy-start(pred[64]{0:T(512)(128)(4,1)} %copy-done.51) | copy-start | bytes 196
  56.4 13.1 %copy-start.54 = (pred[64]{0:T(512)(128)(4,1)S(1)}, pred[64]{0:T(512)(128)(4,1)}, u32[]{:S(2)}) copy-start(pred[64]{0:T(512)(128)(4,1)} %copy-done.53) | copy-start | bytes 196
  56.4 19.2 %copy-start.55 = (f32[512]{0:T(512)S(1)}, f32[512]{0:T(512)}, u32[]{:S(2)}) copy-start(f32[512]{0:T(512)} %get-tuple-element.123) | copy-start | bytes 6148
  56.4 19.7 %copy-start.57 = (bf16[768]{0:T(1024)(128)(2,1)S(1)}, bf16[768]{0:T(1024)(128)(2,1)}, u32[]{:S(2)}) copy-start(bf16[768]{0:T(1024)(128)(2,1)} %param.22) | copy-start | bytes 4612
  56.4 20.3 %copy-start.60 = (bf16[768]{0:T(1024)(128)(2,1)S(1)}, bf16[768]{0:T(1024)(128)(2,1)}, u32[]{:S(2)}) copy-start(bf16[768]{0:T(1024)(128)(2,1)} %param.32) | copy-start | bytes 4612
  56.4 23.8 %copy-start.33 = (bf16[3,512,128]{2,1,0:T(8,128)(2,1)S(1)}, bf16[3,512,128]{2,1,0:T(8,128)(2,1)}, u32[]{:S(2)}) copy-start(bf16[3,512,128]{2,1,0:T(8,128)(2,1)} %get-tuple-element.203) | copy-start | bytes 1179652
  64.9 43.7 %collective-permute-start.3 = (bf16[3,864,128]{2,1,0:T(8,128)(2,1)}, bf16[3,864,128]{2,1,0:T(8,128)(2,1)}, u32[]{:S(2)}, u32[]{:S(2)}) collective-permute-start(bf16[3,864,128]{2,1,0:T(8,128)(2,1)} %get-tuple-element.66), channel_id=1, source_target_pairs={{0,8},{2,10},{4,12},{6,14},{16,24},{18,26},{20,28},{22,30},{1,9},{... | collective-permute-start | bytes 1990664 | tf_op jit(solution)/shard_map/ppermute | solution.py:614
  70.4 37.5 %collective-permute-start.5 = (bf16[3,352,128]{2,1,0:T(8,128)(2,1)}, bf16[3,352,128]{2,1,0:T(8,128)(2,1)}, u32[]{:S(2)}, u32[]{:S(2)}) collective-permute-start(bf16[3,352,128]{2,1,0:T(8,128)(2,1)} %get-tuple-element.67), channel_id=1, source_target_pairs={{0,16},{2,18},{4,20},{6,22},{8,24},{10,26},{12,28},{14,30},{1,17},... | collective-permute-start | bytes 811016 | tf_op jit(solution)/shard_map/ppermute | solution.py:614
  76.8 47.5 %collective-permute-start.2 = (bf16[3,1024,128]{2,1,0:T(8,128)(2,1)}, bf16[3,1024,128]{2,1,0:T(8,128)(2,1)S(1)}, u32[]{:S(2)}, u32[]{:S(2)}) collective-permute-start(bf16[3,1024,128]{2,1,0:T(8,128)(2,1)} %get-tuple-element.63), channel_id=1, source_target_pairs={{0,4},{2,6},{8,12},{10,14},{16,20},{18,22},{24,28},{26,30},{1,5},{... | collective-permute-start | bytes 2359304 | tf_op jit(solution)/shard_map/ppermute | solution.py:614
  107.9 15.6 %collective-permute-start.6 = (bf16[3,352,128]{2,1,0:T(8,128)(2,1)}, bf16[3,352,128]{2,1,0:T(8,128)(2,1)S(1)}, u32[]{:S(2)}, u32[]{:S(2)}) collective-permute-start(bf16[3,352,128]{2,1,0:T(8,128)(2,1)} %collective-permute-done.5.refs_2_), channel_id=1, source_target_pairs={{16,24},{18,26},{20,28},{22,30},{24,16},{26,18},{28,20},{30,22},{1... | collective-permute-start | bytes 811016 | tf_op jit(solution)/shard_map/ppermute | solution.py:608
  108.6 20.2 %collective-permute-start.4 = (bf16[3,864,128]{2,1,0:T(8,128)(2,1)}, bf16[3,864,128]{2,1,0:T(8,128)(2,1)S(1)}, u32[]{:S(2)}, u32[]{:S(2)}) collective-permute-start(bf16[3,864,128]{2,1,0:T(8,128)(2,1)} %collective-permute-done.3.refs_0_), channel_id=1, source_target_pairs={{8,12},{10,14},{12,8},{14,10},{24,28},{26,30},{28,24},{30,26},{9,1... | collective-permute-start | bytes 1990664 | tf_op jit(solution)/shard_map/ppermute | solution.py:608
  122.9 5.8 %collective-permute-start.7 = (bf16[3,352,128]{2,1,0:T(8,128)(2,1)}, bf16[3,352,128]{2,1,0:T(8,128)(2,1)S(1)}, u32[]{:S(2)}, u32[]{:S(2)}) collective-permute-start(bf16[3,352,128]{2,1,0:T(8,128)(2,1)} %collective-permute-done.5.refs_2_), channel_id=1, source_target_pairs={{16,20},{18,22},{20,16},{22,18},{24,28},{26,30},{28,24},{30,26},{1... | collective-permute-start | bytes 811016 | tf_op jit(solution)/shard_map/ppermute | solution.py:608
  123.6 5.2 collective-permute-start.8
  140.7 13.0 %collective-permute-start.9 = (bf16[192,1024]{0,1:T(8,128)(2,1)}, bf16[192,1024]{0,1:T(8,128)(2,1)}, u32[]{:S(2)}, u32[]{:S(2)}) collective-permute-start(bf16[192,1024]{0,1:T(8,128)(2,1)} %copy.96), channel_id=1, source_target_pairs={{0,2},{2,0},{4,6},{6,4},{8,10},{10,8},{12,14},{14,12},{16,18},{18,... | collective-permute-start | bytes 1179656 | tf_op jit(solution)/shard_map/ppermute | solution.py:608
  155.1 1.9 collective-permute-start.10
  171.6 23.7 %copy-start.28 = (bf16[512,768]{1,0:T(8,128)(2,1)S(1)}, bf16[512,768]{1,0:T(8,128)(2,1)}, u32[]{:S(2)}) copy-start(bf16[512,768]{1,0:T(8,128)(2,1)} %param.41) | copy-start | bytes 2359300
  208.2 9.1 %copy-start.13 = (f32[512,768]{1,0:T(8,128)S(1)}, f32[512,768]{1,0:T(8,128)}, u32[]{:S(2)}) copy-start(f32[512,768]{1,0:T(8,128)} %copy-done.12) | copy-start | bytes 4718596
  234.0 44.7 %collective-permute-start.12 = (bf16[384,512]{0,1:T(8,128)(2,1)S(1)}, bf16[384,512]{0,1:T(8,128)(2,1)}, u32[]{:S(2)}, u32[]{:S(2)}) collective-permute-start(bf16[384,512]{0,1:T(8,128)(2,1)S(1)} %dynamic-slice_bitcast_fusion.2), channel_id=1, source_target_pairs={{0,1},{1,0},{2,3},{3,2},{4,5},{5,4},{6,7},{7,6},{8,9},{9,8},{10,11... | collective-permute-start | bytes 1179656 | tf_op jit(solution)/shard_map/ppermute | solution.py:608
  281.4 14.2 %collective-permute-start.13 = (bf16[192,1024]{0,1:T(8,128)(2,1)S(1)}, bf16[192,1024]{0,1:T(8,128)(2,1)}, u32[]{:S(2)}, u32[]{:S(2)}) collective-permute-start(bf16[192,1024]{0,1:T(8,128)(2,1)S(1)} %fusion.54), channel_id=1, source_target_pairs={{0,2},{2,0},{4,6},{6,4},{8,10},{10,8},{12,14},{14,12},{16,18},{18,... | collective-permute-start | bytes 1179656 | tf_op jit(solution)/shard_map/ppermute | solution.py:608
  305.8 7.2 %copy-start.14 = (f32[512,768]{1,0:T(8,128)S(1)}, f32[512,768]{1,0:T(8,128)}, u32[]{:S(2)}) copy-start(f32[512,768]{1,0:T(8,128)} %copy-done.12) | copy-start | bytes 4718596
  312.2 7.6 %copy-start.69 = (bf16[3,352,128]{2,1,0:T(8,128)(2,1)S(1)}, bf16[3,352,128]{2,1,0:T(8,128)(2,1)}, u32[]{:S(2)}) copy-start(bf16[3,352,128]{2,1,0:T(8,128)(2,1)} %get-tuple-element.91) | copy-start | bytes 811012
  312.2 8.3 %copy-start.46 = (bf16[3,352,128]{2,1,0:T(8,128)(2,1)S(1)}, bf16[3,352,128]{2,1,0:T(8,128)(2,1)}, u32[]{:S(2)}) copy-start(bf16[3,352,128]{2,1,0:T(8,128)(2,1)} %get-tuple-element.92) | copy-start | bytes 811012
  312.2 8.2 %collective-permute-start.18 = (bf16[3,352,128]{2,1,0:T(8,128)(2,1)}, bf16[3,352,128]{2,1,0:T(8,128)(2,1)S(1)}, u32[]{:S(2)}, u32[]{:S(2)}) collective-permute-start(bf16[3,352,128]{2,1,0:T(8,128)(2,1)} %get-tuple-element.93), channel_id=1, source_target_pairs={{16,20},{18,22},{20,16},{22,18},{24,28},{26,30},{28,24},{30,26},{1... | collective-permute-start | bytes 811016 | tf_op jit(solution)/shard_map/ppermute | solution.py:608
  319.0 9.2 %collective-permute-start.15 = (bf16[3,864,128]{2,1,0:T(8,128)(2,1)S(1)}, bf16[3,864,128]{2,1,0:T(8,128)(2,1)S(1)}, u32[]{:S(2)}, u32[]{:S(2)}) collective-permute-start(bf16[3,864,128]{2,1,0:T(8,128)(2,1)S(1)} %copy-done.65), channel_id=1, source_target_pairs={{8,12},{10,14},{12,8},{14,10},{24,28},{26,30},{28,24},{30,26},{9,1... | collective-permute-start | bytes 1990664 | tf_op jit(solution)/shard_map/ppermute | solution.py:608
  319.7 7.0 %collective-permute-start.17 = (bf16[3,352,128]{2,1,0:T(8,128)(2,1)S(1)}, bf16[3,352,128]{2,1,0:T(8,128)(2,1)S(1)}, u32[]{:S(2)}, u32[]{:S(2)}) collective-permute-start(bf16[3,352,128]{2,1,0:T(8,128)(2,1)S(1)} %copy-done.69), channel_id=1, source_target_pairs={{16,20},{18,22},{20,16},{22,18},{24,28},{26,30},{28,24},{30,26},{1... | collective-permute-start | bytes 811016 | tf_op jit(solution)/shard_map/ppermute | solution.py:608
  320.5 6.2 %collective-permute-start.19 = (bf16[3,352,128]{2,1,0:T(8,128)(2,1)S(1)}, bf16[3,352,128]{2,1,0:T(8,128)(2,1)S(1)}, u32[]{:S(2)}, u32[]{:S(2)}) collective-permute-start(bf16[3,352,128]{2,1,0:T(8,128)(2,1)S(1)} %add_convert_fusion.8), channel_id=1, source_target_pairs={{16,24},{18,26},{20,28},{22,30},{24,16},{26,18},{28,20},{30,22},{1... | collective-permute-start | bytes 811016 | tf_op jit(solution)/shard_map/ppermute | solution.py:608
  325.4 31.4 %collective-permute-start.14 = (bf16[3,1024,128]{2,1,0:T(8,128)(2,1)}, bf16[3,1024,128]{2,1,0:T(8,128)(2,1)S(1)}, u32[]{:S(2)}, u32[]{:S(2)}) collective-permute-start(bf16[3,1024,128]{2,1,0:T(8,128)(2,1)} %get-tuple-element.87), channel_id=1, source_target_pairs={{4,0},{6,2},{12,8},{14,10},{20,16},{22,18},{28,24},{30,26},{5,1},{... | collective-permute-start | bytes 2359304 | tf_op jit(solution)/shard_map/ppermute | solution.py:627
  326.9 81.5 %collective-permute-start.20 = (bf16[3,352,128]{2,1,0:T(8,128)(2,1)S(1)}, bf16[3,352,128]{2,1,0:T(8,128)(2,1)S(1)}, u32[]{:S(2)}, u32[]{:S(2)}) collective-permute-start(bf16[3,352,128]{2,1,0:T(8,128)(2,1)S(1)} %add_convert_fusion.7), channel_id=1, source_target_pairs={{16,0},{18,2},{20,4},{22,6},{24,8},{26,10},{28,12},{30,14},{17,1},... | collective-permute-start | bytes 811016 | tf_op jit(solution)/shard_map/ppermute | solution.py:627
  328.4 80.0 %collective-permute-start.16 = (bf16[3,864,128]{2,1,0:T(8,128)(2,1)S(1)}, bf16[3,864,128]{2,1,0:T(8,128)(2,1)S(1)}, u32[]{:S(2)}, u32[]{:S(2)}) collective-permute-start(bf16[3,864,128]{2,1,0:T(8,128)(2,1)S(1)} %add_convert_fusion.5), channel_id=1, source_target_pairs={{8,0},{10,2},{12,4},{14,6},{24,16},{26,18},{28,20},{30,22},{9,1},{... | collective-permute-start | bytes 1990664 | tf_op jit(solution)/shard_map/ppermute | solution.py:627
  356.9 51.5 %copy-start.38 = (bf16[3,1024,128]{2,1,0:T(8,128)(2,1)}, bf16[3,1024,128]{2,1,0:T(8,128)(2,1)S(1)}, u32[]{:S(2)}) copy-start(bf16[3,1024,128]{2,1,0:T(8,128)(2,1)S(1)} %collective-permute-done.14.refs_3_) | copy-start | bytes 2359300
  425.9 18.2 %copy-start.23 = (bf16[2048,768]{1,0:T(8,128)(2,1)S(1)}, bf16[2048,768]{1,0:T(8,128)(2,1)}, u32[]{:S(2)}) copy-start(bf16[2048,768]{1,0:T(8,128)(2,1)} %get-tuple-element.135) | copy-start | bytes 9437188
  425.9 15.8 %collective-permute-start.23 = (f32[24,128]{1,0:T(8,128)S(1)}, f32[24,128]{1,0:T(8,128)S(1)}, u32[]{:S(2)}, u32[]{:S(2)}) collective-permute-start(f32[24,128]{1,0:T(8,128)S(1)} %pad_bitcast_fusion.1), channel_id=1, source_target_pairs={{0,16},{2,18},{4,20},{6,22},{8,24},{10,26},{12,28},{14,30},{16,0},... | collective-permute-start | bytes 36872 | tf_op jit(solution)/shard_map/ppermute | solution.py:608
  437.4 10.1 %copy-start.37 = (bf16[3,64,2048]{2,1,0:T(8,128)(2,1)S(1)}, bf16[3,64,2048]{2,1,0:T(8,128)(2,1)}, u32[]{:S(2)}) copy-start(bf16[3,64,2048]{2,1,0:T(8,128)(2,1)} %get-tuple-element.94) | copy-start | bytes 2359300
  441.7 4.8 collective-permute-start.24
  444.3 54.8 %collective-permute-start.21 = (bf16[2,512,768]{2,1,0:T(8,128)(2,1)S(1)}, bf16[2,512,768]{2,1,0:T(8,128)(2,1)}, u32[]{:S(2)}, u32[]{:S(2)}) collective-permute-start(bf16[2,512,768]{2,1,0:T(8,128)(2,1)S(1)} %dynamic-slice_bitcast_fusion), channel_id=1, source_target_pairs={{0,1},{1,0},{2,3},{3,2},{4,5},{5,4},{6,7},{7,6},{8,9},{9,8},{10,11... | collective-permute-start | bytes 4718600 | tf_op jit(solution)/shard_map/ppermute | solution.py:608
  446.5 3.7 collective-permute-start.25
  450.2 4.2 collective-permute-start.26
  451.7 29.4 %collective-permute-start.28 = (bf16[4,96,576]{2,1,0:T(8,128)(2,1)S(1)}, bf16[4,96,576]{2,1,0:T(8,128)(2,1)S(1)}, u32[]{:S(2)}, u32[]{:S(2)}) collective-permute-start(bf16[4,96,576]{2,1,0:T(8,128)(2,1)S(1)} %fusion.56), channel_id=1, source_target_pairs={{0,16},{2,18},{4,20},{6,22},{8,24},{10,26},{12,28},{14,30},{16,0},... | collective-permute-start | bytes 1327112 | tf_op jit(solution)/shard_map/ppermute | solution.py:608
  455.8 25.6 %collective-permute-start.27 = (f32[12,128]{1,0:T(8,128)}, f32[12,128]{1,0:T(8,128)}, u32[]{:S(2)}, u32[]{:S(2)}) collective-permute-start(f32[12,128]{1,0:T(8,128)} %fusion.182), channel_id=1, source_target_pairs={{0,1},{1,0},{2,3},{3,2},{4,5},{5,4},{6,7},{7,6},{8,9},{9,8},{10,11... | collective-permute-start | bytes 18440 | tf_op jit(solution)/shard_map/ppermute | solution.py:608
  481.4 7.8 %collective-permute-start.29 = (bf16[2,96,576]{2,1,0:T(8,128)(2,1)S(1)}, bf16[2,96,576]{2,1,0:T(8,128)(2,1)S(1)}, u32[]{:S(2)}, u32[]{:S(2)}) collective-permute-start(bf16[2,96,576]{2,1,0:T(8,128)(2,1)S(1)} %constant_dynamic-slice_fusion.4), channel_id=1, source_target_pairs={{0,8},{2,10},{4,12},{6,14},{8,0},{10,2},{12,4},{14,6},{16,24},{18,... | collective-permute-start | bytes 663560 | tf_op jit(solution)/shard_map/ppermute | solution.py:608
  489.3 4.9 collective-permute-start.30
  494.3 4.3 collective-permute-start.31
  501.4 17.5 %copy-start.11 = (bf16[512,768]{1,0:T(8,128)(2,1)S(1)}, bf16[512,768]{1,0:T(8,128)(2,1)}, u32[]{:S(2)}) copy-start(bf16[512,768]{1,0:T(8,128)(2,1)} %copy-done.10) | copy-start | bytes 2359300
  501.4 17.5 %copy-start.48 = (f32[768]{0:T(1024)S(1)}, f32[768]{0:T(1024)}, u32[]{:S(2)}) copy-start(f32[768]{0:T(1024)} %convert_element_type.276) | copy-start | bytes 9220
  501.4 17.5 %copy-start.50 = (f32[512]{0:T(512)S(1)}, f32[512]{0:T(512)}, u32[]{:S(2)}) copy-start(f32[512]{0:T(512)} %broadcast_multiply_fusion.2) | copy-start | bytes 6148
  502.3 16.5 %collective-permute-start.22 = (bf16[512,768]{1,0:T(8,128)(2,1)}, bf16[512,768]{1,0:T(8,128)(2,1)}, u32[]{:S(2)}, u32[]{:S(2)}) collective-permute-start(bf16[512,768]{1,0:T(8,128)(2,1)} %dynamic-slice_bitcast_fusion.1), channel_id=1, source_target_pairs={{0,2},{2,0},{4,6},{6,4},{8,10},{10,8},{12,14},{14,12},{16,18},{18,... | collective-permute-start | bytes 2359304 | tf_op jit(solution)/shard_map/ppermute | solution.py:608
  522.8 8.5 %copy-start.1 = (bf16[768,384]{1,0:T(8,128)(2,1)S(1)}, bf16[768,384]{1,0:T(8,128)(2,1)}, u32[]{:S(2)}) copy-start(bf16[768,384]{1,0:T(8,128)(2,1)} %param.24) | copy-start | bytes 1769476
  (45 other events, 144.4 us)
Sparse Core Ops, SparseCore 0:
  16.5 100.5 all-gather.2
  278.7 203.4 reduce-scatter.1

commit v2 on v1

--- a/solution.py
+++ b/solution.py
@@ -26,10 +26,6 @@
     centered = values - center
     spread = jnp.mean(centered * centered, axis=-1, keepdims=True)
     return centered * lax.rsqrt(spread + EPS) * gain + shift
-
-
-def gelu_norm(before, gain, shift):
-    return layer_norm(jax.nn.gelu(before, approximate=False), gain, shift)
 
 
 def dot_rows(left_side, right_side):
@@ -125,7 +121,7 @@
         total = 1.0 + jnp.where((both & 1) > 0, 1.0, 0.0) + f4 + f6 + f12
     elif stride == 2:
         total = 1.0 + f4 + f6 + f12
-    elif stride == 4:
+    elif stride == 4 and not plan.fold:
         total = 1.0 + f12
     elif stride == 6 and plan.fold:
         total = 1.0 + f12
@@ -378,6 +374,18 @@
     return jnp.concatenate([picked, extra_q], axis=0)
 
 
+def sides(facts, group):
+    return facts[4 * group + 4], facts[4 * group + 5]
+
+
+def swap_if(flag, first, second):
+    return jnp.where(flag == 0, first, second), jnp.where(flag == 0, second, first)
+
+
+def join_if(flag, mine, other, axis):
+    return jnp.concatenate(swap_if(flag, mine, other), axis=axis)
+
+
 def near_kernel(plan, group, facts, q, *refs):
     space = plan.spaces[0]
     count = len(plan.masks(1))
@@ -403,7 +411,7 @@
         packets[level] = [refs.pop(0) for _ in plan.masks(level)]
     spaces = plan.spaces[1:]
     extras = {s.stride: (refs.pop(0), refs.pop(0)) for s in spaces}
-    combined, lse_all = refs.pop(0), refs.pop(0)
+    combined, lse_all, same, other, away = [refs.pop(0) for _ in range(5)]
     held = {s.stride: (refs.pop(0), refs.pop(0)) for s in spaces}
     head = pl.program_id(0)
     near = plan.spaces[0]
@@ -440,19 +448,233 @@
         out, lse = held[space.stride]
         total_here = stat_down(space, first, total_two)
         two = two + wide_up(space, first, out[...] * jnp.exp(lse[0:1] - total_here))
-    combined[0] = out_own[0] * jnp.exp(lse_own[0, 0:1] - total) + wide_up(near, firsts[2], two)
-
-
-def prepare_kernel(plan, group, facts, q, g, combined, lse, *refs):
+    got = out_own[0] * jnp.exp(lse_own[0, 0:1] - total) + wide_up(near, firsts[2], two)
+    combined[0] = got
+    low = got.astype(BF)
+    cross, core = sides(facts, group)
+    half = plan.window // 2
+    mine, gone = swap_if(cross, low[:, :half], low[:, half:])
+    same[0], other[0] = swap_if(core, mine[:, : half // 2], mine[:, half // 2 :])
+    away[0] = jnp.concatenate(swap_if(core, gone[:, : half // 2], gone[:, half // 2 :]), axis=1)
+
+
+def norm_parts(values, width):
+    center = jnp.sum(values, axis=1, keepdims=True) * (1.0 / width)
+    centered = values - center
+    spread = jnp.sum(centered * centered, axis=1, keepdims=True) * (1.0 / width)
+    scale = lax.rsqrt(spread + EPS)
+    return centered * scale, scale
+
+
+def norm_back(grads, gain, plain, scale, width):
+    up = grads * gain
+    mean = jnp.sum(up, axis=1, keepdims=True) * (1.0 / width)
+    cross = jnp.sum(up * plain, axis=1, keepdims=True) * (1.0 / width)
+    gain_grad = jnp.sum(grads * plain, axis=0, keepdims=True)
+    shift_grad = jnp.sum(grads, axis=0, keepdims=True)
+    return (up - mean - plain * cross) * scale, gain_grad, shift_grad
+
+
+class Shares:
+    def __init__(self, devices, width, ff):
+        self.devices, self.width, self.fold = devices, width, ff // width
+        self.up_rows, self.down_rows = width // devices, ff // devices
+        self.out_rows = 2 * width // devices
+        self.up_span = -(-self.up_rows // 16) * 16
+        self.down_at = 2 * self.fold * self.up_span
+        self.out_at = self.down_at + 2 * self.down_rows
+        self.small_at = self.out_at + self.out_rows
+        self.small_size = 3 * self.down_rows + 6 * self.up_rows
+        rows = self.small_at + -(-2 * self.small_size // width)
+        self.rows = -(-rows // 16) * 16
+        self.direct = not (self.up_rows % 8 or self.down_rows % 16 or self.out_rows % 16)
+
+    def stack(self, up, down, out):
+        half = self.width // 2
+        up = up.reshape(self.fold, self.devices, self.up_rows, 2, half)
+        up = jnp.pad(up, ((0, 0), (0, 0), (0, self.up_span - self.up_rows), (0, 0), (0, 0)))
+        up = up.transpose(1, 0, 3, 2, 4).reshape(self.devices, -1, half)
+        down = down.reshape(self.devices, self.down_rows, 2, half)
+        down = down.transpose(0, 2, 1, 3).reshape(self.devices, -1, half)
+        out = out.reshape(-1, self.out_rows, 2, half)
+        out = out.transpose(0, 2, 1, 3).reshape(self.devices, -1, half)
+        stack = jnp.concatenate([up, down, out], axis=1)
+        return jnp.pad(stack, ((0, 0), (0, self.rows - stack.shape[1]), (0, 0)))
+
+    def small(self, values):
+        values = jnp.concatenate(values, axis=1)
+        pad = -values.shape[1] % (self.width // 2)
+        values = jnp.pad(values, ((0, 0), (0, pad)))
+        return values.reshape(self.devices, -1, self.width // 2)
+
+
+def feed_kernel(
+    group,
+    fold,
+    shares,
+    direct,
+    facts,
+    same,
+    across,
+    beside,
+    beyond,
+    tok,
+    cot,
+    out_w,
+    up_w,
+    down_w,
+    narrow,
+    broad,
+    output,
+    hidden_grad,
+    gone,
+    kept_away,
+    kept,
+    broad_g,
+    narrow_g,
+    *rest,
+):
+    *grad_refs, gelu, slope, inner_g = rest
+    cross, core = sides(facts, group)
+    rows, width = tok.shape
+    half = width // 2
+
+    def put_up(j, value):
+        if not direct:
+            grad_refs[0][j] = value.astype(BF)
+            return
+        stack, step, span = grad_refs[0], shares.up_rows, shares.up_span
+        for device in range(shares.devices):
+            piece = value[device * step : device * step + span]
+            if piece.shape[0] < span:
+                piece = jnp.concatenate(
+                    [piece, jnp.zeros((span - piece.shape[0], width), F32)], axis=0
+                )
+            piece = piece.astype(BF)
+            for part in range(2):
+                at = pl.multiple_of((2 * j + part) * span, span)
+                stack[device, pl.ds(at, span)] = piece[:, part * half : (part + 1) * half]
+
+    def put_down(j, value):
+        value = value.astype(BF)
+        if not direct:
+            grad_refs[1][j] = value
+            return
+        stack, step = grad_refs[0], shares.down_rows
+        count = width // step
+        for i in range(count):
+            for part in range(2):
+                at = shares.down_at + part * step
+                stack[j * count + i, at : at + step] = value[
+                    i * step : (i + 1) * step, part * half : (part + 1) * half
+                ]
+
+    def put_out(value):
+        value = value.astype(BF)
+        if not direct:
+            grad_refs[2][...] = value
+            return
+        stack, step = grad_refs[0], shares.out_rows
+        for device in range(shares.devices):
+            i, part = device // 2, device % 2
+            stack[device, shares.out_at : shares.out_at + step] = value[
+                i * step : (i + 1) * step, part * half : (part + 1) * half
+            ]
+    cols = same.shape[0]
+    ff = fold * width
+    here = join_if(cross, same[...], across[:, :rows], 0)
+    there = join_if(cross, beside[...], beyond[...], 0)
+    combined = join_if(core, here, there, 0).T.astype(F32)
+    attn_plain, attn_scale = norm_parts(combined, width)
+    mixed = (attn_plain * narrow[0:1] + narrow[1:2]).astype(BF)
+    hidden = tok[...].astype(F32) + mm(mixed, out_w[...]) + narrow[2:3]
+    feed_plain, feed_scale = norm_parts(hidden, width)
+    feed_in = (feed_plain * narrow[3:4] + narrow[4:5]).astype(BF)
+
+    def forward(j, total):
+        before = mm(feed_in, up_w[j]) + broad[0, j]
+        phi = 0.5 + 0.5 * lax.erf(before * 0.5**0.5)
+        value = before * phi
+        gelu[j] = value
+        slope[j] = phi + before * jnp.exp(before * before * -0.5) * (2.0 * jnp.pi) ** -0.5
+        return total + jnp.sum(value, axis=1, keepdims=True)
+
+    zero = jnp.zeros((rows, 1), F32)
+    center = lax.fori_loop(0, fold, forward, zero) * (1.0 / ff)
+
+    def squares(j, total):
+        value = gelu[j] - center
+        return total + jnp.sum(value * value, axis=1, keepdims=True)
+
+    scale = lax.rsqrt(lax.fori_loop(0, fold, squares, zero) * (1.0 / ff) + EPS)
+
+    def middle(j, carry):
+        total, up_sum, cross_sum = carry
+        plain = (gelu[j] - center) * scale
+        inner = (plain * broad[1, j] + broad[2, j]).astype(BF)
+        total = total + mm(inner, down_w[j])
+        grads = dot_cols(cot[...], down_w[j])
+        put_down(j, dot_rows(inner, cot[...]))
+        broad_g[1, j] = jnp.sum(grads * plain, axis=0, keepdims=True)
+        broad_g[2, j] = jnp.sum(grads, axis=0, keepdims=True)
+        up = grads * broad[1, j]
+        inner_g[j] = up
+        up_sum = up_sum + jnp.sum(up, axis=1, keepdims=True)
+        cross_sum = cross_sum + jnp.sum(up * plain, axis=1, keepdims=True)
+        return total, up_sum, cross_sum
+
+    start = hidden + narrow[5:6]
+    total, up_sum, cross_sum = lax.fori_loop(0, fold, middle, (start, zero, zero))
+    output[...] = total.astype(BF)
+    up_mean = up_sum * (1.0 / ff)
+    cross_mean = cross_sum * (1.0 / ff)
+
+    def back(j, total):
+        plain = (gelu[j] - center) * scale
+        grads = ((inner_g[j] - up_mean - plain * cross_mean) * scale * slope[j]).astype(BF)
+        broad_g[0, j] = jnp.sum(grads.astype(F32), axis=0, keepdims=True)
+        put_up(j, dot_rows(feed_in, grads))
+        return total + dot_cols(grads, up_w[j])
+
+    feed_grads = lax.fori_loop(0, fold, back, jnp.zeros((rows, width), F32))
+    cot_wide = cot[...].astype(F32)
+    got, feed_gain_g, feed_shift_g = norm_back(
+        feed_grads, narrow[3:4], feed_plain, feed_scale, width
+    )
+    hidden_g = cot_wide + got
+    hidden_grad[...] = hidden_g
+    branch = hidden_g.astype(BF)
+    put_out(dot_rows(branch, mixed))
+    mixed_g, attn_gain_g, attn_shift_g = norm_back(
+        dot_cols(branch, out_w[...]), narrow[0:1], attn_plain, attn_scale, width
+    )
+    turned = mixed_g.astype(BF).T
+    mine, other = swap_if(core, turned[: 2 * cols], turned[2 * cols :])
+    gone[...] = jnp.concatenate(swap_if(cross, other[:cols], other[cols:]), axis=0)
+    kept[...], kept_away[...] = swap_if(cross, mine[:cols], mine[cols:])
+    narrow_g[0:1] = jnp.sum(cot_wide, axis=0, keepdims=True)
+    narrow_g[1:2] = feed_gain_g
+    narrow_g[2:3] = feed_shift_g
+    narrow_g[3:4] = jnp.sum(branch.astype(F32), axis=0, keepdims=True)
+    narrow_g[4:5] = attn_gain_g
+    narrow_g[5:6] = attn_shift_g
+    narrow_g[6:8] = jnp.zeros((2, width), F32)
+
+
+def prepare_kernel(plan, group, facts, q, kept, near, far, last, combined, lse, *refs):
     refs = list(refs)
+    cross, core = sides(facts, group)
+    mine = join_if(core, kept[0], near[0], 1)
+    other = join_if(core, far[0], last[0], 1)
+    g = join_if(cross, mine, other, 1)
     strides = [1] + [s.stride for s in plan.spaces]
     extras = {s: refs.pop(0) for s in strides}
     outs = {s: (refs.pop(0), refs.pop(0), refs.pop(0)) for s in strides}
     head = pl.program_id(0)
     total = -lse[0, 0:1]
-    dots = -jnp.sum(g[0].astype(F32) * combined[0], axis=0, keepdims=True)
+    dots = -jnp.sum(g.astype(F32) * combined[0], axis=0, keepdims=True)
     stats = jnp.concatenate([stat_rows(total, 16), stat_rows(dots, 16)], axis=0)
-    stack = jnp.concatenate([q[0], g[0], stats], axis=0)
+    stack = jnp.concatenate([q[0], g, stats], axis=0)
     held = {1: stack}
     for stride in strides:
         if stride > 1:
@@ -608,13 +830,16 @@
     return lax.ppermute(array, axis, [(i, i ^ bit) for i in range(count) if only(i)])
 
 
-def level_send(plan, level, packet):
+def level_jump(plan, level, packet):
     step = 1 << level
     pairs = [(i, i + step) for i in range(plan.seq_count) if not i & step]
-    found = [lax.ppermute(packet, "seq", pairs)]
-    for bit in reversed(range(level - 1)):
-        found = found + [swap(f, "seq", 2 << bit, lambda i: i & step) for f in found]
-    return found
+    return lax.ppermute(packet, "seq", pairs)
+
+
+def level_hop(plan, level, found, hop):
+    bit = level - 2 - hop
+    if bit >= 0:
+        found += [swap(f, "seq", 2 << bit, lambda i: i & (1 << level)) for f in found]
 
 
 def level_return(plan, level, grads):
@@ -677,10 +902,21 @@
     heads = core * heads_here + cross * group + jnp.arange(group, dtype=jnp.int32)
     ff = up_weight.shape[1]
 
+    tokens_half = pick_half(tokens, core, 0)
+    tokens_half, up_weight, down_weight, out_weight, small = lax.optimization_barrier(
+        (
+            tokens_half,
+            up_weight,
+            down_weight,
+            out_weight,
+            [up_bias, inner_gain, inner_shift, feed_gain, feed_shift, down_bias],
+        )
+    )
+
     up_rows = up_weight.shape[0]
     fold = ff // width
     down_rows = down_weight.shape[0]
-    small = jnp.concatenate([up_bias, inner_gain, inner_shift, feed_gain, feed_shift, down_bias])
+    small = jnp.concatenate(small)
     small_at = [down_rows, down_rows, down_rows, up_rows, up_rows, up_rows]
     pad = -small.shape[0] % width
     small_rows = jnp.pad(small, (0, pad)).reshape(-1, width)
@@ -691,7 +927,7 @@
     packed = jnp.pad(packed, ((0, -packed.shape[0] % 16), (0, 0)))
     gathered = lax.all_gather(packed, BOTH, axis=0, tiled=False)
 
-    got = swap(pick_half(tokens, core, 0), "seq", 1)
+    got = swap(tokens_half, "seq", 1)
     other = swap(got, "head", 1)
     partner = in_order(core, got, other, 0)
     window_tokens = in_order(cross, tokens, partner, 0)
@@ -706,7 +942,9 @@
     firsts = [first_of(plan, s, window_index, heads) for s in (2, 4, 6, 12)]
     firsts = [firsts[0]] + [jnp.mod(f - firsts[0], s) // 2 for f, s in zip(firsts[1:], (4, 6, 12))]
     flags = jnp.stack([(window_index >> b) & 1 for b in range(4)])
-    facts = jnp.concatenate([jnp.stack(firsts, axis=1).reshape(-1), flags]).astype(jnp.int32)
+    side = jnp.stack([cross, core])
+    facts = jnp.concatenate([jnp.stack(firsts, axis=1).reshape(-1), flags, side])
+    facts = facts.astype(jnp.int32)
 
     wq = pick_half(query_weight, cross, 1).T
     wk = pick_half(key_weight, cross, 1).reshape(width, group, HEAD_DIM)
@@ -735,7 +973,7 @@
         compiler_params=pltpu.CompilerParams(vmem_limit_bytes=VMEM_LIMIT),
     )(facts, window_tokens, mix_gain_wide, mix_shift_wide, wq, bq, wkv, bkv)
 
-    received = {lv: level_send(plan, lv, pk) for lv, pk in zip(plan.levels, packets)}
+    received = {lv: [level_jump(plan, lv, pk)] for lv, pk in zip(plan.levels, packets)}
 
     on = jnp.asarray(True)
     extra_k = {1: extra_keys(plan, 1, plan.window, window_index, heads, on)}
@@ -763,6 +1001,9 @@
         [(HEAD_DIM, window, F32), (8, window, F32)],
         cost=4 * group * window * window * 128,
     )
+    received, out_own, lse_own = lax.optimization_barrier((received, out_own, lse_own))
+    for lv in plan.levels:
+        level_hop(plan, lv, received[lv], 0)
     out_near, lse_near = head_call(
         functools.partial(near_kernel, plan, group),
         group,
@@ -771,45 +1012,45 @@
         [(HEAD_DIM, near.queries, F32), (8, near.queries, F32)],
         cost=2 * group * window * window * 128,
     )
+    up_full = jnp.stack(
+        [
+            gathered[:, j * up_rows : (j + 1) * up_rows].reshape(width, width)
+            for j in range(fold)
+        ]
+    )
+    down_at = fold * up_rows
+    down_full = gathered[:, down_at : down_at + down_rows].reshape(fold, width, width)
+    received, out_near, lse_near, up_full, down_full = lax.optimization_barrier(
+        (received, out_near, lse_near, up_full, down_full)
+    )
+    for lv in plan.levels:
+        for hop in range(1, lv - 1):
+            level_hop(plan, lv, received[lv], hop)
     far_packets = [r for lv in plan.levels[1:] for r in received[lv]]
     far_extras = [e for s in far for e in (extra_k[s.stride], extra_q[s.stride])]
     scratch = []
     for s in far:
         scratch += [pltpu.VMEM((HEAD_DIM, s.queries), F32), pltpu.VMEM((8, s.queries), F32)]
-    combined, lse_all = head_call(
+    combined, lse_all, same, other, away = head_call(
         functools.partial(far_kernel, plan, group),
         group,
         facts,
         [queries_turned, out_own, lse_own, out_near, lse_near, *far_packets, *far_extras],
-        [(HEAD_DIM, window, F32), (8, window, F32)],
+        [
+            (HEAD_DIM, window, F32),
+            (8, window, F32),
+            (HEAD_DIM, half_rows, BF),
+            (HEAD_DIM, half_rows, BF),
+            (HEAD_DIM, tok_rows, BF),
+        ],
         scratch,
         cost=2 * group * window * window * 128,
     )
 
-    mixed_low = combined.reshape(cols, window).astype(BF)
-    got = swap(pick_half(mixed_low, 1 - cross, 1), "seq", 1)
-    joined = in_order(cross, pick_half(mixed_low, cross, 1), got, 0)
-    got = swap(pick_half(joined, 1 - core, 1), "head", 1)
-    joined = in_order(core, pick_half(joined, core, 1), got, 0)
-
-    mixed_wide = joined.astype(F32).T
-    attn_gain_wide = attn_gain_full.astype(F32)
-    normal_wide, attn_pull = jax.vjp(
-        layer_norm, mixed_wide, attn_gain_wide, attn_shift_full.astype(F32)
-    )
-    mixed = normal_wide.astype(BF)
-    tokens_half = pick_half(tokens, core, 0).astype(F32)
-    hidden = tokens_half + mm(mixed, out_full) + out_bias.astype(F32)
-
-    up_full = jnp.concatenate(
-        [
-            gathered[:, j * up_rows : (j + 1) * up_rows].reshape(width, width)
-            for j in range(fold)
-        ],
-        axis=1,
-    )
-    down_at = fold * up_rows
-    down_full = gathered[:, down_at : down_at + down_rows].reshape(ff, width)
+    across = swap(away, "seq", 1)
+    beside = swap(other, "head", 1)
+    beyond = swap(across[:, :, half_rows:], "head", 1)
+
     small_full = gathered[:, down_at + down_rows : down_at + down_rows + small_rows.shape[0]]
     small_full = small_full.reshape(devices, -1).astype(F32)
     pieces, at = [], 0
@@ -818,32 +1059,61 @@
         at += size
     up_bias_w, inner_gain_w, inner_shift_w, feed_gain_w, feed_shift_w, down_bias_w = pieces
 
-    feed_wide, feed_pull = jax.vjp(layer_norm, hidden, feed_gain_w, feed_shift_w)
-    feed_in = feed_wide.astype(BF)
-    before = mm(feed_in, up_full) + up_bias_w
-    inner_wide, inner_pull = jax.vjp(gelu_norm, before, inner_gain_w, inner_shift_w)
-    inner = inner_wide.astype(BF)
-    output = (hidden + mm(inner, down_full) + down_bias_w).astype(BF)
-
-    cot_wide = cotangent.astype(F32)
-    down_weight_grad = dot_rows(inner, cotangent)
-    down_bias_grad = jnp.sum(cot_wide, axis=0)
-    inner_grad = dot_cols(cotangent, down_full)
-    before_grad, inner_gain_grad, inner_shift_grad = inner_pull(inner_grad)
-    before_low = before_grad.astype(BF)
-    up_weight_grad = dot_rows(feed_in, before_low)
-    up_bias_grad = jnp.sum(before_low.astype(F32), axis=0)
-    feed_grad = dot_cols(before_low, up_full)
-    hidden_norm_grad, feed_gain_grad, feed_shift_grad = feed_pull(feed_grad)
-    hidden_grad = cot_wide + hidden_norm_grad
-    branch_low = hidden_grad.astype(BF)
-    out_bias_grad = jnp.sum(branch_low.astype(F32), axis=0)
-    out_grad_turned = dot_rows(branch_low, mixed)
-    mixed_grad, attn_gain_grad, attn_shift_grad = attn_pull(dot_cols(branch_low, out_full))
-
-    out_rows = width // seq_count
-    out_blocks = out_grad_turned.reshape(seq_count, 2, out_rows // 2, 2, width // 2)
-    out_blocks = out_blocks.transpose(0, 3, 2, 1, 4).reshape(devices, out_rows // 2, width)
+    narrow = [attn_gain_full, attn_shift_full, out_bias, feed_gain_w, feed_shift_w, down_bias_w]
+    narrow = jnp.stack([v.astype(F32) for v in narrow])
+    broad = jnp.stack([up_bias_w, inner_gain_w, inner_shift_w]).reshape(3, fold, 1, width)
+    feed_ins = [
+        same.reshape(cols, half_rows),
+        across.reshape(cols, tok_rows),
+        beside.reshape(cols, half_rows),
+        beyond.reshape(cols, half_rows),
+        tokens_half,
+        cotangent,
+        out_full,
+        up_full,
+        down_full,
+        narrow,
+        broad,
+    ]
+    rows_wide = (half_rows, width)
+    shapes = [
+        (rows_wide, BF),
+        (rows_wide, F32),
+        ((2 * cols, half_rows), BF),
+        ((cols, half_rows), BF),
+        ((cols, half_rows), BF),
+        ((3, fold, 1, width), F32),
+        ((8, width), F32),
+    ]
+    shares = Shares(devices, width, ff)
+    if shares.direct:
+        shapes += [((devices, shares.rows, width // 2), BF)]
+    else:
+        shapes += [((fold, width, width), BF), ((fold, width, width), BF), ((width, width), BF)]
+    (
+        output,
+        hidden_grad,
+        gone,
+        kept_away,
+        kept,
+        broad_grads,
+        narrow_grads,
+        *stack,
+    ) = pl.pallas_call(
+        functools.partial(feed_kernel, group, fold, shares, shares.direct),
+        in_specs=[pl.BlockSpec(memory_space=pltpu.SMEM)] + [whole] * len(feed_ins),
+        out_specs=[whole] * len(shapes),
+        out_shape=[jax.ShapeDtypeStruct(shape, dtype) for shape, dtype in shapes],
+        scratch_shapes=[pltpu.VMEM((fold, half_rows, width), F32)] * 3,
+        compiler_params=pltpu.CompilerParams(vmem_limit_bytes=62 * 2**20),
+        cost_estimate=pl.CostEstimate(
+            flops=12 * half_rows * width * ff, bytes_accessed=2**25, transcendentals=0
+        ),
+    )(facts, *feed_ins)
+    up_bias_grad, inner_gain_grad, inner_shift_grad = broad_grads.reshape(3, ff)
+    down_bias_grad, feed_gain_grad, feed_shift_grad = narrow_grads[0:3]
+    out_bias_grad, attn_gain_grad, attn_shift_grad = narrow_grads[3:6]
+
     by_device = [up_bias_grad, inner_gain_grad, inner_shift_grad, down_bias_grad]
     by_device += [feed_gain_grad, feed_shift_grad, out_bias_grad]
     by_core = [attn_gain_grad, attn_shift_grad]
@@ -852,27 +1122,18 @@
         g.reshape(2, seq_count, -1).transpose(1, 0, 2).reshape(devices, -1) for g in by_core
     ]
     small_sizes = [g.shape[1] for g in small_grads]
-    small_grads = jnp.concatenate(small_grads, axis=1)
-    small_grads = jnp.pad(small_grads, ((0, 0), (0, -small_grads.shape[1] % width)))
-    small_grads = small_grads.reshape(devices, -1, width)
-    up_blocks = [
-        up_weight_grad[:, j * width : (j + 1) * width].reshape(devices, up_rows, width)
-        for j in range(fold)
-    ]
-    down_blocks = down_weight_grad.reshape(devices, down_rows, width)
-    stack = [b.astype(BF) for b in (*up_blocks, down_blocks, out_blocks, small_grads)]
-    stack = jnp.concatenate(stack, axis=1)
-    stack = jnp.pad(stack, ((0, 0), (0, -stack.shape[1] % 16), (0, 0)))
+    small_grads = shares.small(small_grads)
+    stack = stack[0] if shares.direct else shares.stack(*stack)
+    stack = lax.dynamic_update_slice(stack, small_grads.astype(BF), (0, shares.small_at, 0))
     summed = lax.psum_scatter(
-        stack.reshape(-1, width), BOTH, scatter_dimension=0, tiled=True
-    ).astype(F32)
-
-    grad_turned = mixed_grad.astype(BF).T
-    got = swap(pick_half(grad_turned, 1 - core, 0), "head", 1)
-    joined = in_order(core, pick_half(grad_turned, core, 0), got, 1)
-    got = swap(pick_half(joined, 1 - cross, 0), "seq", 1)
-    joined = in_order(cross, pick_half(joined, cross, 0), got, 1)
-    grads_turned = joined.reshape(group, HEAD_DIM, window)
+        stack.reshape(-1, width // 2), BOTH, scatter_dimension=0, tiled=True
+    )
+
+    near_grads = swap(gone, "head", 1)
+    far_grads = swap(kept_away, "seq", 1)
+    last_grads = swap(near_grads[cols:], "seq", 1)
+    grad_pieces = [kept, near_grads[:cols], far_grads, last_grads]
+    grad_pieces = [g.reshape(group, HEAD_DIM, half_rows) for g in grad_pieces]
 
     strides = [1] + [s.stride for s in plan.spaces]
     counts = [window] + [s.queries for s in plan.spaces]
@@ -880,7 +1141,7 @@
         functools.partial(prepare_kernel, plan, group),
         group,
         facts,
-        [queries_turned, grads_turned, combined, lse_all, *[extra_q[s] for s in strides]],
+        [queries_turned, *grad_pieces, combined, lse_all, *[extra_q[s] for s in strides]],
         [o for n in counts for o in ((128, n, BF), (128, n, BF), (n, 128, BF))],
     )
     prepared = {s: prepared[3 * j : 3 * j + 3] for j, s in enumerate(strides)}
@@ -941,14 +1202,9 @@
     away = lax.dynamic_index_in_dim(part_low, 1 - core, 1, keepdims=False)
     got = swap(away, "head", 1)
     both = (mine.astype(F32) + got.astype(F32)).astype(BF)
-    mine = lax.dynamic_index_in_dim(both, cross, 0, keepdims=False)
+    near_part = lax.dynamic_index_in_dim(both, cross, 0, keepdims=False)
     away = lax.dynamic_index_in_dim(both, 1 - cross, 0, keepdims=False)
-    normed_grad = mine.astype(F32) + swap(away, "seq", 1).astype(F32)
-    tokens_norm_grad = jax.vjp(layer_norm, tokens_half, mix_gain.astype(F32), mix_shift.astype(F32))[
-        1
-    ](normed_grad)[0]
-    tokens_grad = hidden_grad + tokens_norm_grad
-
+    away_got = swap(away, "seq", 1)
     weight_part = jnp.concatenate(
         [dot_rows(normed, pair_low), dot_cols(normed.T, query_low)], axis=1
     ).astype(BF)
@@ -960,12 +1216,20 @@
     block_rows = width // seq_count
     weight_part = weight_part.reshape(seq_count // 2, 2 * block_rows, 3 * cols)
     bits = (seq_count // 2).bit_length() - 1
-    for bit in reversed(range(bits)):
+    for bit in range(bits):
         here = (window_index >> bit) & 1
-        mine = pick_half(weight_part, here, 0)
-        got = swap(pick_half(weight_part, 1 - here, 0), "seq", 2 << bit)
+        pairs = weight_part.reshape(-1, 2, 2 * block_rows, 3 * cols)
+        mine = lax.dynamic_index_in_dim(pairs, here, 1, keepdims=False)
+        got = lax.dynamic_index_in_dim(pairs, 1 - here, 1, keepdims=False)
+        got = swap(got, "seq", 2 << bit)
         weight_part = (mine.astype(F32) + got.astype(F32)).astype(BF)
         sums = sums + swap(sums, "seq", 2 << bit)
+    weight_part, sums, away_got = lax.optimization_barrier((weight_part, sums, away_got))
+    normed_grad = near_part.astype(F32) + away_got.astype(F32)
+    tokens_norm_grad = jax.vjp(
+        layer_norm, tokens_half.astype(F32), mix_gain.astype(F32), mix_shift.astype(F32)
+    )[1](normed_grad)[0]
+    tokens_grad = hidden_grad + tokens_norm_grad
     weight_part = weight_part[0]
     got = swap(pick_half(weight_part, 1 - cross, 0), "seq", 1)
     mine = pick_half(weight_part, cross, 0)
@@ -992,16 +1256,14 @@
         for a, b in zip(parts_of(flat[: 3 * cols]), parts_of(flat_other[: 3 * cols]))
     ]
 
-    up_sum = jnp.concatenate(
-        [summed[j * up_rows : (j + 1) * up_rows] for j in range(fold)], axis=1
-    )
-    at = fold * up_rows
-    down_sum = summed[at : at + down_rows]
-    at += down_rows
-    out_sum = summed[at : at + out_rows // 2].reshape(out_rows // 2, 2, width // 2)
-    out_sum = out_sum.transpose(1, 0, 2).reshape(out_rows, width // 2).T
-    at += out_rows // 2
-    flat_small = summed[at : at + small_grads.shape[1]].reshape(-1)
+    span, step = shares.up_span, down_rows
+    up_sum = [summed[p * span : p * span + up_rows] for p in range(2 * fold)]
+    up_sum = jnp.concatenate(up_sum, axis=1).astype(F32)
+    down_sum = summed[shares.down_at : shares.out_at].reshape(2, step, width // 2)
+    down_sum = jnp.concatenate([down_sum[0], down_sum[1]], axis=1).astype(F32)
+    out_sum = summed[shares.out_at : shares.small_at].T.astype(F32)
+    flat_small = summed[shares.small_at : shares.small_at + small_grads.shape[1]]
+    flat_small = flat_small.reshape(-1).astype(F32)
     smalls, place = [], 0
     for size in small_sizes:
         smalls.append(flat_small[place : place + size])

time: 545 us -> 436 us (0.80)
  the two profiles are of different devices: /device:TPU:0 before, /device:TPU:29 now
where the time goes in v2:
time: 436 us; the launch traced here: 429 us
  Pallas kernels  145 us (33%)
  waiting for transfers between devices  92.1 us (21%)
  starting transfers between devices  63.5 us (15%)
  other arithmetic  53.6 us (12%)
  local copies, waits for them, and re-layouts  50.1 us (11%)
  between operations  15.8 us (4%)
  matrix products  9.33 us (2%)
    pallas_call x8, Pallas kernels, head_call(): pl.pallas_call(kernel, grid=(group,), in_specs=[pl.BlockSpec(memory_space...  98.3 us
    ppermute x28, starting transfers between devices, swap(): lax.ppermute(array, axis, [(i, i ^ bit) for i in range(count) if only(i)])  55.6 us
    ppermute x28, waiting for transfers between devices, swap(): lax.ppermute(array, axis, [(i, i ^ bit) for i in range(count) if only(i)])  54.5 us
    pallas_call x1, Pallas kernels, per_device(): pl.pallas_call(functools.partial(feed_kernel, group, fold, shares, shares...  38.2 us
    ppermute x3, waiting for transfers between devices, level_jump(): return lax.ppermute(packet, 'seq', pairs)  27.3 us
    unnamed x125, local copies, waits for them, and re-layouts  15.4 us
    ppermute x3, waiting for transfers between devices, level_return(): return lax.ppermute(grads[0], 'seq', pairs)  10.3 us
  transfers between devices with their start and end apart: 36, of which 13 were waited for; matrix products, arithmetic and copies ran while one was open for 21% of the time, Pallas kernels for 21%

profile of v2, /device:TPU:29, one launch (start us, length us, event | category | flops | bytes accessed | tf_op | source)
XLA Modules:
  0.0 429.4 jit_solution(8426686799273158165)
XLA Ops:
  7.4 1.3 constant_dynamic-slice_fusion.6.tok
  13.0 1.6 constant_dynamic-slice_fusion.3
  22.9 1.4 fusion.23.refs_2_.refs_1_
  25.5 2.2 select_convert_fusion.1.refs_1_
  33.0 2.2 fusion.13.extra_q.refs_0_
  36.3 3.5 select_convert_fusion.extra_k
  41.7 1.4 broadcast_select_fusion.3
  45.1 1.9 pad_maximum_fusion.1.tok
  47.0 8.4 %shard_map.364 = (bf16[2048,768]{1,0:T(8,128)(2,1)}, bf16[3,64,2048]{2,1,0:T(8,128)(2,1)}, bf16[3,2048,128]{2,1,0:T(8,128)(2,1)}, bf16[3,1024,128]{2,1,0:T(8,128...) custom-call(s32[18]{0:T(128)} %concatenate.102.facts, bf16[2048,768]{1,0:T(8,128)(2,1)} %pad_maximum_fusion.1.tok, ...), custom_call_target="tpu_custom_call" | custom-call | tf_op jit(solution)/shard_map/pallas_call | solution.py:963
  55.4 1.3 collective-permute-start.2
  56.7 1.3 collective-permute-start.3
  58.1 1.3 collective-permute-start.4
  59.4 13.8 %shard_map.365 = (f32[3,64,2048]{2,1,0:T(8,128)}, f32[3,8,2048]{2,1,0:T(8,128)}) custom-call(bf16[3,2048,128]{2,1,0:T(8,128)(2,1)} %get-tuple-element.102.kv, bf16[3,2048,128]{2,1,0:T(8,128)(2,1)} %select_convert_fusion.extra_k, bf16[3,64,2048]{2,1,0:T(8,128)(2,1)} %get-tuple-element.98.q, bf16[3,64,2048]{2,1,0:T(8,128)(2,1)} %fusion.13.extra_q.refs_0_), custom_call_target="tpu_custom_call" | custom-call | flops 6442450944 | bytes 4718592 | tf_op jit(solution)/shard_map/pallas_call | solution.py:816
  74.0 26.4 %collective-permute-done.3.refs_0_ = bf16[3,864,128]{2,1,0:T(8,128)(2,1)} collective-permute-done((bf16[3,864,128]{2,1,0:T(8,128)(2,1)}, bf16[3,864,128]{2,1,0:T(8,128)(2,1)}, u32[]{:S(2)}, u32[]{:S(2)}) %collective-permute-start.3) | collective-permute-done | bytes 663584 | tf_op jit(solution)/shard_map/ppermute | solution.py:836
  100.5 8.2 %collective-permute-start.5 = (bf16[3,864,128]{2,1,0:T(8,128)(2,1)}, bf16[3,864,128]{2,1,0:T(8,128)(2,1)}, u32[]{:S(2)}, u32[]{:S(2)}) collective-permute-start(bf16[3,864,128]{2,1,0:T(8,128)(2,1)} %collective-permute-done.3.refs_0_), channel_id=1, source_target_pairs={{8,12},{10,14},{12,8},{14,10},{24,28},{26,30},{28,24},{30,26},{9,1... | collective-permute-start | bytes 1990664 | tf_op jit(solution)/shard_map/ppermute | solution.py:830
  108.7 1.9 collective-permute-start.6
  110.6 8.3 %shard_map.366 = (f32[3,64,1024]{2,1,0:T(8,128)}, f32[3,8,1024]{2,1,0:T(8,128)}) custom-call(s32[18]{0:T(128)} %concatenate.102.facts, bf16[3,64,2048]{2,1,0:T(8,128)(2,1)} %get-tuple-element.98.q, bf16[3,1024,128]{2,1,0:T(8,128)(2,1)} %copy-done.44, bf16[3,1024,128]{2,1,0:T(8,128)(2,1)} %select_convert_fusion.1.refs_1_, ...), custom_call_target="tpu_custom_call" | custom-call | flops 3221225472 | bytes 2752512 | tf_op jit(solution)/shard_map/pallas_call | solution.py:816
  118.9 4.8 %slice.310 = bf16[32,96,768]{2,1,0:T(8,128)(2,1)} slice(bf16[32,208,768]{2,1,0:T(8,128)(2,1)} %bitcast.126), slice={[0:32], [96:192], [0:768]} | slice | bytes 9437184 | tf_op jit(solution)/shard_map/slice | solution.py:1022
  123.7 2.7 fusion.273
  126.4 2.5 pad_maximum_fusion.up_w
  128.9 1.9 collective-permute-start.7
  130.8 3.4 collective-permute-start.8
  136.4 3.5 collective-permute-done.8.refs_5_
  140.7 17.4 %shard_map.367 = (f32[3,64,2048]{2,1,0:T(8,128)}, f32[3,8,2048]{2,1,0:T(8,128)}, bf16[3,64,512]{2,1,0:T(8,128)(2,1)}, bf16[3,64,512]{2,1,0:T(8,128)(2,1)}, bf16[3,64,1024]{2,1,0:T(8,128)(2,1)}) custom-call(s32[18]{0:T(128)} %concatenate.102.facts, bf16[3,64,2048]{2,1,0:T(8,128)(2,1)} %get-tuple-element.98.q, f32[3,64,2048]{2,1,0:T(8,128)} %get-tuple-element.105.out_own, ...), custom_call_target="tpu_custom_call" | custom-call | flops 3221225472 | bytes 8601600 | tf_op jit(solution)/shard_map/pallas_call | solution.py:816
  158.7 5.7 %collective-permute-start.10 = (bf16[3,64,512]{2,1,0:T(8,128)(2,1)}, bf16[3,64,512]{2,1,0:T(8,128)(2,1)S(1)}, u32[]{:S(2)}, u32[]{:S(2)}) collective-permute-start(bf16[3,64,512]{2,1,0:T(8,128)(2,1)} %get-tuple-element.128), channel_id=1, source_target_pairs={{0,1},{1,0},{2,3},{3,2},{4,5},{5,4},{6,7},{7,6},{8,9},{9,8},{10,11... | collective-permute-start | bytes 589832 | tf_op jit(solution)/shard_map/ppermute | solution.py:830
  165.1 6.7 %collective-permute-start.11 = (bf16[3,64,512]{2,1,0:T(8,128)(2,1)S(1)}, bf16[3,64,512]{2,1,0:T(8,128)(2,1)S(1)}, u32[]{:S(2)}, u32[]{:S(2)}) collective-permute-start(bf16[3,64,512]{2,1,0:T(8,128)(2,1)S(1)} %slice.311), channel_id=1, source_target_pairs={{0,1},{1,0},{2,3},{3,2},{4,5},{5,4},{6,7},{7,6},{8,9},{9,8},{10,11... | collective-permute-start | bytes 589832 | tf_op jit(solution)/shard_map/ppermute | solution.py:830
  174.4 38.2 %shard_map.368 = (bf16[512,768]{1,0:T(8,128)(2,1)}, f32[512,768]{1,0:T(8,128)}, bf16[384,512]{1,0:T(8,128)(2,1)}, bf16[192,512]{1,0:T(8,128)(2,1)}, bf16[192,512...) custom-call(s32[18]{0:T(128)} %concatenate.102.facts, ...), custom_call_target="tpu_custom_call" | custom-call | flops 14495514624 | bytes 33554432 | tf_op jit(solution)/shard_map/pallas_call | solution.py:1102
  217.0 1.9 convert_reduce_fusion
  221.2 3.8 collective-permute-done.14
  225.0 4.2 collective-permute-done.15
  229.9 7.3 %shard_map.369 = (bf16[3,128,2048]{2,1,0:T(8,128)(2,1)}, bf16[3,128,2048]{2,1,0:T(8,128)(2,1)}, bf16[3,2048,128]{2,1,0:T(8,128)(2,1)}, bf16[3,128,1024]{2,1,0:T(...) custom-call(s32[18]{0:T(128)} %concatenate.102.facts, ...), custom_call_target="tpu_custom_call" | custom-call | bytes 4866048 | tf_op jit(solution)/shard_map/pallas_call | solution.py:816
  237.3 13.8 %shard_map.372 = (bf16[3,864,128]{2,1,0:T(8,128)(2,1)}, bf16[3,864,128]{2,1,0:T(8,128)(2,1)}, bf16[3,352,128]{2,1,0:T(8,128)(2,1)}, bf16[3,352,128]{2,1,0:T(8,12...) custom-call(s32[18]{0:T(128)} %concatenate.102.facts, ...), custom_call_target="tpu_custom_call" | custom-call | flops 8053063680 | bytes 6881280 | tf_op jit(solution)/shard_map/pallas_call | solution.py:816
  251.0 2.5 collective-permute-start.20
  253.6 2.9 fusion.2
  256.5 4.9 %copy.59 = bf16[768,2048]{1,0:T(8,128)(2,1)} copy(bf16[768,2048]{0,1:T(8,128)(2,1)} %bitcast.125) | data formatting | bytes 6291456 | tf_op jit(solution)/shard_map/dot_general | solution.py:38
  261.4 2.8 collective-permute-start.17
  264.2 2.5 collective-permute-start.19
  266.8 1.9 collective-permute-start.21
  268.7 10.5 %shard_map.371 = (bf16[3,1024,128]{2,1,0:T(8,128)(2,1)}, f32[3,64,1024]{2,1,0:T(8,128)}) custom-call(s32[18]{0:T(128)} %concatenate.102.facts, bf16[3,1024,128]{2,1,0:T(8,128)(2,1)} %copy-done.44, bf16[3,1024,128]{2,1,0:T(8,128)(2,1)} %select_convert_fusion.1.refs_1_, bf16[3,128,1024]{2,1,0:T(8,128)(2,1)} %get-tuple-element.145.refs_2_, ...), custom_call_target="tpu_custom_call" | custom-call | flops 8053063680 | bytes 3932160 | tf_op jit(solution)/shard_map/pallas_call | solution.py:816
  279.2 1.3 collective-permute-start.16
  280.6 14.6 %collective-permute-done.19 = bf16[3,352,128]{2,1,0:T(8,128)(2,1)S(1)} collective-permute-done((bf16[3,352,128]{2,1,0:T(8,128)(2,1)S(1)}, bf16[3,352,128]{2,1,0:T(8,128)(2,1)S(1)}, u32[]{:S(2)}, u32[]{:S(2)}) %collective-permute-start.19) | collective-permute-done | bytes 270368 | tf_op jit(solution)/shard_map/ppermute | solution.py:830
  295.3 1.3 collective-permute-start.22
  296.9 1.3 collective-permute-start.18
  298.3 20.8 %shard_map.370 = (f32[3,2048,128]{2,1,0:T(8,128)}, f32[3,64,2048]{2,1,0:T(8,128)}) custom-call(bf16[3,2048,128]{2,1,0:T(8,128)(2,1)} %get-tuple-element.102.kv, bf16[3,2048,128]{2,1,0:T(8,128)(2,1)} %select_convert_fusion.extra_k, bf16[3,128,2048]{2,1,0:T(8,128)(2,1)} %get-tuple-element.139.queries, bf16[3,128,2048]{2,1,0:T(8,128)(2,1)} %get-tuple-element.140.grads, ...), custom_call_target="tpu_custom_call" | custom-call | flops 16106127360 | bytes 7864320 | tf_op jit(solution)/shard_map/pallas_call | solution.py:816
  319.1 10.3 %collective-permute-done.18.refs_4_ = bf16[3,864,128]{2,1,0:T(8,128)(2,1)S(1)} collective-permute-done((bf16[3,864,128]{2,1,0:T(8,128)(2,1)S(1)}, bf16[3,864,128]{2,1,0:T(8,128)(2,1)S(1)}, u32[]{:S(2)}, u32[]{:S(2)}) %collective-permute-start.18) | collective-permute-done | bytes 663584 | tf_op jit(solution)/shard_map/ppermute | solution.py:852
  330.3 6.4 %shard_map.373 = (bf16[2048,384]{1,0:T(8,128)(2,1)}, bf16[3,64,2048]{2,1,0:T(8,128)(2,1)}) custom-call(s32[18]{0:T(128)} %concatenate.102.facts, f32[3,2048,128]{2,1,0:T(8,128)} %get-tuple-element.142.pair, f32[3,64,2048]{2,1,0:T(8,128)} %get-tuple-element.143.own_q, f32[3,64,1024]{2,1,0:T(8,128)} %get-tuple-element.148.refs_0_, ...), custom_call_target="tpu_custom_call" | custom-call | bytes 7913472 | tf_op jit(solution)/shard_map/pallas_call | solution.py:816
  336.6 1.4 convert_reduce_fusion.3
  338.1 1.8 convert_reduce_fusion.1
  340.0 1.8 fusion.282
  341.8 4.7 %fusion.272 = (f32[768]{0:T(1024)S(1)}, f32[768]{0:T(1024)S(1)}, bf16[2048,768]{1,0:T(8,128)(2,1)}) fusion(f32[2048]{0:T(1024)S(1)} %add_rsqrt_fusion, f32[2048]{0:T(1024)S(1)} %broadcast_multiply_fusion, bf16[1024,768]{1,0:T(8,128)(2,1)S(1)} %copy-done.4, bf16[1024,768]{1,0:T(8,128)(2,1)S(1)} %get-tuple-element.197, f32[2048,768]{1,0:T(8,128)S(1)} %fusion.282, ...), kind=kOutput, calls=%fused_computation.605 | convolution fusion | flops 621279744 | bytes 13686784 | tf_op jit(solution)/shard_map/dot_general | solution.py:32
  347.4 1.7 dynamic-slice_bitcast_fusion
  349.1 2.6 collective-permute-start.23
  354.0 1.8 convolution_convert_fusion
  356.9 2.3 collective-permute-start.28
  359.4 1.4 collective-permute-done.28
  360.8 8.4 %collective-permute-done.24 = bf16[4,96,576]{2,1,0:T(8,128)(2,1)} collective-permute-done((bf16[4,96,576]{2,1,0:T(8,128)(2,1)}, bf16[4,96,576]{2,1,0:T(8,128)(2,1)}, u32[]{:S(2)}, u32[]{:S(2)}) %collective-permute-start.24) | collective-permute-done | bytes 442400 | tf_op jit(solution)/shard_map/ppermute | solution.py:830
  370.4 2.4 collective-permute-start.25
  372.7 2.3 fusion.5
  376.0 2.4 collective-permute-done.25
  380.7 6.6 %collective-permute-done.26 = bf16[1,96,576]{2,1,0:T(8,128)(2,1)S(1)} collective-permute-done((bf16[1,96,576]{2,1,0:T(8,128)(2,1)}, bf16[1,96,576]{2,1,0:T(8,128)(2,1)S(1)}, u32[]{:S(2)}, u32[]{:S(2)}) %collective-permute-start.26) | collective-permute-done | bytes 110624 | tf_op jit(solution)/shard_map/ppermute | solution.py:830
  387.3 9.0 %collective-permute-done.30 = bf16[512,768]{1,0:T(8,128)(2,1)S(1)} collective-permute-done((bf16[512,768]{1,0:T(8,128)(2,1)}, bf16[512,768]{1,0:T(8,128)(2,1)S(1)}, u32[]{:S(2)}, u32[]{:S(2)}) %collective-permute-start.30) | collective-permute-done | bytes 786464 | tf_op jit(solution)/shard_map/ppermute | solution.py:830
  400.1 1.8 add_add_fusion.1
  402.3 3.2 collective-permute-start.32
  420.7 1.4 convert_bitcast_fusion
  (349 shorter events, 68.4 us)
Async XLA Ops:
  7.2 10.0 %copy-start = (bf16[768,384]{1,0:T(8,128)(2,1)S(1)}, bf16[768,384]{1,0:T(8,128)(2,1)}, u32[]{:S(2)}) copy-start(bf16[768,384]{1,0:T(8,128)(2,1)} %param.24) | copy-start | bytes 1769476
  7.3 3.8 copy-start.31
  7.3 3.8 copy-start.33
  7.3 111.6 %all-gather.3.cloned.1.call-start = ((), (), s32[]{:S(2)}) async-start(), calls=%async_computation.2 | async-start | bytes 10543104 | tf_op jit(solution)/shard_map/all_gather | solution.py:928
  7.4 3.8 copy-start.14
  8.7 5.9 %copy-start.5 = (bf16[512,768]{1,0:T(8,128)(2,1)}, bf16[512,768]{1,0:T(8,128)(2,1)S(1)}, u32[]{:S(2)}) copy-start(bf16[512,768]{1,0:T(8,128)(2,1)S(1)} %constant_dynamic-slice_fusion.6.tok) | copy-start | bytes 2359300
  9.8 400.8 %reduce-scatter.2.cloned.1.call-start = ((), (), s32[]{:S(2)}) async-start(), calls=%async_computation.1 | async-start | bytes 12976128 | tf_op jit(solution)/shard_map/reduce_scatter | solution.py:1128
  9.8 26.4 %collective-permute-start = (bf16[512,768]{1,0:T(8,128)(2,1)S(1)}, bf16[512,768]{1,0:T(8,128)(2,1)}, u32[]{:S(2)}, u32[]{:S(2)}) collective-permute-start(bf16[512,768]{1,0:T(8,128)(2,1)S(1)} %constant_dynamic-slice_fusion.6.tok), channel_id=1, source_target_pairs={{0,2},{2,0},{4,6},{6,4},{8,10},{10,8},{12,14},{14,12},{16,18},{18,... | collective-permute-start | bytes 2359304 | tf_op jit(solution)/shard_map/ppermute | solution.py:830
  12.0 27.8 %collective-permute-start.12 = (bf16[400,768]{1,0:T(8,128)(2,1)}, bf16[400,768]{1,0:T(8,128)(2,1)}, u32[]{:S(2)}, u32[]{:S(2)}) collective-permute-start(bf16[400,768]{1,0:T(8,128)(2,1)} %fusion.29), channel_id=1, source_target_pairs={{0,1},{1,0},{2,3},{3,2},{4,5},{5,4},{6,7},{7,6},{8,9},{9,8},{10,11... | collective-permute-start | bytes 1843208 | tf_op jit(solution)/shard_map/ppermute | solution.py:830
  13.0 3.4 copy-start.53
  13.0 3.6 copy-start.43
  18.4 12.4 %copy-start.10 = (bf16[768,3,128]{0,2,1:T(8,128)(2,1)}, bf16[768,3,128]{0,2,1:T(8,128)(2,1)S(1)}, u32[]{:S(2)}) copy-start(bf16[768,3,128]{0,2,1:T(8,128)(2,1)S(1)} %pad_maximum_fusion.5) | copy-start | bytes 1769476
  21.1 6.9 %copy-start.30 = (bf16[768]{0:T(1024)(128)(2,1)S(1)}, bf16[768]{0:T(1024)(128)(2,1)}, u32[]{:S(2)}) copy-start(bf16[768]{0:T(1024)(128)(2,1)} %param.22) | copy-start | bytes 4612
  21.1 7.5 %copy-start.35 = (bf16[768]{0:T(1024)(128)(2,1)S(1)}, bf16[768]{0:T(1024)(128)(2,1)}, u32[]{:S(2)}) copy-start(bf16[768]{0:T(1024)(128)(2,1)} %param.23) | copy-start | bytes 4612
  22.9 4.8 %copy-start.29 = (bf16[3,2112,128]{2,1,0:T(8,128)(2,1)}, bf16[3,2112,128]{2,1,0:T(8,128)(2,1)S(1)}, u32[]{:S(2)}) copy-start(bf16[3,2112,128]{2,1,0:T(8,128)(2,1)S(1)} %fusion.43.refs_8_.refs_10_) | copy-start | bytes 4866052
  25.5 7.0 %copy-start.36 = (bf16[768]{0:T(1024)(128)(2,1)S(1)}, bf16[768]{0:T(1024)(128)(2,1)}, u32[]{:S(2)}) copy-start(bf16[768]{0:T(1024)(128)(2,1)} %param.32) | copy-start | bytes 4612
  36.3 5.4 %collective-permute-start.1 = (bf16[512,768]{1,0:T(8,128)(2,1)}, bf16[512,768]{1,0:T(8,128)(2,1)S(1)}, u32[]{:S(2)}, u32[]{:S(2)}) collective-permute-start(bf16[512,768]{1,0:T(8,128)(2,1)} %collective-permute-done), channel_id=1, source_target_pairs={{0,1},{1,0},{2,3},{3,2},{4,5},{5,4},{6,7},{7,6},{8,9},{9,8},{10,11... | collective-permute-start | bytes 2359304 | tf_op jit(solution)/shard_map/ppermute | solution.py:830
  47.0 11.0 %copy-start.32 = (bf16[384]{0:T(512)(128)(2,1)S(1)}, bf16[384]{0:T(512)(128)(2,1)}, u32[]{:S(2)}) copy-start(bf16[384]{0:T(512)(128)(2,1)} %param.30) | copy-start | bytes 2308
  47.0 11.0 %copy-start.34 = (bf16[384]{0:T(512)(128)(2,1)S(1)}, bf16[384]{0:T(512)(128)(2,1)}, u32[]{:S(2)}) copy-start(bf16[384]{0:T(512)(128)(2,1)} %param.29) | copy-start | bytes 2308
  55.4 45.0 %collective-permute-start.2 = (bf16[3,1024,128]{2,1,0:T(8,128)(2,1)}, bf16[3,1024,128]{2,1,0:T(8,128)(2,1)S(1)}, u32[]{:S(2)}, u32[]{:S(2)}) collective-permute-start(bf16[3,1024,128]{2,1,0:T(8,128)(2,1)} %get-tuple-element.99), channel_id=1, source_target_pairs={{0,4},{2,6},{8,12},{10,14},{16,20},{18,22},{24,28},{26,30},{1,5},{... | collective-permute-start | bytes 2359304 | tf_op jit(solution)/shard_map/ppermute | solution.py:836
  56.7 43.7 %collective-permute-start.3 = (bf16[3,864,128]{2,1,0:T(8,128)(2,1)}, bf16[3,864,128]{2,1,0:T(8,128)(2,1)}, u32[]{:S(2)}, u32[]{:S(2)}) collective-permute-start(bf16[3,864,128]{2,1,0:T(8,128)(2,1)} %get-tuple-element.100), channel_id=1, source_target_pairs={{0,8},{2,10},{4,12},{6,14},{16,24},{18,26},{20,28},{22,30},{1,9},{... | collective-permute-start | bytes 1990664 | tf_op jit(solution)/shard_map/ppermute | solution.py:836
  58.1 16.0 %collective-permute-start.4 = (bf16[3,352,128]{2,1,0:T(8,128)(2,1)}, bf16[3,352,128]{2,1,0:T(8,128)(2,1)S(1)}, u32[]{:S(2)}, u32[]{:S(2)}) collective-permute-start(bf16[3,352,128]{2,1,0:T(8,128)(2,1)} %get-tuple-element.101), channel_id=1, source_target_pairs={{0,16},{2,18},{4,20},{6,22},{8,24},{10,26},{12,28},{14,30},{1,17},... | collective-permute-start | bytes 811016 | tf_op jit(solution)/shard_map/ppermute | solution.py:836
  74.0 54.8 %copy-start.46 = (bf16[3,352,128]{2,1,0:T(8,128)(2,1)}, bf16[3,352,128]{2,1,0:T(8,128)(2,1)S(1)}, u32[]{:S(2)}) copy-start(bf16[3,352,128]{2,1,0:T(8,128)(2,1)S(1)} %collective-permute-done.4.refs_2_) | copy-start | bytes 811012
  100.5 10.1 %copy-start.44 = (bf16[3,1024,128]{2,1,0:T(8,128)(2,1)}, bf16[3,1024,128]{2,1,0:T(8,128)(2,1)S(1)}, u32[]{:S(2)}) copy-start(bf16[3,1024,128]{2,1,0:T(8,128)(2,1)S(1)} %collective-permute-done.2.refs_0_) | copy-start | bytes 2359300
  100.5 28.4 %collective-permute-start.5 = (bf16[3,864,128]{2,1,0:T(8,128)(2,1)}, bf16[3,864,128]{2,1,0:T(8,128)(2,1)}, u32[]{:S(2)}, u32[]{:S(2)}) collective-permute-start(bf16[3,864,128]{2,1,0:T(8,128)(2,1)} %collective-permute-done.3.refs_0_), channel_id=1, source_target_pairs={{8,12},{10,14},{12,8},{14,10},{24,28},{26,30},{28,24},{30,26},{9,1... | collective-permute-start | bytes 1990664 | tf_op jit(solution)/shard_map/ppermute | solution.py:830
  108.7 20.2 %collective-permute-start.6 = (bf16[3,352,128]{2,1,0:T(8,128)(2,1)S(1)}, bf16[3,352,128]{2,1,0:T(8,128)(2,1)}, u32[]{:S(2)}, u32[]{:S(2)}) collective-permute-start(bf16[3,352,128]{2,1,0:T(8,128)(2,1)S(1)} %collective-permute-done.4.refs_2_), channel_id=1, source_target_pairs={{16,24},{18,26},{20,28},{22,30},{24,16},{26,18},{28,20},{30,22},{1... | collective-permute-start | bytes 811016 | tf_op jit(solution)/shard_map/ppermute | solution.py:830
  128.9 7.5 %collective-permute-start.7 = (bf16[3,352,128]{2,1,0:T(8,128)(2,1)S(1)}, bf16[3,352,128]{2,1,0:T(8,128)(2,1)S(1)}, u32[]{:S(2)}, u32[]{:S(2)}) collective-permute-start(bf16[3,352,128]{2,1,0:T(8,128)(2,1)S(1)} %collective-permute-done.4.refs_2_), channel_id=1, source_target_pairs={{16,20},{18,22},{20,16},{22,18},{24,28},{26,30},{28,24},{30,26},{1... | collective-permute-start | bytes 811016 | tf_op jit(solution)/shard_map/ppermute | solution.py:830
  130.8 9.2 %collective-permute-start.8 = (bf16[3,352,128]{2,1,0:T(8,128)(2,1)}, bf16[3,352,128]{2,1,0:T(8,128)(2,1)S(1)}, u32[]{:S(2)}, u32[]{:S(2)}) collective-permute-start(bf16[3,352,128]{2,1,0:T(8,128)(2,1)} %collective-permute-done.6.refs_3_), channel_id=1, source_target_pairs={{16,20},{18,22},{20,16},{22,18},{24,28},{26,30},{28,24},{30,26},{1... | collective-permute-start | bytes 811016 | tf_op jit(solution)/shard_map/ppermute | solution.py:830
  136.4 4.3 %copy-start.47 = (bf16[3,352,128]{2,1,0:T(8,128)(2,1)}, bf16[3,352,128]{2,1,0:T(8,128)(2,1)S(1)}, u32[]{:S(2)}) copy-start(bf16[3,352,128]{2,1,0:T(8,128)(2,1)S(1)} %collective-permute-done.7.refs_4_) | copy-start | bytes 811012
  158.2 6.9 %collective-permute-start.9 = (bf16[3,64,1024]{2,1,0:T(8,128)(2,1)}, bf16[3,64,1024]{2,1,0:T(8,128)(2,1)S(1)}, u32[]{:S(2)}, u32[]{:S(2)}) collective-permute-start(bf16[3,64,1024]{2,1,0:T(8,128)(2,1)} %get-tuple-element.127), channel_id=1, source_target_pairs={{0,2},{2,0},{4,6},{6,4},{8,10},{10,8},{12,14},{14,12},{16,18},{18,... | collective-permute-start | bytes 1179656 | tf_op jit(solution)/shard_map/ppermute | solution.py:830
  158.7 14.9 %collective-permute-start.10 = (bf16[3,64,512]{2,1,0:T(8,128)(2,1)}, bf16[3,64,512]{2,1,0:T(8,128)(2,1)S(1)}, u32[]{:S(2)}, u32[]{:S(2)}) collective-permute-start(bf16[3,64,512]{2,1,0:T(8,128)(2,1)} %get-tuple-element.128), channel_id=1, source_target_pairs={{0,1},{1,0},{2,3},{3,2},{4,5},{5,4},{6,7},{7,6},{8,9},{9,8},{10,11... | collective-permute-start | bytes 589832 | tf_op jit(solution)/shard_map/ppermute | solution.py:830
  165.1 8.6 %copy-start.28 = (bf16[3,64,1024]{2,1,0:T(8,128)(2,1)}, bf16[3,64,1024]{2,1,0:T(8,128)(2,1)S(1)}, u32[]{:S(2)}) copy-start(bf16[3,64,1024]{2,1,0:T(8,128)(2,1)S(1)} %collective-permute-done.9) | copy-start | bytes 1179652
  165.1 8.6 %collective-permute-start.11 = (bf16[3,64,512]{2,1,0:T(8,128)(2,1)S(1)}, bf16[3,64,512]{2,1,0:T(8,128)(2,1)S(1)}, u32[]{:S(2)}, u32[]{:S(2)}) collective-permute-start(bf16[3,64,512]{2,1,0:T(8,128)(2,1)S(1)} %slice.311), channel_id=1, source_target_pairs={{0,1},{1,0},{2,3},{3,2},{4,5},{5,4},{6,7},{7,6},{8,9},{9,8},{10,11... | collective-permute-start | bytes 589832 | tf_op jit(solution)/shard_map/ppermute | solution.py:830
  217.0 2.4 collective-permute-start.13
  219.0 6.0 %collective-permute-start.14 = (bf16[192,512]{1,0:T(8,128)(2,1)S(1)}, bf16[192,512]{1,0:T(8,128)(2,1)S(1)}, u32[]{:S(2)}, u32[]{:S(2)}) collective-permute-start(bf16[192,512]{1,0:T(8,128)(2,1)S(1)} %copy-done.50), channel_id=1, source_target_pairs={{0,2},{2,0},{4,6},{6,4},{8,10},{10,8},{12,14},{14,12},{16,18},{18,... | collective-permute-start | bytes 589832 | tf_op jit(solution)/shard_map/ppermute | solution.py:830
  220.1 9.1 %collective-permute-start.15 = (bf16[192,512]{1,0:T(8,128)(2,1)S(1)}, bf16[192,512]{1,0:T(8,128)(2,1)S(1)}, u32[]{:S(2)}, u32[]{:S(2)}) collective-permute-start(bf16[192,512]{1,0:T(8,128)(2,1)S(1)} %get-tuple-element.205), channel_id=1, source_target_pairs={{0,2},{2,0},{4,6},{6,4},{8,10},{10,8},{12,14},{14,12},{16,18},{18,... | collective-permute-start | bytes 589832 | tf_op jit(solution)/shard_map/ppermute | solution.py:830
  225.0 4.2 copy-start.24
  237.3 16.3 %copy-start.3 = (bf16[1024,768]{1,0:T(8,128)(2,1)S(1)}, bf16[1024,768]{1,0:T(8,128)(2,1)}, u32[]{:S(2)}) copy-start(bf16[1024,768]{1,0:T(8,128)(2,1)} %copy-done.2) | copy-start | bytes 4718596
  251.0 15.7 %collective-permute-start.20 = (bf16[3,352,128]{2,1,0:T(8,128)(2,1)}, bf16[3,352,128]{2,1,0:T(8,128)(2,1)S(1)}, u32[]{:S(2)}, u32[]{:S(2)}) collective-permute-start(bf16[3,352,128]{2,1,0:T(8,128)(2,1)} %get-tuple-element.163), channel_id=1, source_target_pairs={{16,20},{18,22},{20,16},{22,18},{24,28},{26,30},{28,24},{30,26},{1... | collective-permute-start | bytes 811016 | tf_op jit(solution)/shard_map/ppermute | solution.py:830
  256.5 7.6 %copy-start.49 = (bf16[3,352,128]{2,1,0:T(8,128)(2,1)S(1)}, bf16[3,352,128]{2,1,0:T(8,128)(2,1)}, u32[]{:S(2)}) copy-start(bf16[3,352,128]{2,1,0:T(8,128)(2,1)} %get-tuple-element.161) | copy-start | bytes 811012
  256.5 10.2 %copy-start.22 = (bf16[3,352,128]{2,1,0:T(8,128)(2,1)S(1)}, bf16[3,352,128]{2,1,0:T(8,128)(2,1)}, u32[]{:S(2)}) copy-start(bf16[3,352,128]{2,1,0:T(8,128)(2,1)} %get-tuple-element.162) | copy-start | bytes 811012
  261.4 35.3 %collective-permute-start.17 = (bf16[3,864,128]{2,1,0:T(8,128)(2,1)}, bf16[3,864,128]{2,1,0:T(8,128)(2,1)S(1)}, u32[]{:S(2)}, u32[]{:S(2)}) collective-permute-start(bf16[3,864,128]{2,1,0:T(8,128)(2,1)} %get-tuple-element.159), channel_id=1, source_target_pairs={{8,12},{10,14},{12,8},{14,10},{24,28},{26,30},{28,24},{30,26},{9,1... | collective-permute-start | bytes 1990664 | tf_op jit(solution)/shard_map/ppermute | solution.py:830
  264.2 31.0 %collective-permute-start.19 = (bf16[3,352,128]{2,1,0:T(8,128)(2,1)S(1)}, bf16[3,352,128]{2,1,0:T(8,128)(2,1)S(1)}, u32[]{:S(2)}, u32[]{:S(2)}) collective-permute-start(bf16[3,352,128]{2,1,0:T(8,128)(2,1)S(1)} %copy-done.49), channel_id=1, source_target_pairs={{16,20},{18,22},{20,16},{22,18},{24,28},{26,30},{28,24},{30,26},{1... | collective-permute-start | bytes 811016 | tf_op jit(solution)/shard_map/ppermute | solution.py:830
  266.8 28.4 %collective-permute-start.21 = (bf16[3,352,128]{2,1,0:T(8,128)(2,1)S(1)}, bf16[3,352,128]{2,1,0:T(8,128)(2,1)S(1)}, u32[]{:S(2)}, u32[]{:S(2)}) collective-permute-start(bf16[3,352,128]{2,1,0:T(8,128)(2,1)S(1)} %add_convert_fusion.2), channel_id=1, source_target_pairs={{16,24},{18,26},{20,28},{22,30},{24,16},{26,18},{28,20},{30,22},{1... | collective-permute-start | bytes 811016 | tf_op jit(solution)/shard_map/ppermute | solution.py:830
  268.7 26.5 %copy-start.23 = (bf16[3,352,128]{2,1,0:T(8,128)(2,1)S(1)}, bf16[3,352,128]{2,1,0:T(8,128)(2,1)}, u32[]{:S(2)}) copy-start(bf16[3,352,128]{2,1,0:T(8,128)(2,1)} %get-tuple-element.160) | copy-start | bytes 811012
  268.7 27.9 %copy-start.19 = (bf16[3,864,128]{2,1,0:T(8,128)(2,1)S(1)}, bf16[3,864,128]{2,1,0:T(8,128)(2,1)}, u32[]{:S(2)}) copy-start(bf16[3,864,128]{2,1,0:T(8,128)(2,1)} %get-tuple-element.158) | copy-start | bytes 1990660
  279.2 39.9 %collective-permute-start.16 = (bf16[3,1024,128]{2,1,0:T(8,128)(2,1)}, bf16[3,1024,128]{2,1,0:T(8,128)(2,1)S(1)}, u32[]{:S(2)}, u32[]{:S(2)}) collective-permute-start(bf16[3,1024,128]{2,1,0:T(8,128)(2,1)} %get-tuple-element.157), channel_id=1, source_target_pairs={{4,0},{6,2},{12,8},{14,10},{20,16},{22,18},{28,24},{30,26},{5,1},{... | collective-permute-start | bytes 2359304 | tf_op jit(solution)/shard_map/ppermute | solution.py:852
  295.3 23.8 %collective-permute-start.22 = (bf16[3,352,128]{2,1,0:T(8,128)(2,1)S(1)}, bf16[3,352,128]{2,1,0:T(8,128)(2,1)S(1)}, u32[]{:S(2)}, u32[]{:S(2)}) collective-permute-start(bf16[3,352,128]{2,1,0:T(8,128)(2,1)S(1)} %add_convert_fusion.1), channel_id=1, source_target_pairs={{16,0},{18,2},{20,4},{22,6},{24,8},{26,10},{28,12},{30,14},{17,1},... | collective-permute-start | bytes 811016 | tf_op jit(solution)/shard_map/ppermute | solution.py:852
  296.9 32.5 %collective-permute-start.18 = (bf16[3,864,128]{2,1,0:T(8,128)(2,1)S(1)}, bf16[3,864,128]{2,1,0:T(8,128)(2,1)S(1)}, u32[]{:S(2)}, u32[]{:S(2)}) collective-permute-start(bf16[3,864,128]{2,1,0:T(8,128)(2,1)S(1)} %add_convert_fusion), channel_id=1, source_target_pairs={{8,0},{10,2},{12,4},{14,6},{24,16},{26,18},{28,20},{30,22},{9,1},{... | collective-permute-start | bytes 1990664 | tf_op jit(solution)/shard_map/ppermute | solution.py:852
  319.1 10.3 %copy-start.18 = (bf16[3,1024,128]{2,1,0:T(8,128)(2,1)}, bf16[3,1024,128]{2,1,0:T(8,128)(2,1)S(1)}, u32[]{:S(2)}) copy-start(bf16[3,1024,128]{2,1,0:T(8,128)(2,1)S(1)} %collective-permute-done.16.refs_3_) | copy-start | bytes 2359300
  319.1 10.3 %copy-start.21 = (bf16[3,352,128]{2,1,0:T(8,128)(2,1)}, bf16[3,352,128]{2,1,0:T(8,128)(2,1)S(1)}, u32[]{:S(2)}) copy-start(bf16[3,352,128]{2,1,0:T(8,128)(2,1)S(1)} %collective-permute-done.22.refs_5_) | copy-start | bytes 811012
  346.6 10.3 %collective-permute-start.27 = (f32[24,128]{1,0:T(8,128)S(1)}, f32[24,128]{1,0:T(8,128)S(1)}, u32[]{:S(2)}, u32[]{:S(2)}) collective-permute-start(f32[24,128]{1,0:T(8,128)S(1)} %pad_bitcast_fusion), channel_id=1, source_target_pairs={{0,4},{2,6},{4,0},{6,2},{8,12},{10,14},{12,8},{14,10},{16,20},{18,... | collective-permute-start | bytes 36872 | tf_op jit(solution)/shard_map/ppermute | solution.py:830
  347.4 4.2 copy-start.13
  349.1 23.7 %collective-permute-start.23 = (bf16[2,512,768]{2,1,0:T(8,128)(2,1)S(1)}, bf16[2,512,768]{2,1,0:T(8,128)(2,1)}, u32[]{:S(2)}, u32[]{:S(2)}) collective-permute-start(bf16[2,512,768]{2,1,0:T(8,128)(2,1)S(1)} %dynamic-slice_bitcast_fusion), channel_id=1, source_target_pairs={{0,1},{1,0},{2,3},{3,2},{4,5},{5,4},{6,7},{7,6},{8,9},{9,8},{10,11... | collective-permute-start | bytes 4718600 | tf_op jit(solution)/shard_map/ppermute | solution.py:830
  356.7 12.5 %collective-permute-start.24 = (bf16[4,96,576]{2,1,0:T(8,128)(2,1)}, bf16[4,96,576]{2,1,0:T(8,128)(2,1)}, u32[]{:S(2)}, u32[]{:S(2)}) collective-permute-start(bf16[4,96,576]{2,1,0:T(8,128)(2,1)} %fusion.31), channel_id=1, source_target_pairs={{0,4},{2,6},{4,0},{6,2},{8,12},{10,14},{12,8},{14,10},{16,20},{18,... | collective-permute-start | bytes 1327112 | tf_op jit(solution)/shard_map/ppermute | solution.py:830
  356.9 3.8 collective-permute-start.28
  360.8 19.2 %collective-permute-start.29 = (f32[24,128]{1,0:T(8,128)S(1)}, f32[24,128]{1,0:T(8,128)}, u32[]{:S(2)}, u32[]{:S(2)}) collective-permute-start(f32[24,128]{1,0:T(8,128)S(1)} %fusion.292), channel_id=1, source_target_pairs={{0,16},{2,18},{4,20},{6,22},{8,24},{10,26},{12,28},{14,30},{16,0},... | collective-permute-start | bytes 36872 | tf_op jit(solution)/shard_map/ppermute | solution.py:830
  370.4 8.0 %collective-permute-start.25 = (bf16[2,96,576]{2,1,0:T(8,128)(2,1)S(1)}, bf16[2,96,576]{2,1,0:T(8,128)(2,1)S(1)}, u32[]{:S(2)}, u32[]{:S(2)}) collective-permute-start(bf16[2,96,576]{2,1,0:T(8,128)(2,1)S(1)} %dynamic-slice_bitcast_fusion.2), channel_id=1, source_target_pairs={{0,8},{2,10},{4,12},{6,14},{8,0},{10,2},{12,4},{14,6},{16,24},{18,... | collective-permute-start | bytes 663560 | tf_op jit(solution)/shard_map/ppermute | solution.py:830
  376.0 20.3 %collective-permute-start.30 = (bf16[512,768]{1,0:T(8,128)(2,1)}, bf16[512,768]{1,0:T(8,128)(2,1)S(1)}, u32[]{:S(2)}, u32[]{:S(2)}) collective-permute-start(bf16[512,768]{1,0:T(8,128)(2,1)} %dynamic-slice_bitcast_fusion.1), channel_id=1, source_target_pairs={{0,2},{2,0},{4,6},{6,4},{8,10},{10,8},{12,14},{14,12},{16,18},{18,... | collective-permute-start | bytes 2359304 | tf_op jit(solution)/shard_map/ppermute | solution.py:830
  379.1 8.2 %collective-permute-start.26 = (bf16[1,96,576]{2,1,0:T(8,128)(2,1)}, bf16[1,96,576]{2,1,0:T(8,128)(2,1)S(1)}, u32[]{:S(2)}, u32[]{:S(2)}) collective-permute-start(bf16[1,96,576]{2,1,0:T(8,128)(2,1)} %constant_dynamic-slice_fusion.2), channel_id=1, source_target_pairs={{0,16},{2,18},{4,20},{6,22},{8,24},{10,26},{12,28},{14,30},{16,0},... | collective-permute-start | bytes 331784 | tf_op jit(solution)/shard_map/ppermute | solution.py:830
  396.3 5.9 %collective-permute-start.31 = (f32[24,128]{1,0:T(8,128)S(1)}, f32[24,128]{1,0:T(8,128)S(1)}, u32[]{:S(2)}, u32[]{:S(2)}) collective-permute-start(f32[24,128]{1,0:T(8,128)S(1)} %add.1777), channel_id=1, source_target_pairs={{0,2},{2,0},{4,6},{6,4},{8,10},{10,8},{12,14},{14,12},{16,18},{18,... | collective-permute-start | bytes 36872 | tf_op jit(solution)/shard_map/ppermute | solution.py:830
  396.6 11.0 %collective-permute-start.33 = (bf16[48,576]{1,0:T(8,128)(2,1)S(1)}, bf16[48,576]{1,0:T(8,128)(2,1)S(1)}, u32[]{:S(2)}, u32[]{:S(2)}) collective-permute-start(bf16[48,576]{1,0:T(8,128)(2,1)S(1)} %get-tuple-element.216), channel_id=1, source_target_pairs={{0,2},{2,0},{4,6},{6,4},{8,10},{10,8},{12,14},{14,12},{16,18},{18,... | collective-permute-start | bytes 165896 | tf_op jit(solution)/shard_map/ppermute | solution.py:830
  402.3 4.7 %collective-permute-start.32 = (f32[12,128]{1,0:T(8,128)S(1)}, f32[12,128]{1,0:T(8,128)S(1)}, u32[]{:S(2)}, u32[]{:S(2)}) collective-permute-start(f32[12,128]{1,0:T(8,128)S(1)} %fusion.146), channel_id=1, source_target_pairs={{0,1},{1,0},{2,3},{3,2},{4,5},{5,4},{6,7},{7,6},{8,9},{9,8},{10,11... | collective-permute-start | bytes 18440 | tf_op jit(solution)/shard_map/ppermute | solution.py:830
  407.6 14.5 %copy-start.1 = (bf16[768,384]{1,0:T(8,128)(2,1)S(1)}, bf16[768,384]{1,0:T(8,128)(2,1)}, u32[]{:S(2)}) copy-start(bf16[768,384]{1,0:T(8,128)(2,1)} %param.24) | copy-start | bytes 1769476
  (26 other events, 41.4 us)
Sparse Core Ops, SparseCore 0:
  11.0 100.2 all-gather.2
  216.2 185.8 reduce-scatter.1
